TPU v7x, 32 devices: a whole 2x2x4 slice. The times are simulated.
32 devices in a mesh: kern: 4 (over x, core), tile: 8 (over z, y).
Axes of the slice: x: 2, y: 2, z: 4, core: 2. Of those that a mesh axis runs over, the one named last changes fastest.
Arguments:
- mask: int32 [256, 512], P('tile'), may hold values 0 or 1
- kernels: bfloat16 [24, 2, 64, 64], replicated, may hold values from -0.09375 to 0.09375
- socs_weights: float32 [24], replicated, may hold values from 0.02 to 0.3
- quencher: float32 [256, 512], P('tile', 'kern'), may hold values from 0.1 to 0.6
Outputs:
- intensity: float32 [256, 512], P('tile', 'kern')
- acid_final: float32 [256, 512], P('tile', 'kern')
- base_final: float32 [256, 512], P('tile', 'kern')
All inputs are finite; a program needn't handle non-finite values. No bound on the sum of `mask` on one device may be relied on, other than what follows from the above.
Results may differ from a plain program's by a relative error of at most 0.0003.
Values sent between devices are 32-bit elements; how exact they have to be, the bound alone decides.
No kernel may reach another device: no remote copies, remote signals or barrier semaphores. Data moves between devices by JAX's collectives and lax.ppermute only.
A program may use at most 128 MiB of HBM per device.

v0:
```python
import jax
import jax.numpy as jnp
from jax import lax
from jax.sharding import PartitionSpec as P

STEPS = 8


DIFFUSE_ACID = 0.2
DIFFUSE_BASE = 0.1
QUENCH_RATE = 0.5
EXPOSURE = 0.35


def shifted(value, axis, steps):
    count = lax.axis_size(axis)
    leading, last = (max(0, -steps), min(count, count - steps))
    return lax.ppermute(value, axis, [(source, source + steps) for source in range(leading, last)])


def padded_2(block, sides, width):
    for axis, dim in sides:
        count = lax.axis_size(axis)
        forward = [(i, i + 1) for i in range(count - 1)]
        backward = [(target, source) for source, target in forward]
        low = lax.ppermute(
            lax.slice_in_dim(block, block.shape[dim] - width, None, axis=dim), axis, forward
        )
        high = lax.ppermute(lax.slice_in_dim(block, 0, width, axis=dim), axis, backward)
        block = jnp.concatenate([low, block, high], axis=dim)
    return block


def react(padded):
    middle = padded[:, 1:-1, 1:-1]
    spread = (
        padded[:, :-2, 1:-1]
        + padded[:, 2:, 1:-1]
        + padded[:, 1:-1, :-2]
        + padded[:, 1:-1, 2:]
        - 4.0 * middle
    )
    quenched = QUENCH_RATE * middle[0] * middle[1]
    acid_next = middle[0] + DIFFUSE_ACID * spread[0] - quenched
    base_next = middle[1] + DIFFUSE_BASE * spread[1] - quenched
    return jnp.stack([acid_next, base_next], axis=0)


def band_table(ambit_size):
    tap_ids = lax.iota(jnp.int32, ambit_size)
    input_ids = lax.iota(jnp.int32, 2 * ambit_size)
    output_ids = lax.iota(jnp.int32, ambit_size)
    offsets = input_ids[None, :, None] - output_ids[None, None, :]
    return (offsets == tap_ids[:, None, None]).astype(jnp.bfloat16)


def field_band(mask_rows, kernel_group, ambit_size, edge_rows):
    column_blocks = (mask_rows.shape[1] - ambit_size) // ambit_size
    padded_rows = jnp.pad(mask_rows, ((edge_rows, edge_rows), (0, 0)))
    total_padded = padded_rows.shape[0]
    halves = padded_rows.reshape(total_padded, column_blocks + 1, ambit_size)
    windows = jnp.concatenate([halves[:, :-1], halves[:, 1:]], axis=2)
    band_rows = total_padded - ambit_size
    kernel_count = kernel_group.shape[0]
    selector = band_table(ambit_size)
    accumulated = jnp.zeros((band_rows * column_blocks, kernel_count * 2 * ambit_size), jnp.float32)
    for group_index in range(ambit_size // 8):
        first = group_index * 8
        stacked = jnp.stack(
            [windows[first + offset : first + offset + band_rows] for offset in range(8)], axis=2
        )
        left_side = stacked.reshape(band_rows * column_blocks, 16 * ambit_size)
        taps = kernel_group[:, :, first : first + 8, :]
        banded_taps = jnp.einsum(
            "kprb,bco->rckpo", taps, selector, preferred_element_type=jnp.float32
        ).astype(jnp.bfloat16)
        right_side = banded_taps.reshape(16 * ambit_size, kernel_count * 2 * ambit_size)
        accumulated = accumulated + jnp.dot(
            left_side, right_side, preferred_element_type=jnp.float32
        )
    banded = accumulated.reshape(band_rows, column_blocks, kernel_count, 2, ambit_size)
    banded = jnp.transpose(banded, (2, 3, 0, 1, 4))
    return banded.reshape(kernel_count, 2, band_rows, column_blocks * ambit_size)


def on_device(mask, kernels, socs_weights, quencher):
    ambit_size = kernels.shape[2]
    half_ambit = ambit_size // 2
    kern_count = lax.axis_size("kern")
    kern_index = lax.axis_index("kern")
    local_rows = mask.shape[0]
    padded_mask = jnp.pad(mask.astype(jnp.bfloat16), ((0, 0), (half_ambit, half_ambit)))
    per_group = kernels.shape[0] // kern_count
    own_kernels = lax.dynamic_slice_in_dim(kernels, kern_index * per_group, per_group, 0)
    own_weights = lax.dynamic_slice_in_dim(socs_weights, kern_index * per_group, per_group, 0)
    fields = field_band(padded_mask, own_kernels, ambit_size, ambit_size)
    upper_rim = fields[:, :, :half_ambit]
    lower_rim = fields[:, :, local_rows + half_ambit :]
    centre = fields[:, :, half_ambit : local_rows + half_ambit]
    from_above = shifted(lower_rim, "tile", 1)
    from_below = shifted(upper_rim, "tile", -1)
    centre = centre + from_above
    centre = centre + from_below
    squared = centre[:, 0] * centre[:, 0] + centre[:, 1] * centre[:, 1]
    partial_value = jnp.sum(own_weights[:, None, None] * squared, axis=0)
    intensity = lax.psum_scatter(partial_value, "kern", scatter_dimension=1, tiled=True)
    acid = 1.0 - jnp.exp(-EXPOSURE * intensity)
    resist_state = jnp.stack([acid, quencher], axis=0)
    for step_index in range(STEPS):
        resist_state = react(padded_2(resist_state, (("kern", 2), ("tile", 1)), 1))
    return (intensity, resist_state[0], resist_state[1])


def solution(mesh):
    placed = (P("tile", None), P(), P(), P("tile", "kern"))
    return jax.shard_map(
        on_device,
        mesh=mesh,
        in_specs=placed,
        out_specs=(P("tile", "kern"), P("tile", "kern"), P("tile", "kern")),
        check_vma=False,
    )
```

profile of v0, /device:TPU:4, one launch (start us, length us, event | category | flops | bytes accessed | tf_op | source)
XLA Modules:
  0.0 319.0 jit_solution(16350086096521838394)
XLA Ops:
  22.2 3.9 %copy.340 = bf16[96,8,8,128]{3,2,1,0:T(8,128)(2,1)} copy(bf16[96,8,8,128]{0,3,1,2:T(8,128)(2,1)} %copy-done.8) | data formatting | bytes 3145728 | tf_op jit(solution)/shard_map/stack | solution.py:69
  28.9 3.9 %copy.342 = bf16[96,8,8,128]{3,2,1,0:T(8,128)(2,1)} copy(bf16[96,8,8,128]{0,3,1,2:T(8,128)(2,1)} %copy-done.9) | data formatting | bytes 3145728 | tf_op jit(solution)/shard_map/stack | solution.py:69
  34.9 3.9 %copy.338 = bf16[96,8,8,128]{3,2,1,0:T(8,128)(2,1)} copy(bf16[96,8,8,128]{0,3,1,2:T(8,128)(2,1)} %copy-done.7) | data formatting | bytes 3145728 | tf_op jit(solution)/shard_map/stack | solution.py:69
  40.9 3.9 %copy.336 = bf16[96,8,8,128]{3,2,1,0:T(8,128)(2,1)} copy(bf16[96,8,8,128]{0,3,1,2:T(8,128)(2,1)} %copy-done.6) | data formatting | bytes 3145728 | tf_op jit(solution)/shard_map/stack | solution.py:69
  47.0 3.9 %copy.334 = bf16[96,8,8,128]{3,2,1,0:T(8,128)(2,1)} copy(bf16[96,8,8,128]{0,3,1,2:T(8,128)(2,1)} %copy-done.5) | data formatting | bytes 3145728 | tf_op jit(solution)/shard_map/stack | solution.py:69
  53.1 3.9 %copy.332 = bf16[96,8,8,128]{3,2,1,0:T(8,128)(2,1)} copy(bf16[96,8,8,128]{0,3,1,2:T(8,128)(2,1)} %copy-done.4) | data formatting | bytes 3145728 | tf_op jit(solution)/shard_map/stack | solution.py:69
  59.2 3.9 %copy.330 = bf16[96,8,8,128]{3,2,1,0:T(8,128)(2,1)} copy(bf16[96,8,8,128]{0,3,1,2:T(8,128)(2,1)} %copy-done.10) | data formatting | bytes 3145728 | tf_op jit(solution)/shard_map/stack | solution.py:69
  65.2 3.9 %copy.328 = bf16[96,8,8,128]{3,2,1,0:T(8,128)(2,1)} copy(bf16[96,8,8,128]{0,3,1,2:T(8,128)(2,1)} %copy-done.11) | data formatting | bytes 3145728 | tf_op jit(solution)/shard_map/stack | solution.py:69
  85.6 4.4 %reshape.131 = f32[96,8,6,2,64]{4,3,2,1,0:T(2,128)} reshape(f32[768,768]{1,0:T(8,128)S(1)} %add_add_fusion) | data formatting | bytes 4718592 | tf_op jit(solution)/shard_map/reshape | solution.py:81
  90.0 5.5 %copy.344 = f32[6,2,96,8,64]{2,4,3,1,0:T(8,128)S(1)} copy(f32[6,2,96,8,64]{4,1,0,3,2:T(2,128)} %bitcast.563) | data formatting | bytes 4718592 | tf_op jit(solution)/shard_map/transpose | solution.py:82
  95.5 5.6 %fusion.425 = (f32[6,2,32,512]{2,3,1,0:T(8,128)}, f32[6,2,32,512]{2,3,1,0:T(8,128)}, f32[6,2,32,512]{2,3,1,0:T(8,128)}) fusion(f32[6,2,96,512]{2,3,1,0:T(8,128)S(1)} %bitcast.562), kind=kLoop, calls=%fused_computation.691 | loop fusion | bytes 4718592 | tf_op jit(solution)/shard_map/slice | solution.py:98
  101.2 3.1 copy.346
  104.3 3.7 %collective-permute-start = (f32[6,2,32,512]{3,2,1,0:T(8,128)}, f32[6,2,32,512]{3,2,1,0:T(8,128)}, u32[]{:S(2)}, u32[]{:S(2)}) collective-permute-start(f32[6,2,32,512]{3,2,1,0:T(8,128)} %copy.346), channel_id=1, source_target_pairs={{0,1},{1,2},{2,3},{3,4},{4,5},{5,6},{6,7},{8,9},{9,10},{10,11},{11... | collective-permute-start | bytes 2359304 | tf_op jit(solution)/shard_map/ppermute | solution.py:18
  108.0 3.1 copy.347
  111.1 3.4 %collective-permute-start.1 = (f32[6,2,32,512]{3,2,1,0:T(8,128)}, f32[6,2,32,512]{3,2,1,0:T(8,128)}, u32[]{:S(2)}, u32[]{:S(2)}) collective-permute-start(f32[6,2,32,512]{3,2,1,0:T(8,128)} %copy.347), channel_id=1, source_target_pairs={{1,0},{2,1},{3,2},{4,3},{5,4},{6,5},{7,6},{9,8},{10,9},{11,10},{12... | collective-permute-start | bytes 2359304 | tf_op jit(solution)/shard_map/ppermute | solution.py:18
  116.7 26.2 %collective-permute-done = f32[6,2,32,512]{3,2,1,0:T(8,128)} collective-permute-done((f32[6,2,32,512]{3,2,1,0:T(8,128)}, f32[6,2,32,512]{3,2,1,0:T(8,128)}, u32[]{:S(2)}, u32[]{:S(2)}) %collective-permute-start) | collective-permute-done | bytes 786464 | tf_op jit(solution)/shard_map/ppermute | solution.py:18
  145.8 21.2 %reduce-scatter.2.cloned.1.call-done = f32[32,128]{0,1:T(8,128)} async-done(((f32[32,512]{0,1:T(8,128)}), f32[32,128]{0,1:T(8,128)}) %reduce-scatter.2.cloned.1.call-update) | async-done | bytes 16400 | tf_op jit(solution)/shard_map/reduce_scatter | solution.py:106
  173.1 3.4 %collective-permute-start.4 = (f32[2,1,130]{1,2,0:T(8,128)S(1)}, f32[2,1,130]{1,2,0:T(8,128)S(1)}, u32[]{:S(2)}, u32[]{:S(2)}) collective-permute-start(f32[2,1,130]{1,2,0:T(8,128)S(1)} %get-tuple-element.91), channel_id=1, source_target_pairs={{0,1},{1,2},{2,3},{3,4},{4,5},{5,6},{6,7},{8,9},{9,10},{10,11},{11... | collective-permute-start | bytes 3128 | tf_op jit(solution)/shard_map/ppermute | solution.py:26
  176.5 2.5 collective-permute-start.5
  180.1 4.6 %collective-permute-done.5 = f32[2,1,130]{1,2,0:T(8,128)S(1)} collective-permute-done((f32[2,1,130]{1,2,0:T(8,128)S(1)}, f32[2,1,130]{1,2,0:T(8,128)S(1)}, u32[]{:S(2)}, u32[]{:S(2)}) %collective-permute-start.5) | collective-permute-done | bytes 1072 | tf_op jit(solution)/shard_map/ppermute | solution.py:29
  185.8 2.8 collective-permute-start.6
  192.4 2.5 collective-permute-start.8
  195.0 3.3 %collective-permute-start.9 = (f32[2,1,130]{1,2,0:T(8,128)S(1)}, f32[2,1,130]{1,2,0:T(8,128)S(1)}, u32[]{:S(2)}, u32[]{:S(2)}) collective-permute-start(f32[2,1,130]{1,2,0:T(8,128)S(1)} %get-tuple-element.90), channel_id=1, source_target_pairs={{1,0},{2,1},{3,2},{4,3},{5,4},{6,5},{7,6},{9,8},{10,9},{11,10},{12... | collective-permute-start | bytes 3128 | tf_op jit(solution)/shard_map/ppermute | solution.py:29
  199.4 3.7 %collective-permute-done.9 = f32[2,1,130]{1,2,0:T(8,128)S(1)} collective-permute-done((f32[2,1,130]{1,2,0:T(8,128)S(1)}, f32[2,1,130]{1,2,0:T(8,128)S(1)}, u32[]{:S(2)}, u32[]{:S(2)}) %collective-permute-start.9) | collective-permute-done | bytes 1072 | tf_op jit(solution)/shard_map/ppermute | solution.py:29
  203.4 2.8 collective-permute-start.10
  210.0 3.4 %collective-permute-start.12 = (f32[2,1,130]{1,2,0:T(8,128)S(1)}, f32[2,1,130]{1,2,0:T(8,128)S(1)}, u32[]{:S(2)}, u32[]{:S(2)}) collective-permute-start(f32[2,1,130]{1,2,0:T(8,128)S(1)} %get-tuple-element.87), channel_id=1, source_target_pairs={{0,1},{1,2},{2,3},{3,4},{4,5},{5,6},{6,7},{8,9},{9,10},{10,11},{11... | collective-permute-start | bytes 3128 | tf_op jit(solution)/shard_map/ppermute | solution.py:26
  213.4 2.5 collective-permute-start.13
  217.0 4.6 %collective-permute-done.13 = f32[2,1,130]{1,2,0:T(8,128)S(1)} collective-permute-done((f32[2,1,130]{1,2,0:T(8,128)S(1)}, f32[2,1,130]{1,2,0:T(8,128)S(1)}, u32[]{:S(2)}, u32[]{:S(2)}) %collective-permute-start.13) | collective-permute-done | bytes 1072 | tf_op jit(solution)/shard_map/ppermute | solution.py:29
  221.9 2.8 collective-permute-start.14
  228.5 2.5 collective-permute-start.16
  231.0 3.3 %collective-permute-start.17 = (f32[2,1,130]{1,2,0:T(8,128)S(1)}, f32[2,1,130]{1,2,0:T(8,128)S(1)}, u32[]{:S(2)}, u32[]{:S(2)}) collective-permute-start(f32[2,1,130]{1,2,0:T(8,128)S(1)} %get-tuple-element.86), channel_id=1, source_target_pairs={{1,0},{2,1},{3,2},{4,3},{5,4},{6,5},{7,6},{9,8},{10,9},{11,10},{12... | collective-permute-start | bytes 3128 | tf_op jit(solution)/shard_map/ppermute | solution.py:29
  235.5 3.8 %collective-permute-done.17 = f32[2,1,130]{1,2,0:T(8,128)S(1)} collective-permute-done((f32[2,1,130]{1,2,0:T(8,128)S(1)}, f32[2,1,130]{1,2,0:T(8,128)S(1)}, u32[]{:S(2)}, u32[]{:S(2)}) %collective-permute-start.17) | collective-permute-done | bytes 1072 | tf_op jit(solution)/shard_map/ppermute | solution.py:29
  239.5 2.8 collective-permute-start.18
  246.1 3.3 %collective-permute-start.20 = (f32[2,1,130]{1,2,0:T(8,128)S(1)}, f32[2,1,130]{1,2,0:T(8,128)S(1)}, u32[]{:S(2)}, u32[]{:S(2)}) collective-permute-start(f32[2,1,130]{1,2,0:T(8,128)S(1)} %get-tuple-element.83), channel_id=1, source_target_pairs={{0,1},{1,2},{2,3},{3,4},{4,5},{5,6},{6,7},{8,9},{9,10},{10,11},{11... | collective-permute-start | bytes 3128 | tf_op jit(solution)/shard_map/ppermute | solution.py:26
  249.4 2.5 collective-permute-start.21
  253.1 4.6 %collective-permute-done.21 = f32[2,1,130]{1,2,0:T(8,128)S(1)} collective-permute-done((f32[2,1,130]{1,2,0:T(8,128)S(1)}, f32[2,1,130]{1,2,0:T(8,128)S(1)}, u32[]{:S(2)}, u32[]{:S(2)}) %collective-permute-start.21) | collective-permute-done | bytes 1072 | tf_op jit(solution)/shard_map/ppermute | solution.py:29
  257.9 2.8 collective-permute-start.22
  264.5 2.6 collective-permute-start.24
  267.1 3.3 %collective-permute-start.25 = (f32[2,1,130]{1,2,0:T(8,128)S(1)}, f32[2,1,130]{1,2,0:T(8,128)S(1)}, u32[]{:S(2)}, u32[]{:S(2)}) collective-permute-start(f32[2,1,130]{1,2,0:T(8,128)S(1)} %get-tuple-element.82), channel_id=1, source_target_pairs={{1,0},{2,1},{3,2},{4,3},{5,4},{6,5},{7,6},{9,8},{10,9},{11,10},{12... | collective-permute-start | bytes 3128 | tf_op jit(solution)/shard_map/ppermute | solution.py:29
  271.5 3.8 %collective-permute-done.25 = f32[2,1,130]{1,2,0:T(8,128)S(1)} collective-permute-done((f32[2,1,130]{1,2,0:T(8,128)S(1)}, f32[2,1,130]{1,2,0:T(8,128)S(1)}, u32[]{:S(2)}, u32[]{:S(2)}) %collective-permute-start.25) | collective-permute-done | bytes 1072 | tf_op jit(solution)/shard_map/ppermute | solution.py:29
  275.5 3.0 collective-permute-start.26
  282.3 2.5 collective-permute-start.28
  284.7 3.4 %collective-permute-start.29 = (f32[2,1,130]{1,2,0:T(8,128)S(1)}, f32[2,1,130]{1,2,0:T(8,128)S(1)}, u32[]{:S(2)}, u32[]{:S(2)}) collective-permute-start(f32[2,1,130]{1,2,0:T(8,128)S(1)} %get-tuple-element.80), channel_id=1, source_target_pairs={{1,0},{2,1},{3,2},{4,3},{5,4},{6,5},{7,6},{9,8},{10,9},{11,10},{12... | collective-permute-start | bytes 3128 | tf_op jit(solution)/shard_map/ppermute | solution.py:29
  289.3 4.0 %collective-permute-done.29 = f32[2,1,130]{1,2,0:T(8,128)S(1)} collective-permute-done((f32[2,1,130]{1,2,0:T(8,128)S(1)}, f32[2,1,130]{1,2,0:T(8,128)S(1)}, u32[]{:S(2)}, u32[]{:S(2)}) %collective-permute-start.29) | collective-permute-done | bytes 1072 | tf_op jit(solution)/shard_map/ppermute | solution.py:29
  293.5 2.5 collective-permute-start.30
  299.4 2.8 collective-permute-start.32
  302.2 3.1 collective-permute-start.33
  306.4 4.2 %collective-permute-done.33 = f32[2,1,130]{1,2,0:T(8,128)S(1)} collective-permute-done((f32[2,1,130]{1,2,0:T(8,128)S(1)}, f32[2,1,130]{1,2,0:T(8,128)S(1)}, u32[]{:S(2)}, u32[]{:S(2)}) %collective-permute-start.33) | collective-permute-done | bytes 1072 | tf_op jit(solution)/shard_map/ppermute | solution.py:29
  (208 shorter events, 96.6 us)
Async XLA Ops:
  7.2 19.0 %copy-start = (bf16[24,2,64,64]{3,2,1,0:T(8,128)(2,1)S(1)}, bf16[24,2,64,64]{3,2,1,0:T(8,128)(2,1)}, u32[]{:S(2)}) copy-start(bf16[24,2,64,64]{3,2,1,0:T(8,128)(2,1)} %param.5) | copy-start | bytes 1179652
  7.2 159.8 %reduce-scatter.2.cloned.1.call-start = ((), (), s32[]{:S(2)}) async-start(), calls=%async_computation.1 | async-start | bytes 327680 | tf_op jit(solution)/shard_map/reduce_scatter | solution.py:106
  69.1 1.9 copy-start.19
  71.0 1.9 copy-start.20
  72.9 1.9 copy-start.21
  74.7 1.9 copy-start.22
  76.6 1.9 copy-start.23
  78.5 1.9 copy-start.24
  80.4 1.9 copy-start.25
  104.3 10.2 %copy-start.2 = (f32[6,2,32,512]{2,3,1,0:T(8,128)S(1)}, f32[6,2,32,512]{2,3,1,0:T(8,128)}, u32[]{:S(2)}) copy-start(f32[6,2,32,512]{2,3,1,0:T(8,128)} %get-tuple-element.20) | copy-start | bytes 2359300
  104.3 38.6 %collective-permute-start = (f32[6,2,32,512]{3,2,1,0:T(8,128)}, f32[6,2,32,512]{3,2,1,0:T(8,128)}, u32[]{:S(2)}, u32[]{:S(2)}) collective-permute-start(f32[6,2,32,512]{3,2,1,0:T(8,128)} %copy.346), channel_id=1, source_target_pairs={{0,1},{1,2},{2,3},{3,4},{4,5},{5,6},{6,7},{8,9},{9,10},{10,11},{11... | collective-permute-start | bytes 2359304 | tf_op jit(solution)/shard_map/ppermute | solution.py:18
  111.1 5.6 %copy-start.28 = (f32[24]{0:T(128)S(1)}, f32[24]{0:T(128)}, u32[]{:S(2)}) copy-start(f32[24]{0:T(128)} %param.6) | copy-start | bytes 292
  111.1 31.8 %collective-permute-start.1 = (f32[6,2,32,512]{3,2,1,0:T(8,128)}, f32[6,2,32,512]{3,2,1,0:T(8,128)}, u32[]{:S(2)}, u32[]{:S(2)}) collective-permute-start(f32[6,2,32,512]{3,2,1,0:T(8,128)} %copy.347), channel_id=1, source_target_pairs={{1,0},{2,1},{3,2},{4,3},{5,4},{6,5},{7,6},{9,8},{10,9},{11,10},{12... | collective-permute-start | bytes 2359304 | tf_op jit(solution)/shard_map/ppermute | solution.py:18
  116.7 29.0 %copy-start.27 = (f32[32,128]{1,0:T(8,128)S(1)}, f32[32,128]{1,0:T(8,128)}, u32[]{:S(2)}) copy-start(f32[32,128]{1,0:T(8,128)} %param.7) | copy-start | bytes 49156
  167.9 3.0 collective-permute-start.2
  169.6 3.4 %collective-permute-start.3 = (f32[2,32,1]{1,2,0:T(1,128)S(1)}, f32[2,32,1]{1,2,0:T(1,128)S(1)}, u32[]{:S(2)}, u32[]{:S(2)}) collective-permute-start(f32[2,32,1]{1,2,0:T(1,128)S(1)} %get-tuple-element.108), channel_id=1, source_target_pairs={{8,0},{16,8},{24,16},{9,1},{17,9},{25,17},{10,2},{18,10},{26,18},{... | collective-permute-start | bytes 776 | tf_op jit(solution)/shard_map/ppermute | solution.py:29
  173.1 7.0 %collective-permute-start.4 = (f32[2,1,130]{1,2,0:T(8,128)S(1)}, f32[2,1,130]{1,2,0:T(8,128)S(1)}, u32[]{:S(2)}, u32[]{:S(2)}) collective-permute-start(f32[2,1,130]{1,2,0:T(8,128)S(1)} %get-tuple-element.91), channel_id=1, source_target_pairs={{0,1},{1,2},{2,3},{3,4},{4,5},{5,6},{6,7},{8,9},{9,10},{10,11},{11... | collective-permute-start | bytes 3128 | tf_op jit(solution)/shard_map/ppermute | solution.py:26
  176.5 8.2 %collective-permute-start.5 = (f32[2,1,130]{1,2,0:T(8,128)S(1)}, f32[2,1,130]{1,2,0:T(8,128)S(1)}, u32[]{:S(2)}, u32[]{:S(2)}) collective-permute-start(f32[2,1,130]{1,2,0:T(8,128)S(1)} %get-tuple-element.92), channel_id=1, source_target_pairs={{1,0},{2,1},{3,2},{4,3},{5,4},{6,5},{7,6},{9,8},{10,9},{11,10},{12... | collective-permute-start | bytes 3128 | tf_op jit(solution)/shard_map/ppermute | solution.py:29
  185.8 4.1 %collective-permute-start.6 = (f32[2,32,1]{1,2,0:T(1,128)S(1)}, f32[2,32,1]{1,2,0:T(1,128)S(1)}, u32[]{:S(2)}, u32[]{:S(2)}) collective-permute-start(f32[2,32,1]{1,2,0:T(1,128)S(1)} %get-tuple-element.105), channel_id=1, source_target_pairs={{0,8},{8,16},{16,24},{1,9},{9,17},{17,25},{2,10},{10,18},{18,26},{... | collective-permute-start | bytes 776 | tf_op jit(solution)/shard_map/ppermute | solution.py:26
  188.7 3.6 %collective-permute-start.7 = (f32[2,32,1]{1,2,0:T(1,128)S(1)}, f32[2,32,1]{1,2,0:T(1,128)S(1)}, u32[]{:S(2)}, u32[]{:S(2)}) collective-permute-start(f32[2,32,1]{1,2,0:T(1,128)S(1)} %get-tuple-element.106), channel_id=1, source_target_pairs={{8,0},{16,8},{24,16},{9,1},{17,9},{25,17},{10,2},{18,10},{26,18},{... | collective-permute-start | bytes 776 | tf_op jit(solution)/shard_map/ppermute | solution.py:29
  192.4 7.0 %collective-permute-start.8 = (f32[2,1,130]{1,2,0:T(8,128)S(1)}, f32[2,1,130]{1,2,0:T(8,128)S(1)}, u32[]{:S(2)}, u32[]{:S(2)}) collective-permute-start(f32[2,1,130]{1,2,0:T(8,128)S(1)} %get-tuple-element.89), channel_id=1, source_target_pairs={{0,1},{1,2},{2,3},{3,4},{4,5},{5,6},{6,7},{8,9},{9,10},{10,11},{11... | collective-permute-start | bytes 3128 | tf_op jit(solution)/shard_map/ppermute | solution.py:26
  195.0 8.2 %collective-permute-start.9 = (f32[2,1,130]{1,2,0:T(8,128)S(1)}, f32[2,1,130]{1,2,0:T(8,128)S(1)}, u32[]{:S(2)}, u32[]{:S(2)}) collective-permute-start(f32[2,1,130]{1,2,0:T(8,128)S(1)} %get-tuple-element.90), channel_id=1, source_target_pairs={{1,0},{2,1},{3,2},{4,3},{5,4},{6,5},{7,6},{9,8},{10,9},{11,10},{12... | collective-permute-start | bytes 3128 | tf_op jit(solution)/shard_map/ppermute | solution.py:29
  203.4 4.1 %collective-permute-start.10 = (f32[2,32,1]{1,2,0:T(1,128)S(1)}, f32[2,32,1]{1,2,0:T(1,128)S(1)}, u32[]{:S(2)}, u32[]{:S(2)}) collective-permute-start(f32[2,32,1]{1,2,0:T(1,128)S(1)} %get-tuple-element.103), channel_id=1, source_target_pairs={{0,8},{8,16},{16,24},{1,9},{9,17},{17,25},{2,10},{10,18},{18,26},{... | collective-permute-start | bytes 776 | tf_op jit(solution)/shard_map/ppermute | solution.py:26
  206.3 3.6 %collective-permute-start.11 = (f32[2,32,1]{1,2,0:T(1,128)S(1)}, f32[2,32,1]{1,2,0:T(1,128)S(1)}, u32[]{:S(2)}, u32[]{:S(2)}) collective-permute-start(f32[2,32,1]{1,2,0:T(1,128)S(1)} %get-tuple-element.104), channel_id=1, source_target_pairs={{8,0},{16,8},{24,16},{9,1},{17,9},{25,17},{10,2},{18,10},{26,18},{... | collective-permute-start | bytes 776 | tf_op jit(solution)/shard_map/ppermute | solution.py:29
  210.0 7.0 %collective-permute-start.12 = (f32[2,1,130]{1,2,0:T(8,128)S(1)}, f32[2,1,130]{1,2,0:T(8,128)S(1)}, u32[]{:S(2)}, u32[]{:S(2)}) collective-permute-start(f32[2,1,130]{1,2,0:T(8,128)S(1)} %get-tuple-element.87), channel_id=1, source_target_pairs={{0,1},{1,2},{2,3},{3,4},{4,5},{5,6},{6,7},{8,9},{9,10},{10,11},{11... | collective-permute-start | bytes 3128 | tf_op jit(solution)/shard_map/ppermute | solution.py:26
  213.4 8.2 %collective-permute-start.13 = (f32[2,1,130]{1,2,0:T(8,128)S(1)}, f32[2,1,130]{1,2,0:T(8,128)S(1)}, u32[]{:S(2)}, u32[]{:S(2)}) collective-permute-start(f32[2,1,130]{1,2,0:T(8,128)S(1)} %get-tuple-element.88), channel_id=1, source_target_pairs={{1,0},{2,1},{3,2},{4,3},{5,4},{6,5},{7,6},{9,8},{10,9},{11,10},{12... | collective-permute-start | bytes 3128 | tf_op jit(solution)/shard_map/ppermute | solution.py:29
  221.9 4.1 %collective-permute-start.14 = (f32[2,32,1]{1,2,0:T(1,128)S(1)}, f32[2,32,1]{1,2,0:T(1,128)S(1)}, u32[]{:S(2)}, u32[]{:S(2)}) collective-permute-start(f32[2,32,1]{1,2,0:T(1,128)S(1)} %get-tuple-element.101), channel_id=1, source_target_pairs={{0,8},{8,16},{16,24},{1,9},{9,17},{17,25},{2,10},{10,18},{18,26},{... | collective-permute-start | bytes 776 | tf_op jit(solution)/shard_map/ppermute | solution.py:26
  224.7 3.6 %collective-permute-start.15 = (f32[2,32,1]{1,2,0:T(1,128)S(1)}, f32[2,32,1]{1,2,0:T(1,128)S(1)}, u32[]{:S(2)}, u32[]{:S(2)}) collective-permute-start(f32[2,32,1]{1,2,0:T(1,128)S(1)} %get-tuple-element.102), channel_id=1, source_target_pairs={{8,0},{16,8},{24,16},{9,1},{17,9},{25,17},{10,2},{18,10},{26,18},{... | collective-permute-start | bytes 776 | tf_op jit(solution)/shard_map/ppermute | solution.py:29
  228.5 7.0 %collective-permute-start.16 = (f32[2,1,130]{1,2,0:T(8,128)S(1)}, f32[2,1,130]{1,2,0:T(8,128)S(1)}, u32[]{:S(2)}, u32[]{:S(2)}) collective-permute-start(f32[2,1,130]{1,2,0:T(8,128)S(1)} %get-tuple-element.85), channel_id=1, source_target_pairs={{0,1},{1,2},{2,3},{3,4},{4,5},{5,6},{6,7},{8,9},{9,10},{10,11},{11... | collective-permute-start | bytes 3128 | tf_op jit(solution)/shard_map/ppermute | solution.py:26
  231.0 8.2 %collective-permute-start.17 = (f32[2,1,130]{1,2,0:T(8,128)S(1)}, f32[2,1,130]{1,2,0:T(8,128)S(1)}, u32[]{:S(2)}, u32[]{:S(2)}) collective-permute-start(f32[2,1,130]{1,2,0:T(8,128)S(1)} %get-tuple-element.86), channel_id=1, source_target_pairs={{1,0},{2,1},{3,2},{4,3},{5,4},{6,5},{7,6},{9,8},{10,9},{11,10},{12... | collective-permute-start | bytes 3128 | tf_op jit(solution)/shard_map/ppermute | solution.py:29
  239.5 4.1 %collective-permute-start.18 = (f32[2,32,1]{1,2,0:T(1,128)S(1)}, f32[2,32,1]{1,2,0:T(1,128)S(1)}, u32[]{:S(2)}, u32[]{:S(2)}) collective-permute-start(f32[2,32,1]{1,2,0:T(1,128)S(1)} %get-tuple-element.99), channel_id=1, source_target_pairs={{0,8},{8,16},{16,24},{1,9},{9,17},{17,25},{2,10},{10,18},{18,26},{... | collective-permute-start | bytes 776 | tf_op jit(solution)/shard_map/ppermute | solution.py:26
  242.3 3.6 %collective-permute-start.19 = (f32[2,32,1]{1,2,0:T(1,128)S(1)}, f32[2,32,1]{1,2,0:T(1,128)S(1)}, u32[]{:S(2)}, u32[]{:S(2)}) collective-permute-start(f32[2,32,1]{1,2,0:T(1,128)S(1)} %get-tuple-element.100), channel_id=1, source_target_pairs={{8,0},{16,8},{24,16},{9,1},{17,9},{25,17},{10,2},{18,10},{26,18},{... | collective-permute-start | bytes 776 | tf_op jit(solution)/shard_map/ppermute | solution.py:29
  246.1 7.0 %collective-permute-start.20 = (f32[2,1,130]{1,2,0:T(8,128)S(1)}, f32[2,1,130]{1,2,0:T(8,128)S(1)}, u32[]{:S(2)}, u32[]{:S(2)}) collective-permute-start(f32[2,1,130]{1,2,0:T(8,128)S(1)} %get-tuple-element.83), channel_id=1, source_target_pairs={{0,1},{1,2},{2,3},{3,4},{4,5},{5,6},{6,7},{8,9},{9,10},{10,11},{11... | collective-permute-start | bytes 3128 | tf_op jit(solution)/shard_map/ppermute | solution.py:26
  249.4 8.2 %collective-permute-start.21 = (f32[2,1,130]{1,2,0:T(8,128)S(1)}, f32[2,1,130]{1,2,0:T(8,128)S(1)}, u32[]{:S(2)}, u32[]{:S(2)}) collective-permute-start(f32[2,1,130]{1,2,0:T(8,128)S(1)} %get-tuple-element.84), channel_id=1, source_target_pairs={{1,0},{2,1},{3,2},{4,3},{5,4},{6,5},{7,6},{9,8},{10,9},{11,10},{12... | collective-permute-start | bytes 3128 | tf_op jit(solution)/shard_map/ppermute | solution.py:29
  257.9 4.1 %collective-permute-start.22 = (f32[2,32,1]{1,2,0:T(1,128)S(1)}, f32[2,32,1]{1,2,0:T(1,128)S(1)}, u32[]{:S(2)}, u32[]{:S(2)}) collective-permute-start(f32[2,32,1]{1,2,0:T(1,128)S(1)} %get-tuple-element.97), channel_id=1, source_target_pairs={{0,8},{8,16},{16,24},{1,9},{9,17},{17,25},{2,10},{10,18},{18,26},{... | collective-permute-start | bytes 776 | tf_op jit(solution)/shard_map/ppermute | solution.py:26
  260.7 3.6 %collective-permute-start.23 = (f32[2,32,1]{1,2,0:T(1,128)S(1)}, f32[2,32,1]{1,2,0:T(1,128)S(1)}, u32[]{:S(2)}, u32[]{:S(2)}) collective-permute-start(f32[2,32,1]{1,2,0:T(1,128)S(1)} %get-tuple-element.98), channel_id=1, source_target_pairs={{8,0},{16,8},{24,16},{9,1},{17,9},{25,17},{10,2},{18,10},{26,18},{... | collective-permute-start | bytes 776 | tf_op jit(solution)/shard_map/ppermute | solution.py:29
  264.4 40.9 %copy-start.26 = (f32[32,128]{0,1:T(8,128)S(1)}, f32[32,128]{0,1:T(8,128)}, u32[]{:S(2)}) copy-start(f32[32,128]{0,1:T(8,128)} %reduce-scatter.2.cloned.1.call-done) | copy-start | bytes 49156
  264.5 7.0 %collective-permute-start.24 = (f32[2,1,130]{1,2,0:T(8,128)S(1)}, f32[2,1,130]{1,2,0:T(8,128)S(1)}, u32[]{:S(2)}, u32[]{:S(2)}) collective-permute-start(f32[2,1,130]{1,2,0:T(8,128)S(1)} %get-tuple-element.81), channel_id=1, source_target_pairs={{0,1},{1,2},{2,3},{3,4},{4,5},{5,6},{6,7},{8,9},{9,10},{10,11},{11... | collective-permute-start | bytes 3128 | tf_op jit(solution)/shard_map/ppermute | solution.py:26
  267.1 8.2 %collective-permute-start.25 = (f32[2,1,130]{1,2,0:T(8,128)S(1)}, f32[2,1,130]{1,2,0:T(8,128)S(1)}, u32[]{:S(2)}, u32[]{:S(2)}) collective-permute-start(f32[2,1,130]{1,2,0:T(8,128)S(1)} %get-tuple-element.82), channel_id=1, source_target_pairs={{1,0},{2,1},{3,2},{4,3},{5,4},{6,5},{7,6},{9,8},{10,9},{11,10},{12... | collective-permute-start | bytes 3128 | tf_op jit(solution)/shard_map/ppermute | solution.py:29
  275.5 36.7 %copy-start.1 = (bf16[24,2,64,64]{3,2,1,0:T(8,128)(2,1)S(1)}, bf16[24,2,64,64]{3,2,1,0:T(8,128)(2,1)}, u32[]{:S(2)}) copy-start(bf16[24,2,64,64]{3,2,1,0:T(8,128)(2,1)} %param.5) | copy-start | bytes 1179652
  275.5 4.3 %collective-permute-start.26 = (f32[2,32,1]{1,2,0:T(1,128)S(1)}, f32[2,32,1]{1,2,0:T(1,128)S(1)}, u32[]{:S(2)}, u32[]{:S(2)}) collective-permute-start(f32[2,32,1]{1,2,0:T(1,128)S(1)} %get-tuple-element.95), channel_id=1, source_target_pairs={{0,8},{8,16},{16,24},{1,9},{9,17},{17,25},{2,10},{10,18},{18,26},{... | collective-permute-start | bytes 776 | tf_op jit(solution)/shard_map/ppermute | solution.py:26
  278.5 3.6 %collective-permute-start.27 = (f32[2,32,1]{1,2,0:T(1,128)S(1)}, f32[2,32,1]{1,2,0:T(1,128)S(1)}, u32[]{:S(2)}, u32[]{:S(2)}) collective-permute-start(f32[2,32,1]{1,2,0:T(1,128)S(1)} %get-tuple-element.96), channel_id=1, source_target_pairs={{8,0},{16,8},{24,16},{9,1},{17,9},{25,17},{10,2},{18,10},{26,18},{... | collective-permute-start | bytes 776 | tf_op jit(solution)/shard_map/ppermute | solution.py:29
  282.3 7.0 %collective-permute-start.28 = (f32[2,1,130]{1,2,0:T(8,128)S(1)}, f32[2,1,130]{1,2,0:T(8,128)S(1)}, u32[]{:S(2)}, u32[]{:S(2)}) collective-permute-start(f32[2,1,130]{1,2,0:T(8,128)S(1)} %get-tuple-element.79), channel_id=1, source_target_pairs={{0,1},{1,2},{2,3},{3,4},{4,5},{5,6},{6,7},{8,9},{9,10},{10,11},{11... | collective-permute-start | bytes 3128 | tf_op jit(solution)/shard_map/ppermute | solution.py:26
  284.7 8.5 %collective-permute-start.29 = (f32[2,1,130]{1,2,0:T(8,128)S(1)}, f32[2,1,130]{1,2,0:T(8,128)S(1)}, u32[]{:S(2)}, u32[]{:S(2)}) collective-permute-start(f32[2,1,130]{1,2,0:T(8,128)S(1)} %get-tuple-element.80), channel_id=1, source_target_pairs={{1,0},{2,1},{3,2},{4,3},{5,4},{6,5},{7,6},{9,8},{10,9},{11,10},{12... | collective-permute-start | bytes 3128 | tf_op jit(solution)/shard_map/ppermute | solution.py:29
  293.5 3.8 %collective-permute-start.30 = (f32[2,32,1]{1,2,0:T(1,128)S(1)}, f32[2,32,1]{1,2,0:T(1,128)S(1)}, u32[]{:S(2)}, u32[]{:S(2)}) collective-permute-start(f32[2,32,1]{1,2,0:T(1,128)S(1)} %get-tuple-element.93), channel_id=1, source_target_pairs={{0,8},{8,16},{16,24},{1,9},{9,17},{17,25},{2,10},{10,18},{18,26},{... | collective-permute-start | bytes 776 | tf_op jit(solution)/shard_map/ppermute | solution.py:26
  296.0 3.2 %collective-permute-start.31 = (f32[2,32,1]{1,2,0:T(1,128)S(1)}, f32[2,32,1]{1,2,0:T(1,128)S(1)}, u32[]{:S(2)}, u32[]{:S(2)}) collective-permute-start(f32[2,32,1]{1,2,0:T(1,128)S(1)} %get-tuple-element.94), channel_id=1, source_target_pairs={{8,0},{16,8},{24,16},{9,1},{17,9},{25,17},{10,2},{18,10},{26,18},{... | collective-permute-start | bytes 776 | tf_op jit(solution)/shard_map/ppermute | solution.py:29
  299.4 7.0 %collective-permute-start.32 = (f32[2,1,130]{1,2,0:T(8,128)S(1)}, f32[2,1,130]{1,2,0:T(8,128)S(1)}, u32[]{:S(2)}, u32[]{:S(2)}) collective-permute-start(f32[2,1,130]{1,2,0:T(8,128)S(1)} %get-tuple-element.77), channel_id=1, source_target_pairs={{0,1},{1,2},{2,3},{3,4},{4,5},{5,6},{6,7},{8,9},{9,10},{10,11},{11... | collective-permute-start | bytes 3128 | tf_op jit(solution)/shard_map/ppermute | solution.py:26
  302.2 8.4 %collective-permute-start.33 = (f32[2,1,130]{1,2,0:T(8,128)S(1)}, f32[2,1,130]{1,2,0:T(8,128)S(1)}, u32[]{:S(2)}, u32[]{:S(2)}) collective-permute-start(f32[2,1,130]{1,2,0:T(8,128)S(1)} %get-tuple-element.78), channel_id=1, source_target_pairs={{1,0},{2,1},{3,2},{4,3},{5,4},{6,5},{7,6},{9,8},{10,9},{11,10},{12... | collective-permute-start | bytes 3128 | tf_op jit(solution)/shard_map/ppermute | solution.py:29
  (16 other events, 23.2 us)
Sparse Core Ops, SparseCore 0:
  145.8 21.1 reduce-scatter.1
where the time goes:
time: 322 us; the launch traced here: 319 us
  waiting for transfers between devices  107 us (33%)
  starting transfers between devices  85.6 us (27%)
  local copies, waits for them, and re-layouts  78 us (24%)
  other arithmetic  16.5 us (5%)
  matrix products  16.5 us (5%)
  between operations  15.2 us (5%)
    ppermute x16, waiting for transfers between devices, padded_2(): lax.ppermute(lax.slice_in_dim(block, 0, width, axis=dim), axis, backward)  51.3 us
    ppermute x16, starting transfers between devices, padded_2(): lax.ppermute(lax.slice_in_dim(block, block.shape[dim] - width, None, axis...  44.3 us
    ppermute x16, starting transfers between devices, padded_2(): lax.ppermute(lax.slice_in_dim(block, 0, width, axis=dim), axis, backward)  34.1 us
    another operation x8, local copies, waits for them, and re-layouts, field_band(): jnp.stack([windows[first + offset:first + offset + band_rows] for offset...  31.3 us
    ppermute x2, waiting for transfers between devices, shifted(): lax.ppermute(value, axis, [(source, source + steps) for source in range(l...  26.2 us
    reduce_scatter x1, waiting for transfers between devices, on_device(): lax.psum_scatter(partial_value, 'kern', scatter_dimension=1, tiled=True)  21.2 us
    unnamed x65, local copies, waits for them, and re-layouts  12.8 us
    dot_general x8, matrix products, field_band(): jnp.dot(left_side, right_side, preferred_element_type=jnp.float32)  11.9 us
  transfers between devices with their start and end apart: 35, of which 26 were waited for; matrix products, arithmetic and copies ran while one was open for 2% of the time, Pallas kernels for 0%

commit v1 on v0

v1 whole, which is shorter than its diff:
```python
import functools

import jax
import jax.numpy as jnp
from jax import lax
from jax.experimental import pallas as pl
from jax.experimental.pallas import tpu as pltpu
from jax.sharding import PartitionSpec as P

STEPS = 8
DIFFUSE_ACID = 0.2
DIFFUSE_BASE = 0.1
QUENCH_RATE = 0.5
EXPOSURE = 0.35

LANES = 128
RIM = 8
GROUP = 4


def lane_roll_left(value, amount):
    width = value.shape[1]
    amount %= width
    return value if amount == 0 else pltpu.roll(value, width - amount, 1)


def three_blocks(ref, rows, kern, kern_count):
    blocks = []
    for step in (-1, 0, 1):
        place = jnp.clip(kern + step, 0, kern_count - 1)
        block = ref[rows, pl.ds(pl.multiple_of(place * LANES, LANES), LANES)].astype(jnp.float32)
        inside = jnp.logical_and(kern + step >= 0, kern + step < kern_count)
        blocks.append(jnp.where(inside, block, 0.0))
    return jnp.concatenate(blocks, axis=1)


def prepare_kernel(kern_count, tile_count, lead, mask_ref, quencher_ref, send_ref, window_ref):
    kern, tile = lax.axis_index("kern"), lax.axis_index("tile")
    rows = mask_ref.shape[0]
    window_ref[...] = lane_roll_left(
        three_blocks(mask_ref, slice(None), kern, kern_count), LANES - lead
    )[:, : 2 * LANES]
    send_ref[...] = jnp.zeros_like(send_ref)
    own = pl.ds(pl.multiple_of(kern * LANES, LANES), LANES)
    for step, value in (
        (1, quencher_ref[rows - RIM :, :]),
        (-1, quencher_ref[:RIM, :]),
        (2, mask_ref[rows - RIM :, own].astype(jnp.float32)),
        (-2, mask_ref[:RIM, own].astype(jnp.float32)),
    ):
        target = tile + step

        @pl.when(jnp.logical_and(target >= 0, target < tile_count))
        def _(target=target, value=value):
            for column in range(kern_count):
                send_ref[column, target] = value

    lane = lax.broadcasted_iota(jnp.int32, (RIM, LANES), 1)
    for step, first in ((-1, 0), (1, LANES - RIM)):
        edge = jnp.zeros((RIM, LANES), jnp.float32)
        for part in range(rows // RIM):
            moved = lane_roll_left(quencher_ref[RIM * part : RIM * part + RIM, :], first - RIM * part)
            here = jnp.logical_and(lane >= RIM * part, lane < RIM * part + RIM)
            edge = jnp.where(here, moved, edge)
        target = kern + step

        @pl.when(jnp.logical_and(target >= 0, target < kern_count))
        def _(target=target, edge=edge):
            send_ref[target, tile] = edge


def shifted(value, axis, steps):
    count = lax.axis_size(axis)
    leading, last = (max(0, -steps), min(count, count - steps))
    return lax.ppermute(value, axis, [(source, source + steps) for source in range(leading, last)])


def resist_kernel(
    kern_count,
    tile_count,
    ambit,
    own_ref,
    above_ref,
    below_ref,
    received_ref,
    quencher_ref,
    taps_ref,
    weights_ref,
    intensity_ref,
    acid_ref,
    base_ref,
    rows_ref,
    slanted_ref,
    main_ref,
    strip_ref,
    total_ref,
    image_ref,
):
    kern, tile = lax.axis_index("kern"), lax.axis_index("tile")
    rows = own_ref.shape[0]
    lead = ambit // 2 + RIM
    height = rows + 2 * RIM
    span = rows + 2 * lead
    planes = taps_ref.shape[0] // (ambit // GROUP)

    def far_rows(step):
        place = jnp.clip(tile + step, 0, tile_count - 1)
        inside_tile = jnp.logical_and(tile + step >= 0, tile + step < tile_count)
        blocks = []
        for side in (-1, 0, 1):
            column = jnp.clip(kern + side, 0, kern_count - 1)
            inside = jnp.logical_and(kern + side >= 0, kern + side < kern_count)
            block = received_ref[column, place]
            blocks.append(jnp.where(jnp.logical_and(inside, inside_tile), block, 0.0))
        return lane_roll_left(jnp.concatenate(blocks, axis=1), LANES - lead)[:, : 2 * LANES]

    rows_ref[:RIM, :] = far_rows(-2)
    rows_ref[RIM : RIM + rows, :] = above_ref[...]
    rows_ref[RIM + rows : RIM + 2 * rows, :] = own_ref[...]
    rows_ref[RIM + 2 * rows : RIM + 3 * rows, :] = below_ref[...]
    rows_ref[RIM + 3 * rows :, :] = far_rows(2)

    window = rows_ref[...]
    for shift in range(8):
        moved = lane_roll_left(window, shift)
        for half in range(2):
            slanted_ref[half, pl.ds(shift, span, stride=8), :] = moved[:, LANES * half : LANES * half + LANES]

    lane = lax.broadcasted_iota(jnp.int32, (8, LANES), 1)

    def slant(row, carry):
        at = pl.multiple_of(row * 8, 8)
        after = pl.multiple_of(jnp.minimum(row + 1, span - 1) * 8, 8)
        low, high = slanted_ref[0, pl.ds(at, 8), :], slanted_ref[1, pl.ds(at, 8), :]
        next_high = slanted_ref[1, pl.ds(after, 8), :]
        for pair in range(ambit // 16):
            mains, strips = [], []
            for offset in (16 * pair, 16 * pair + 8):
                moved_high = lane_roll_left(high, offset)
                mains.append(jnp.where(lane < LANES - offset, lane_roll_left(low, offset), moved_high))
                strips.append(
                    jnp.where(lane < LANES // 2, moved_high, lane_roll_left(next_high, offset - LANES // 2))
                )
            place = pl.ds(pl.multiple_of(row * ambit + 16 * pair, 16), 16)
            main_ref[place, :] = jnp.concatenate(mains, axis=0).astype(jnp.bfloat16)
            strip_ref[place, :] = jnp.concatenate(strips, axis=0).astype(jnp.bfloat16)
        return carry

    lax.fori_loop(0, span, slant, 0, unroll=4)

    groups = height // GROUP
    tap_groups = ambit // GROUP
    tile_depth = GROUP * ambit
    total_ref[...] = jnp.zeros_like(total_ref)
    for s in range(groups + tap_groups - 1):
        first, last = max(0, s - tap_groups + 1), min(groups - 1, s)
        taps = taps_ref[planes * (tap_groups - 1 - s + first) : planes * (tap_groups - s + last), :]
        at = s * tile_depth
        for part, pieces in enumerate(
            (
                (main_ref[at : at + tile_depth], main_ref[at + ambit : at + ambit + tile_depth]),
                (main_ref[at + 2 * ambit : at + 2 * ambit + tile_depth], main_ref[at + 3 * ambit : at + 3 * ambit + tile_depth]),
                (strip_ref[at : at + tile_depth], strip_ref[at + 2 * ambit : at + 2 * ambit + tile_depth]),
            )
        ):
            total_ref[planes * first : planes * (last + 1), 2 * LANES * part : 2 * LANES * (part + 1)] += jnp.dot(
                taps, jnp.concatenate(pieces, axis=1), preferred_element_type=jnp.float32
            )

    plane = lax.broadcasted_iota(jnp.int32, (planes, 1), 0)
    weight = jnp.zeros((planes, 1), jnp.float32)
    for member in range(planes // 2):
        weight = jnp.where(plane // 2 == member, weights_ref[member], weight)
    for group in range(groups):
        field = total_ref[planes * group : planes * (group + 1), :]
        summed = jnp.sum(weight * (field * field), axis=0, keepdims=True)
        for part in range(GROUP):
            row = GROUP * group + part
            image_ref[row : row + 1, :LANES] = summed[:, LANES * part : LANES * (part + 1)]
            at = LANES * (GROUP + part // 2)
            strip = summed[:, at : at + LANES]
            image_ref[row : row + 1, LANES:] = strip if part % 2 == 0 else lane_roll_left(strip, LANES // 2)

    image = image_ref[...]
    row_id = lax.broadcasted_iota(jnp.int32, image.shape, 0)
    lane_id = lax.broadcasted_iota(jnp.int32, image.shape, 1)
    at_row = tile * rows + row_id - RIM
    at_column = kern * LANES + lane_id - RIM
    valid = (at_row >= 0) & (at_row < tile_count * rows) & (at_column >= 0) & (at_column < kern_count * LANES)
    valid = valid & (lane_id < LANES + 2 * RIM)

    def rim_rows(step):
        place = jnp.clip(tile + step, 0, tile_count - 1)
        return jnp.concatenate(
            [received_ref[jnp.clip(kern + side, 0, kern_count - 1), place] for side in (-1, 0, 1)], axis=1
        )

    before = received_ref[jnp.clip(kern - 1, 0, kern_count - 1), tile]
    after = received_ref[jnp.clip(kern + 1, 0, kern_count - 1), tile]
    middle = [
        jnp.concatenate(
            [
                lane_roll_left(before, RIM * part + RIM),
                quencher_ref[RIM * part : RIM * part + RIM, :],
                lane_roll_left(after, RIM * part),
            ],
            axis=1,
        )
        for part in range(rows // RIM)
    ]
    base = jnp.concatenate([rim_rows(-1)] + middle + [rim_rows(1)], axis=0)
    base = lane_roll_left(base, LANES - RIM)[:, : 2 * LANES]
    base = jnp.where(valid, base, 0.0)
    acid = jnp.where(valid, 1.0 - jnp.exp(-EXPOSURE * image), 0.0)

    def spread(value):
        return (
            pltpu.roll(value, 1, 0)
            + pltpu.roll(value, value.shape[0] - 1, 0)
            + pltpu.roll(value, 1, 1)
            + pltpu.roll(value, value.shape[1] - 1, 1)
            - 4.0 * value
        )

    for _ in range(STEPS):
        quenched = QUENCH_RATE * acid * base
        acid, base = (
            jnp.where(valid, acid + DIFFUSE_ACID * spread(acid) - quenched, 0.0),
            jnp.where(valid, base + DIFFUSE_BASE * spread(base) - quenched, 0.0),
        )
    for ref, value in ((intensity_ref, image), (acid_ref, acid), (base_ref, base)):
        ref[...] = lane_roll_left(value, RIM)[RIM : RIM + rows, :LANES]


def on_device(mask, kernels, socs_weights, quencher):
    ambit = kernels.shape[2]
    planes = kernels.shape[0] * kernels.shape[1]
    kern_count, tile_count = lax.axis_size("kern"), lax.axis_size("tile")
    rows = mask.shape[0]
    lead = ambit // 2 + RIM
    height = rows + 2 * RIM
    span = rows + 2 * lead

    send, window = pl.pallas_call(
        functools.partial(prepare_kernel, kern_count, tile_count, lead),
        out_shape=(
            jax.ShapeDtypeStruct((kern_count, tile_count, RIM, LANES), jnp.float32),
            jax.ShapeDtypeStruct((rows, 2 * LANES), jnp.float32),
        ),
        name="prepare",
    )(mask, quencher)
    received = lax.all_to_all(
        send.reshape(kern_count * tile_count, RIM, LANES), ("kern", "tile"), 0, 0, tiled=True
    ).reshape(send.shape)
    above = shifted(window, "tile", 1)
    below = shifted(window, "tile", -1)
    tap_groups = ambit // GROUP
    taps = kernels.reshape(planes, tap_groups, GROUP * ambit)[:, ::-1].transpose(1, 0, 2)
    taps = taps.reshape(tap_groups * planes, GROUP * ambit)
    block = jax.ShapeDtypeStruct((rows, LANES), jnp.float32)
    vmem = pl.BlockSpec(memory_space=pltpu.VMEM)
    return pl.pallas_call(
        functools.partial(resist_kernel, kern_count, tile_count, ambit),
        out_shape=(block, block, block),
        in_specs=[vmem] * 6 + [pl.BlockSpec(memory_space=pltpu.SMEM)],
        scratch_shapes=[
            pltpu.VMEM((span, 2 * LANES), jnp.float32),
            pltpu.VMEM((2, 8 * span, LANES), jnp.float32),
            pltpu.VMEM((span * ambit, LANES), jnp.bfloat16),
            pltpu.VMEM((span * ambit, LANES), jnp.bfloat16),
            pltpu.VMEM((height // GROUP * planes, 6 * LANES), jnp.float32),
            pltpu.VMEM((height, 2 * LANES), jnp.float32),
        ],
        compiler_params=pltpu.CompilerParams(vmem_limit_bytes=48 * 1024 * 1024),
        name="image_and_resist",
    )(window, above, below, received, quencher, taps, socs_weights)


def solution(mesh):
    placed = (P("tile", None), P(), P(), P("tile", "kern"))
    return jax.shard_map(
        on_device,
        mesh=mesh,
        in_specs=placed,
        out_specs=(P("tile", "kern"), P("tile", "kern"), P("tile", "kern")),
        check_vma=False,
    )
```

time: 322 us -> 29.3 us (0.09)
  the two profiles are of different devices: /device:TPU:4 before, /device:TPU:8 now
where the time goes in v1:
time: 29.3 us; the launch traced here: 28.9 us
  starting transfers between devices  11.9 us (41%)
  Pallas kernels  11.4 us (39%)
  local copies, waits for them, and re-layouts  2.59 us (9%)
  waiting for transfers between devices  2.26 us (8%)
  between operations  0.71 us (2%)
    pallas_call x1, Pallas kernels, on_device(): pl.pallas_call(functools.partial(resist_kernel, kern_count, tile_count, a...  9.69 us
    all_to_all x1, starting transfers between devices, on_device(): lax.all_to_all(send.reshape(kern_count * tile_count, RIM, LANES), ('kern'...  6.05 us
    ppermute x2, starting transfers between devices, shifted(): lax.ppermute(value, axis, [(source, source + steps) for source in range(l...  5.84 us
    ppermute x2, waiting for transfers between devices, shifted(): lax.ppermute(value, axis, [(source, source + steps) for source in range(l...  2.26 us
    reshape x2, local copies, waits for them, and re-layouts, on_device(): kernels.reshape(planes, tap_groups, GROUP * ambit)[:, ::-1]  1.9 us
    pallas_call x1, Pallas kernels, on_device(): pl.pallas_call(functools.partial(prepare_kernel, kern_count, tile_count,...  1.74 us
    unnamed x6, local copies, waits for them, and re-layouts  0.66 us
  transfers between devices with their start and end apart: 3, of which 1 were waited for; matrix products, arithmetic and copies ran while one was open for 7% of the time, Pallas kernels for 0%

profile of v1, /device:TPU:8, one launch (start us, length us, event | category | flops | bytes accessed | tf_op | source)
XLA Modules:
  0.0 28.9 jit_solution(17592837472275520602)
XLA Ops:
  0.6 1.7 %prepare.1 = (f32[4,8,8,128]{3,2,1,0:T(8,128)}, f32[32,256]{1,0:T(8,128)}) custom-call(s32[32,512]{1,0:T(8,128)} %mask_ref.1, f32[32,128]{1,0:T(8,128)} %quencher_ref.3), custom_call_target="tpu_custom_call" | custom-call | tf_op jit(solution)/shard_map/prepare/pallas_call | solution.py:244
  2.4 0.0 copy-start.1
  2.4 6.0 %all-to-all-start = ((f32[32,8,128]{2,1,0:T(8,128)}), f32[32,8,128]{2,1,0:T(8,128)S(1)}, u32[]{:S(2)}, u32[]{:S(2)}) async-start(f32[32,8,128]{2,1,0:T(8,128)} %bitcast.9), calls=%async_computation | async-start | bytes 262144 | tf_op jit(solution)/shard_map/all_to_all | solution.py:252
  8.4 0.0 copy-done.1
  8.4 3.4 %collective-permute-start.1 = (f32[32,256]{1,0:T(8,128)S(1)}, f32[32,256]{1,0:T(8,128)S(1)}, u32[]{:S(2)}, u32[]{:S(2)}) collective-permute-start(f32[32,256]{1,0:T(8,128)S(1)} %copy-done.1), channel_id=1, source_target_pairs={{1,0},{2,1},{3,2},{4,3},{5,4},{6,5},{7,6},{9,8},{10,9},{11,10},{12... | collective-permute-start | bytes 98312 | tf_op jit(solution)/shard_map/ppermute | solution.py:75
  11.8 2.5 %collective-permute-start = (f32[32,256]{1,0:T(8,128)S(1)}, f32[32,256]{1,0:T(8,128)S(1)}, u32[]{:S(2)}, u32[]{:S(2)}) collective-permute-start(f32[32,256]{1,0:T(8,128)S(1)} %copy-done.1), channel_id=1, source_target_pairs={{0,1},{1,2},{2,3},{3,4},{4,5},{5,6},{6,7},{8,9},{9,10},{10,11},{11... | collective-permute-start | bytes 98312 | tf_op jit(solution)/shard_map/ppermute | solution.py:75
  14.3 1.8 %reshape.20 = bf16[48,16,256]{2,1,0:T(8,128)(2,1)S(1)} reshape(bf16[24,2,64,64]{3,2,1,0:T(8,128)(2,1)} %param.5) | data formatting | bytes 786432 | tf_op jit(solution)/shard_map/reshape | solution.py:258
  16.1 0.1 copy.7
  16.2 0.0 copy-start
  16.3 0.0 collective-permute-done.1.below_ref
  16.3 2.3 %collective-permute-done.above_ref = f32[32,256]{1,0:T(8,128)S(1)} collective-permute-done((f32[32,256]{1,0:T(8,128)S(1)}, f32[32,256]{1,0:T(8,128)S(1)}, u32[]{:S(2)}, u32[]{:S(2)}) %collective-permute-start) | collective-permute-done | bytes 32800 | tf_op jit(solution)/shard_map/ppermute | solution.py:75
  18.5 0.0 all-to-all-done
  18.5 0.0 copy-start.2
  18.5 0.0 copy-done
  18.5 0.6 %copy-done.2 = f32[24]{0:T(128)S(1)} copy-done((f32[24]{0:T(128)S(1)}, f32[24]{0:T(128)}, u32[]{:S(2)}) %copy-start.2) | copy-done | bytes 120
  19.2 9.7 %image_and_resist.1 = (f32[32,128]{1,0:T(8,128)}, f32[32,128]{1,0:T(8,128)}, f32[32,128]{1,0:T(8,128)}) custom-call(f32[32,256]{1,0:T(8,128)S(1)} %copy-done.1, f32[32,256]{1,0:T(8,128)S(1)} %collective-permute-done.above_ref, f32[32,256]{1,0:T(8,128)S(1)} %collective-permute-done.1.below_ref, f32[4,8,8,128]{3,2,1,0:T(8,128)S(1)} %bitcast.8, ...), custom_call_target="tpu_custom_call" | custom-call | tf_op jit(solution)/shard_map/image_and_resist/pallas_call | solution.py:262
  (1 shorter events, 0.0 us)
Async XLA Ops:
  2.4 6.1 %copy-start.1 = (f32[32,256]{1,0:T(8,128)S(1)}, f32[32,256]{1,0:T(8,128)}, u32[]{:S(2)}) copy-start(f32[32,256]{1,0:T(8,128)} %get-tuple-element.5.own_ref) | copy-start | bytes 98308
  2.4 16.2 %all-to-all-start = ((f32[32,8,128]{2,1,0:T(8,128)}), f32[32,8,128]{2,1,0:T(8,128)S(1)}, u32[]{:S(2)}, u32[]{:S(2)}) async-start(f32[32,8,128]{2,1,0:T(8,128)} %bitcast.9), calls=%async_computation | async-start | bytes 262144 | tf_op jit(solution)/shard_map/all_to_all | solution.py:252
  8.4 7.8 %collective-permute-start.1 = (f32[32,256]{1,0:T(8,128)S(1)}, f32[32,256]{1,0:T(8,128)S(1)}, u32[]{:S(2)}, u32[]{:S(2)}) collective-permute-start(f32[32,256]{1,0:T(8,128)S(1)} %copy-done.1), channel_id=1, source_target_pairs={{1,0},{2,1},{3,2},{4,3},{5,4},{6,5},{7,6},{9,8},{10,9},{11,10},{12... | collective-permute-start | bytes 98312 | tf_op jit(solution)/shard_map/ppermute | solution.py:75
  11.8 6.7 %collective-permute-start = (f32[32,256]{1,0:T(8,128)S(1)}, f32[32,256]{1,0:T(8,128)S(1)}, u32[]{:S(2)}, u32[]{:S(2)}) collective-permute-start(f32[32,256]{1,0:T(8,128)S(1)} %copy-done.1), channel_id=1, source_target_pairs={{0,1},{1,2},{2,3},{3,4},{4,5},{5,6},{6,7},{8,9},{9,10},{10,11},{11... | collective-permute-start | bytes 98312 | tf_op jit(solution)/shard_map/ppermute | solution.py:75
  16.2 2.3 %copy-start = (f32[32,128]{1,0:T(8,128)S(1)}, f32[32,128]{1,0:T(8,128)}, u32[]{:S(2)}) copy-start(f32[32,128]{1,0:T(8,128)} %quencher_ref.3) | copy-start | bytes 49156
  18.5 0.7 %copy-start.2 = (f32[24]{0:T(128)S(1)}, f32[24]{0:T(128)}, u32[]{:S(2)}) copy-start(f32[24]{0:T(128)} %weights_ref.1) | copy-start | bytes 292

commit v2 on v1

v2 whole, which is shorter than its diff:
```python
import functools

import jax
import jax.numpy as jnp
from jax import lax
from jax.experimental import pallas as pl
from jax.experimental.pallas import tpu as pltpu
from jax.sharding import PartitionSpec as P

STEPS = 8
DIFFUSE_ACID = 0.2
DIFFUSE_BASE = 0.1
QUENCH_RATE = 0.5
EXPOSURE = 0.35

LANES = 128
RIM = 8
GROUP = 4
WORD = 16


def lane_roll_left(value, amount):
    width = value.shape[1]
    amount %= width
    return value if amount == 0 else pltpu.roll(value, width - amount, 1)


def three_blocks(ref, rows, kern, kern_count):
    blocks = []
    for step in (-1, 0, 1):
        place = jnp.clip(kern + step, 0, kern_count - 1)
        block = ref[rows, pl.ds(pl.multiple_of(place * LANES, LANES), LANES)].astype(jnp.float32)
        inside = jnp.logical_and(kern + step >= 0, kern + step < kern_count)
        blocks.append(jnp.where(inside, block, 0.0))
    return jnp.concatenate(blocks, axis=1)


def own_window(mask_ref, kern, kern_count, lead):
    blocks = three_blocks(mask_ref, slice(None), kern, kern_count)
    return lane_roll_left(blocks, LANES - lead)[:, : 2 * LANES]


def prepare_kernel(kern_count, tile_count, lead, mask_ref, quencher_ref, send_ref, window_ref):
    kern, tile = lax.axis_index("kern"), lax.axis_index("tile")
    rows = mask_ref.shape[0]
    window_ref[...] = own_window(mask_ref, kern, kern_count, lead)
    send_ref[...] = jnp.zeros_like(send_ref)
    own = pl.ds(pl.multiple_of(kern * LANES, LANES), LANES)
    for step, value in (
        (1, quencher_ref[rows - RIM :, :]),
        (-1, quencher_ref[:RIM, :]),
        (2, mask_ref[rows - RIM :, own].astype(jnp.float32)),
        (-2, mask_ref[:RIM, own].astype(jnp.float32)),
    ):
        target = tile + step

        @pl.when(jnp.logical_and(target >= 0, target < tile_count))
        def _(target=target, value=value):
            for column in range(kern_count):
                send_ref[column, target] = value

    lane = lax.broadcasted_iota(jnp.int32, (RIM, LANES), 1)
    for step, first in ((-1, 0), (1, LANES - RIM)):
        edge = jnp.zeros((RIM, LANES), jnp.float32)
        for part in range(rows // RIM):
            moved = lane_roll_left(quencher_ref[RIM * part : RIM * part + RIM, :], first - RIM * part)
            here = jnp.logical_and(lane >= RIM * part, lane < RIM * part + RIM)
            edge = jnp.where(here, moved, edge)
        target = kern + step

        @pl.when(jnp.logical_and(target >= 0, target < kern_count))
        def _(target=target, edge=edge):
            send_ref[target, tile] = edge


def swapped(value, axis, first):
    count = lax.axis_size(axis)
    pairs = [(low, low + 1) for low in range(first, count - 1, 2)]
    return lax.ppermute(value, axis, pairs + [(high, low) for low, high in pairs])


def mask_words(window):
    bits = window.astype(jnp.int32)
    row = lax.broadcasted_iota(jnp.int32, (WORD, bits.shape[1]), 0)
    count = bits.shape[0] // WORD
    low = [
        jnp.sum(bits[WORD * w : WORD * (w + 1)] << row, axis=0, keepdims=True) for w in range(count)
    ]
    return [low[w] + (((low[w + 1] & 0xFF) << WORD) if w + 1 < count else 0) for w in range(count)]


def lay_shifts(window, ambit, main_ref, strip_ref, main_rows, strip_rows):
    words = mask_words(window)
    slanted = jnp.concatenate([jnp.broadcast_to(word, (8, 2 * LANES)) for word in words], axis=0)
    sublane = lax.broadcasted_iota(jnp.int32, slanted.shape, 0)
    for bit in (1, 2, 4):
        slanted = jnp.where((sublane & bit) != 0, lane_roll_left(slanted, bit), slanted)
    low, high = slanted[:, :LANES], slanted[:, LANES:]
    lane = lax.broadcasted_iota(jnp.int32, low.shape, 1)
    mains, strips = [], []
    for offset in range(0, ambit, 8):
        mains.append(lane_roll_left(jnp.where(lane < offset, high, low), offset))
        strip = lane_roll_left(high, offset)
        for width in (16, 32, 64):
            strip = jnp.where(lane < width, strip, pltpu.roll(strip, width, 1))
        strips.append(strip >> (lane // 16))
    for shifts, ref, rows in ((mains, main_ref, main_rows), (strips, strip_ref, strip_rows)):
        for w in range(len(words)):
            for pair in range(ambit // 16):
                word = jnp.concatenate(
                    [shifts[2 * pair][8 * w : 8 * w + 8], shifts[2 * pair + 1][8 * w : 8 * w + 8]], axis=0
                )
                for bit in range(WORD):
                    row = WORD * w + bit
                    if row in rows:
                        plane = ((word >> bit) & 1).astype(jnp.float32).astype(jnp.bfloat16)
                        ref[ambit * row + 16 * pair : ambit * row + 16 * pair + 16, :] = plane


def add_main(total_ref, taps_ref, main_ref, s, first_row, groups, tap_groups, ambit):
    planes = taps_ref.shape[0] // tap_groups
    first, last = max(0, s - tap_groups + 1), min(groups - 1, s)
    taps = taps_ref[planes * (tap_groups - 1 - s + first) : planes * (tap_groups - s + last), :]
    depth = GROUP * ambit
    for half in range(2):
        at = ambit * (GROUP * s + 2 * half - first_row)
        shifts = jnp.concatenate([main_ref[at : at + depth], main_ref[at + ambit : at + ambit + depth]], axis=1)
        place = (slice(planes * first, planes * (last + 1)), slice(2 * LANES * half, 2 * LANES * (half + 1)))
        total_ref[place] += jnp.dot(taps, shifts, preferred_element_type=jnp.float32)


def add_strip(total_ref, taps_ref, strip_ref, s, first_row, groups, tap_groups, ambit):
    planes = taps_ref.shape[0] // tap_groups
    members = [g for g in range(groups // GROUP) if 0 <= s - GROUP * g < tap_groups]
    pieces = [tap_groups - 1 - s + GROUP * g for g in members]
    taps = jnp.concatenate([taps_ref[planes * p : planes * (p + 1), :] for p in pieces], axis=0)
    depth = GROUP * ambit
    at = ambit * (GROUP * s - first_row)
    shifts = jnp.concatenate(
        [strip_ref[at : at + depth], strip_ref[at + 8 * ambit : at + 8 * ambit + depth]], axis=1
    )
    total_ref[planes * members[0] : planes * (members[-1] + 1), :] += jnp.dot(
        taps, shifts, preferred_element_type=jnp.float32
    )


class Plan:
    def __init__(self, rows, ambit):
        self.rows, self.ambit = rows, ambit
        self.lead = ambit // 2 + RIM
        self.height, self.span = rows + 2 * RIM, rows + 2 * self.lead
        self.groups, self.tap_groups = self.height // GROUP, ambit // GROUP
        self.strip_groups = self.height // 16
        own = range(self.lead, self.lead + rows)
        self.main = {s: range(GROUP * s, GROUP * s + 7) for s in range(self.groups + self.tap_groups - 1)}
        self.strip = {
            s: range(GROUP * s, GROUP * s + 12) for s in range(GROUP * (self.strip_groups - 1) + self.tap_groups)
        }
        self.own_main = [s for s, used in self.main.items() if used[0] in own and used[-1] in own]
        self.own_strip = [s for s, used in self.strip.items() if used[0] in own and used[-1] + 7 in own]
        self.far_main = [s for s in self.main if s not in self.own_main]
        self.far_strip = [s for s in self.strip if s not in self.own_strip]


def own_rows_kernel(
    plan,
    kern_count,
    kernels_ref,
    weights_ref,
    mask_ref,
    taps_ref,
    main_total_ref,
    strip_total_ref,
    window_ref,
    weight_ref,
    wide_ref,
    main_ref,
    strip_ref,
):
    ambit, lead = plan.ambit, plan.lead
    planes = kernels_ref.shape[0] * kernels_ref.shape[1]
    wanted = (weight_ref.shape[0], weights_ref.shape[0])
    plane = lax.broadcasted_iota(jnp.int32, wanted, 0)
    member = lax.broadcasted_iota(jnp.int32, wanted, 1)
    spread = jnp.broadcast_to(weights_ref[...].reshape(1, wanted[1]), wanted)
    column = jnp.sum(jnp.where(plane // 2 == member, spread, 0.0), axis=1, keepdims=True)
    weight_ref[...] = jnp.broadcast_to(column, weight_ref.shape)
    kern = lax.axis_index("kern")
    window_ref[...] = own_window(mask_ref, kern, kern_count, lead)
    wide_ref[...] = kernels_ref[...].reshape(planes * ambit, ambit).astype(jnp.float32)
    for group in range(plan.tap_groups):
        pieces = [wide_ref[pl.ds(GROUP * group + part, planes, stride=ambit), :] for part in range(GROUP)]
        place = planes * (plan.tap_groups - 1 - group)
        taps_ref[place : place + planes, :] = jnp.concatenate(pieces, axis=1).astype(jnp.bfloat16)
    main_rows = {row - lead for s in plan.own_main for row in plan.main[s]}
    strip_rows = {row - lead for s in plan.own_strip for row in plan.strip[s]}
    lay_shifts(window_ref[...], ambit, main_ref, strip_ref, main_rows, strip_rows)
    main_total_ref[...] = jnp.zeros_like(main_total_ref)
    strip_total_ref[...] = jnp.zeros_like(strip_total_ref)
    for s in plan.own_main:
        add_main(main_total_ref, taps_ref, main_ref, s, lead, plan.groups, plan.tap_groups, ambit)
    for s in plan.own_strip:
        add_strip(strip_total_ref, taps_ref, strip_ref, s, lead, plan.groups, plan.tap_groups, ambit)


def resist_kernel(
    plan,
    kern_count,
    tile_count,
    own_ref,
    pair_ref,
    other_ref,
    received_ref,
    quencher_ref,
    taps_ref,
    own_main_ref,
    own_strip_ref,
    weight_ref,
    intensity_ref,
    acid_ref,
    base_ref,
    main_ref,
    strip_ref,
    main_total_ref,
    strip_total_ref,
    image_ref,
):
    kern, tile = lax.axis_index("kern"), lax.axis_index("tile")
    rows, ambit = plan.rows, plan.ambit
    planes = taps_ref.shape[0] // plan.tap_groups
    main_total_ref[...] = own_main_ref[...]
    strip_total_ref[...] = own_strip_ref[...]

    def far_rows(step):
        place = jnp.clip(tile + step, 0, tile_count - 1)
        inside_tile = jnp.logical_and(tile + step >= 0, tile + step < tile_count)
        blocks = []
        for side in (-1, 0, 1):
            column = jnp.clip(kern + side, 0, kern_count - 1)
            inside = jnp.logical_and(kern + side >= 0, kern + side < kern_count)
            block = received_ref[column, place]
            blocks.append(jnp.where(jnp.logical_and(inside, inside_tile), block, 0.0))
        return lane_roll_left(jnp.concatenate(blocks, axis=1), LANES - plan.lead)[:, : 2 * LANES]

    even = tile % 2 == 0
    pair, other = pair_ref[...], other_ref[...]
    above, below = jnp.where(even, other, pair), jnp.where(even, pair, other)
    window = jnp.concatenate([far_rows(-2), above, own_ref[...], below, far_rows(2)], axis=0)
    main_rows = {row for s in plan.far_main for row in plan.main[s]}
    strip_rows = {row for s in plan.far_strip for row in plan.strip[s]}
    lay_shifts(window, ambit, main_ref, strip_ref, main_rows, strip_rows)
    for s in plan.far_main:
        add_main(main_total_ref, taps_ref, main_ref, s, 0, plan.groups, plan.tap_groups, ambit)
    for s in plan.far_strip:
        add_strip(strip_total_ref, taps_ref, strip_ref, s, 0, plan.groups, plan.tap_groups, ambit)

    weight = weight_ref[:, :1]

    def weighted(total_ref, group):
        field = total_ref[planes * group : planes * (group + 1), :]
        return jnp.sum(weight * (field * field), axis=0, keepdims=True)

    for group in range(plan.groups):
        summed = weighted(main_total_ref, group)
        for part in range(GROUP):
            row = GROUP * group + part
            image_ref[row : row + 1, :LANES] = summed[:, LANES * part : LANES * (part + 1)]
    for group in range(plan.strip_groups):
        summed = weighted(strip_total_ref, group)
        for part in range(16):
            row = 16 * group + part
            half = summed[:, LANES * (part // 8) : LANES * (part // 8 + 1)]
            image_ref[row : row + 1, LANES:] = lane_roll_left(half, 16 * (part % 8))

    image = image_ref[...]
    row_id = lax.broadcasted_iota(jnp.int32, image.shape, 0)
    lane_id = lax.broadcasted_iota(jnp.int32, image.shape, 1)
    at_row = tile * rows + row_id - RIM
    at_column = kern * LANES + lane_id - RIM
    valid = (at_row >= 0) & (at_row < tile_count * rows) & (at_column >= 0) & (at_column < kern_count * LANES)
    valid = valid & (lane_id < LANES + 2 * RIM)

    def rim_rows(step):
        place = jnp.clip(tile + step, 0, tile_count - 1)
        return jnp.concatenate(
            [received_ref[jnp.clip(kern + side, 0, kern_count - 1), place] for side in (-1, 0, 1)], axis=1
        )

    before = received_ref[jnp.clip(kern - 1, 0, kern_count - 1), tile]
    after = received_ref[jnp.clip(kern + 1, 0, kern_count - 1), tile]
    middle = [
        jnp.concatenate(
            [
                lane_roll_left(before, RIM * part + RIM),
                quencher_ref[RIM * part : RIM * part + RIM, :],
                lane_roll_left(after, RIM * part),
            ],
            axis=1,
        )
        for part in range(rows // RIM)
    ]
    base = jnp.concatenate([rim_rows(-1)] + middle + [rim_rows(1)], axis=0)
    base = lane_roll_left(base, LANES - RIM)[:, : 2 * LANES]
    base = jnp.where(valid, base, 0.0)
    acid = jnp.where(valid, 1.0 - jnp.exp(-EXPOSURE * image), 0.0)

    def spread(value):
        return (
            pltpu.roll(value, 1, 0)
            + pltpu.roll(value, value.shape[0] - 1, 0)
            + pltpu.roll(value, 1, 1)
            + pltpu.roll(value, value.shape[1] - 1, 1)
            - 4.0 * value
        )

    for _ in range(STEPS):
        quenched = QUENCH_RATE * acid * base
        acid, base = (
            jnp.where(valid, acid + DIFFUSE_ACID * spread(acid) - quenched, 0.0),
            jnp.where(valid, base + DIFFUSE_BASE * spread(base) - quenched, 0.0),
        )
    for ref, value in ((intensity_ref, image), (acid_ref, acid), (base_ref, base)):
        ref[...] = lane_roll_left(value, RIM)[RIM : RIM + rows, :LANES]


def on_device(mask, kernels, socs_weights, quencher):
    ambit = kernels.shape[2]
    planes = kernels.shape[0] * kernels.shape[1]
    kern_count, tile_count = lax.axis_size("kern"), lax.axis_size("tile")
    rows = mask.shape[0]
    plan = Plan(rows, ambit)
    vmem = pl.BlockSpec(memory_space=pltpu.VMEM)
    limit = pltpu.CompilerParams(vmem_limit_bytes=24 * 1024 * 1024)

    send, window = pl.pallas_call(
        functools.partial(prepare_kernel, kern_count, tile_count, plan.lead),
        out_shape=(
            jax.ShapeDtypeStruct((kern_count, tile_count, RIM, LANES), jnp.float32),
            jax.ShapeDtypeStruct((rows, 2 * LANES), jnp.float32),
        ),
        cost_estimate=pl.CostEstimate(flops=10**9, bytes_accessed=10**7, transcendentals=0),
        name="prepare",
    )(mask, quencher)
    received = lax.all_to_all(
        send.reshape(kern_count * tile_count, RIM, LANES), ("kern", "tile"), 0, 0, tiled=True
    ).reshape(send.shape)
    pair = swapped(window, "tile", 0)
    other = swapped(window, "tile", 1)

    main_total = jax.ShapeDtypeStruct((plan.groups * planes, 4 * LANES), jnp.float32)
    strip_total = jax.ShapeDtypeStruct((plan.strip_groups * planes, 2 * LANES), jnp.float32)
    taps, own_main, own_strip, own_mask, weight = pl.pallas_call(
        functools.partial(own_rows_kernel, plan, kern_count),
        out_shape=(
            jax.ShapeDtypeStruct((plan.tap_groups * planes, GROUP * ambit), jnp.bfloat16),
            main_total,
            strip_total,
            jax.ShapeDtypeStruct(window.shape, jnp.float32),
            jax.ShapeDtypeStruct((planes, LANES), jnp.float32),
        ),
        in_specs=[vmem] * 3,
        out_specs=(vmem,) * 5,
        scratch_shapes=[
            pltpu.VMEM((planes * ambit, ambit), jnp.float32),
            pltpu.VMEM((rows * ambit, LANES), jnp.bfloat16),
            pltpu.VMEM((rows * ambit, LANES), jnp.bfloat16),
        ],
        compiler_params=limit,
        name="own_rows",
    )(kernels, socs_weights, mask)
    block = jax.ShapeDtypeStruct((rows, LANES), jnp.float32)
    return pl.pallas_call(
        functools.partial(resist_kernel, plan, kern_count, tile_count),
        out_shape=(block, block, block),
        in_specs=[vmem] * 9,
        scratch_shapes=[
            pltpu.VMEM((plan.span * ambit, LANES), jnp.bfloat16),
            pltpu.VMEM((plan.span * ambit, LANES), jnp.bfloat16),
            pltpu.VMEM(main_total.shape, jnp.float32),
            pltpu.VMEM(strip_total.shape, jnp.float32),
            pltpu.VMEM((plan.height, 2 * LANES), jnp.float32),
        ],
        compiler_params=limit,
        name="image_and_resist",
    )(own_mask, pair, other, received, quencher, taps, own_main, own_strip, weight)


def solution(mesh):
    placed = (P("tile", None), P(), P(), P("tile", "kern"))
    return jax.shard_map(
        on_device,
        mesh=mesh,
        in_specs=placed,
        out_specs=(P("tile", "kern"), P("tile", "kern"), P("tile", "kern")),
        check_vma=False,
    )
```

time: 29.3 us -> 22.5 us (0.77)
  the two profiles are of different devices: /device:TPU:8 before, /device:TPU:0 now
where the time goes in v2:
time: 22.5 us; the launch traced here: 22.3 us
  starting transfers between devices  12.5 us (56%)
  Pallas kernels  8.92 us (40%)
  between operations  0.7 us (3%)
    all_to_all x1, starting transfers between devices, on_device(): lax.all_to_all(send.reshape(kern_count * tile_count, RIM, LANES), ('kern'...  7.3 us
    ppermute x2, starting transfers between devices, swapped(): lax.ppermute(value, axis, pairs + [(high, low) for low, high in pairs])  5.21 us
    pallas_call x1, Pallas kernels, on_device(): pl.pallas_call(functools.partial(resist_kernel, plan, kern_count, tile_co...  4.74 us
    pallas_call x1, Pallas kernels, on_device(): pl.pallas_call(functools.partial(own_rows_kernel, plan, kern_count), out_...  2.36 us
    pallas_call x1, Pallas kernels, on_device(): pl.pallas_call(functools.partial(prepare_kernel, kern_count, tile_count,...  1.82 us
  transfers between devices with their start and end apart: 3, of which 1 were waited for; matrix products, arithmetic and copies ran while one was open for 0% of the time, Pallas kernels for 11%

profile of v2, /device:TPU:0, one launch (start us, length us, event | category | flops | bytes accessed | tf_op | source)
XLA Modules:
  0.0 22.3 jit_solution(17038600042426171598)
XLA Ops:
  0.6 0.0 copy-start.2
  0.6 0.0 copy-start.1
  0.7 0.0 copy-start.3
  0.7 0.0 copy-start
  0.7 1.8 %prepare.1 = (f32[4,8,8,128]{3,2,1,0:T(8,128)}, f32[32,256]{1,0:T(8,128)}) custom-call(s32[32,512]{1,0:T(8,128)} %mask_ref.3, f32[32,128]{1,0:T(8,128)} %quencher_ref.3), custom_call_target="tpu_custom_call" | custom-call | flops 1000000000 | bytes 10000000 | tf_op jit(solution)/shard_map/prepare/pallas_call | solution.py:335
  2.5 7.3 %all-to-all-start = ((f32[32,8,128]{2,1,0:T(8,128)}), f32[32,8,128]{2,1,0:T(8,128)S(1)}, u32[]{:S(2)}, u32[]{:S(2)}) async-start(f32[32,8,128]{2,1,0:T(8,128)} %bitcast.3), calls=%async_computation | async-start | bytes 262144 | tf_op jit(solution)/shard_map/all_to_all | solution.py:344
  9.8 0.7 %collective-permute-start.1 = (f32[32,256]{1,0:T(8,128)}, f32[32,256]{1,0:T(8,128)S(1)}, u32[]{:S(2)}, u32[]{:S(2)}) collective-permute-start(f32[32,256]{1,0:T(8,128)} %get-tuple-element.11), channel_id=1, source_target_pairs={{1,2},{3,4},{5,6},{2,1},{4,3},{6,5},{9,10},{11,12},{13,14},{10,9},... | collective-permute-start | bytes 98312 | tf_op jit(solution)/shard_map/ppermute | solution.py:79
  10.5 4.5 %collective-permute-start = (f32[32,256]{1,0:T(8,128)}, f32[32,256]{1,0:T(8,128)S(1)}, u32[]{:S(2)}, u32[]{:S(2)}) collective-permute-start(f32[32,256]{1,0:T(8,128)} %get-tuple-element.11), channel_id=1, source_target_pairs={{0,1},{2,3},{4,5},{6,7},{1,0},{3,2},{5,4},{7,6},{8,9},{10,11},{12,... | collective-permute-start | bytes 98312 | tf_op jit(solution)/shard_map/ppermute | solution.py:79
  15.0 0.0 copy-done.1
  15.0 0.0 copy-done.3
  15.0 0.0 copy-done
  15.0 2.4 %own_rows.1 = (bf16[768,256]{1,0:T(8,128)(2,1)S(1)}, f32[576,512]{1,0:T(8,128)S(1)}, f32[144,256]{1,0:T(8,128)S(1)}, f32[32,256]{1,0:T(8,128)S(1)}, f32[48,128]{1,0:T(8,128)S(1)}) custom-call(bf16[24,2,64,64]{3,2,1,0:T(8,128)(2,1)S(1)} %copy-done, f32[24]{0:T(128)S(1)} %copy-done.3, s32[32,512]{1,0:T(8,128)S(1)} %copy-done.1), custom_call_target="tpu_custom_call" | custom-call | tf_op jit(solution)/shard_map/own_rows/pallas_call | solution.py:352
  17.4 0.0 collective-permute-done.1.other_ref
  17.4 0.0 collective-permute-done.pair_ref
  17.4 0.1 all-to-all-done
  17.5 0.0 copy-done.2
  17.5 4.7 %image_and_resist.1 = (f32[32,128]{1,0:T(8,128)}, f32[32,128]{1,0:T(8,128)}, f32[32,128]{1,0:T(8,128)}) custom-call(f32[32,256]{1,0:T(8,128)S(1)} %get-tuple-element.10.own_ref, f32[32,256]{1,0:T(8,128)S(1)} %collective-permute-done.pair_ref, f32[32,256]{1,0:T(8,128)S(1)} %collective-permute-done.1.other_ref, f32[4,8,8,128]{3,2,1,0:T(8,128)S(1)} %bitcast.2, ...), custom_call_target="tpu_custom_call" | custom-call | tf_op jit(solution)/shard_map/image_and_resist/pallas_call | solution.py:372
Async XLA Ops:
  0.6 16.9 %copy-start.2 = (f32[32,128]{1,0:T(8,128)S(1)}, f32[32,128]{1,0:T(8,128)}, u32[]{:S(2)}) copy-start(f32[32,128]{1,0:T(8,128)} %quencher_ref.3) | copy-start | bytes 49156
  0.6 14.4 %copy-start.1 = (s32[32,512]{1,0:T(8,128)S(1)}, s32[32,512]{1,0:T(8,128)}, u32[]{:S(2)}) copy-start(s32[32,512]{1,0:T(8,128)} %mask_ref.3) | copy-start | bytes 196612
  0.7 14.4 %copy-start.3 = (f32[24]{0:T(128)S(1)}, f32[24]{0:T(128)}, u32[]{:S(2)}) copy-start(f32[24]{0:T(128)} %weights_ref.1) | copy-start | bytes 292
  0.7 14.4 %copy-start = (bf16[24,2,64,64]{3,2,1,0:T(8,128)(2,1)S(1)}, bf16[24,2,64,64]{3,2,1,0:T(8,128)(2,1)}, u32[]{:S(2)}) copy-start(bf16[24,2,64,64]{3,2,1,0:T(8,128)(2,1)} %kernels_ref.1) | copy-start | bytes 1179652
  2.5 15.0 %all-to-all-start = ((f32[32,8,128]{2,1,0:T(8,128)}), f32[32,8,128]{2,1,0:T(8,128)S(1)}, u32[]{:S(2)}, u32[]{:S(2)}) async-start(f32[32,8,128]{2,1,0:T(8,128)} %bitcast.3), calls=%async_computation | async-start | bytes 262144 | tf_op jit(solution)/shard_map/all_to_all | solution.py:344
  9.8 7.6 %collective-permute-start.1 = (f32[32,256]{1,0:T(8,128)}, f32[32,256]{1,0:T(8,128)S(1)}, u32[]{:S(2)}, u32[]{:S(2)}) collective-permute-start(f32[32,256]{1,0:T(8,128)} %get-tuple-element.11), channel_id=1, source_target_pairs={{1,2},{3,4},{5,6},{2,1},{4,3},{6,5},{9,10},{11,12},{13,14},{10,9},... | collective-permute-start | bytes 98312 | tf_op jit(solution)/shard_map/ppermute | solution.py:79
  10.5 6.9 %collective-permute-start = (f32[32,256]{1,0:T(8,128)}, f32[32,256]{1,0:T(8,128)S(1)}, u32[]{:S(2)}, u32[]{:S(2)}) collective-permute-start(f32[32,256]{1,0:T(8,128)} %get-tuple-element.11), channel_id=1, source_target_pairs={{0,1},{2,3},{4,5},{6,7},{1,0},{3,2},{5,4},{7,6},{8,9},{10,11},{12,... | collective-permute-start | bytes 98312 | tf_op jit(solution)/shard_map/ppermute | solution.py:79

commit v3 on v2

--- a/solution.py
+++ b/solution.py
@@ -1,3 +1,4 @@
+import copy
 import functools
 
 import jax
@@ -89,58 +90,79 @@
     return [low[w] + (((low[w + 1] & 0xFF) << WORD) if w + 1 < count else 0) for w in range(count)]
 
 
-def lay_shifts(window, ambit, main_ref, strip_ref, main_rows, strip_rows):
-    words = mask_words(window)
-    slanted = jnp.concatenate([jnp.broadcast_to(word, (8, 2 * LANES)) for word in words], axis=0)
-    sublane = lax.broadcasted_iota(jnp.int32, slanted.shape, 0)
-    for bit in (1, 2, 4):
-        slanted = jnp.where((sublane & bit) != 0, lane_roll_left(slanted, bit), slanted)
-    low, high = slanted[:, :LANES], slanted[:, LANES:]
-    lane = lax.broadcasted_iota(jnp.int32, low.shape, 1)
-    mains, strips = [], []
-    for offset in range(0, ambit, 8):
-        mains.append(lane_roll_left(jnp.where(lane < offset, high, low), offset))
-        strip = lane_roll_left(high, offset)
-        for width in (16, 32, 64):
-            strip = jnp.where(lane < width, strip, pltpu.roll(strip, width, 1))
-        strips.append(strip >> (lane // 16))
-    for shifts, ref, rows in ((mains, main_ref, main_rows), (strips, strip_ref, strip_rows)):
-        for w in range(len(words)):
-            for pair in range(ambit // 16):
-                word = jnp.concatenate(
-                    [shifts[2 * pair][8 * w : 8 * w + 8], shifts[2 * pair + 1][8 * w : 8 * w + 8]], axis=0
+class Shifts:
+    def __init__(self, window, ambit, first_row, main_ref, strip_ref):
+        words = mask_words(window)
+        slanted = jnp.concatenate([jnp.broadcast_to(word, (8, 2 * LANES)) for word in words], axis=0)
+        sublane = lax.broadcasted_iota(jnp.int32, slanted.shape, 0)
+        for bit in (1, 2, 4):
+            slanted = jnp.where((sublane & bit) != 0, lane_roll_left(slanted, bit), slanted)
+        low, high = slanted[:, :LANES], slanted[:, LANES:]
+        lane = lax.broadcasted_iota(jnp.int32, low.shape, 1)
+        mains, strips = [], []
+        for offset in range(0, ambit, 8):
+            mains.append(lane_roll_left(jnp.where(lane < offset, high, low), offset))
+            strip = lane_roll_left(high, offset)
+            for width in (16, 32, 64):
+                strip = jnp.where(lane < width, strip, pltpu.roll(strip, width, 1))
+            strips.append(strip >> (lane // 16))
+        self.ambit, self.first_row = ambit, first_row
+        self.sources = {"main": mains, "strip": strips}
+        self.refs = {"main": main_ref, "strip": strip_ref}
+        self.laid = {"main": set(), "strip": set()}
+
+    def view(self, first_row):
+        view = copy.copy(self)
+        view.first_row, view.laid = first_row, {"main": set(), "strip": set()}
+        return view
+
+    def lay(self, kind, rows):
+        for row in rows:
+            row -= self.first_row
+            if row in self.laid[kind]:
+                continue
+            self.laid[kind].add(row)
+            word, bit = divmod(row, WORD)
+            source = self.sources[kind]
+            for pair in range(self.ambit // 16):
+                value = jnp.concatenate(
+                    [source[2 * pair + part][8 * word : 8 * word + 8] for part in range(2)], axis=0
                 )
-                for bit in range(WORD):
-                    row = WORD * w + bit
-                    if row in rows:
-                        plane = ((word >> bit) & 1).astype(jnp.float32).astype(jnp.bfloat16)
-                        ref[ambit * row + 16 * pair : ambit * row + 16 * pair + 16, :] = plane
-
-
-def add_main(total_ref, taps_ref, main_ref, s, first_row, groups, tap_groups, ambit):
+                plane = ((value >> bit) & 1).astype(jnp.float32).astype(jnp.bfloat16)
+                at = self.ambit * row + 16 * pair
+                self.refs[kind][at : at + 16, :] = plane
+
+
+def add_main(plan, total_ref, taps_ref, shifts, s):
+    groups, tap_groups, ambit = plan.groups, plan.tap_groups, plan.ambit
     planes = taps_ref.shape[0] // tap_groups
+    shifts.lay("main", plan.main[s])
+    main_ref = shifts.refs["main"]
     first, last = max(0, s - tap_groups + 1), min(groups - 1, s)
     taps = taps_ref[planes * (tap_groups - 1 - s + first) : planes * (tap_groups - s + last), :]
     depth = GROUP * ambit
     for half in range(2):
-        at = ambit * (GROUP * s + 2 * half - first_row)
-        shifts = jnp.concatenate([main_ref[at : at + depth], main_ref[at + ambit : at + ambit + depth]], axis=1)
+        at = ambit * (GROUP * s + 2 * half - shifts.first_row)
+        moved = jnp.concatenate([main_ref[at : at + depth], main_ref[at + ambit : at + ambit + depth]], axis=1)
         place = (slice(planes * first, planes * (last + 1)), slice(2 * LANES * half, 2 * LANES * (half + 1)))
-        total_ref[place] += jnp.dot(taps, shifts, preferred_element_type=jnp.float32)
-
-
-def add_strip(total_ref, taps_ref, strip_ref, s, first_row, groups, tap_groups, ambit):
+        total_ref[place] += jnp.dot(taps, moved, preferred_element_type=jnp.float32)
+
+
+def add_strip(plan, total_ref, taps_ref, shifts, s):
+    groups, tap_groups, ambit = plan.groups, plan.tap_groups, plan.ambit
     planes = taps_ref.shape[0] // tap_groups
+    shifts.lay("strip", plan.strip[s])
+    strip_ref = shifts.refs["strip"]
     members = [g for g in range(groups // GROUP) if 0 <= s - GROUP * g < tap_groups]
     pieces = [tap_groups - 1 - s + GROUP * g for g in members]
     taps = jnp.concatenate([taps_ref[planes * p : planes * (p + 1), :] for p in pieces], axis=0)
     depth = GROUP * ambit
-    at = ambit * (GROUP * s - first_row)
-    shifts = jnp.concatenate(
+    at = ambit * (GROUP * s - shifts.first_row)
+    moved = jnp.concatenate(
         [strip_ref[at : at + depth], strip_ref[at + 8 * ambit : at + 8 * ambit + depth]], axis=1
     )
     total_ref[planes * members[0] : planes * (members[-1] + 1), :] += jnp.dot(
-        taps, shifts, preferred_element_type=jnp.float32
+        taps, moved, preferred_element_type=jnp.float32
     )
 
 
@@ -151,15 +173,36 @@
         self.height, self.span = rows + 2 * RIM, rows + 2 * self.lead
         self.groups, self.tap_groups = self.height // GROUP, ambit // GROUP
         self.strip_groups = self.height // 16
-        own = range(self.lead, self.lead + rows)
-        self.main = {s: range(GROUP * s, GROUP * s + 7) for s in range(self.groups + self.tap_groups - 1)}
-        self.strip = {
+        main = {s: range(GROUP * s, GROUP * s + 7) for s in range(self.groups + self.tap_groups - 1)}
+        strip = {
             s: range(GROUP * s, GROUP * s + 12) for s in range(GROUP * (self.strip_groups - 1) + self.tap_groups)
         }
-        self.own_main = [s for s, used in self.main.items() if used[0] in own and used[-1] in own]
-        self.own_strip = [s for s, used in self.strip.items() if used[0] in own and used[-1] + 7 in own]
-        self.far_main = [s for s in self.main if s not in self.own_main]
-        self.far_strip = [s for s in self.strip if s not in self.own_strip]
+        self.main, self.strip = main, strip
+        first, middle, last = RIM, self.lead, self.lead + rows
+        self.parts = {}
+        taken = {"main": set(), "strip": set()}
+        for name, low, high in (
+            ("own", middle, last),
+            ("upper", first, last),
+            ("lower", middle, last + rows),
+            ("top", 0, last),
+            ("bottom", middle, self.span),
+        ):
+            self.parts[name] = {}
+            for kind, steps, reach in (("main", main, 0), ("strip", strip, 7)):
+                chosen = [
+                    s for s, used in steps.items()
+                    if s not in taken[kind] and low <= used[0] and used[-1] + reach < high
+                ]
+                taken[kind].update(chosen)
+                self.parts[name][kind] = chosen
+        assert taken == {"main": set(main), "strip": set(strip)}
+
+    def add(self, name, main_total_ref, strip_total_ref, taps_ref, shifts):
+        for s in self.parts[name]["main"]:
+            add_main(self, main_total_ref, taps_ref, shifts, s)
+        for s in self.parts[name]["strip"]:
+            add_strip(self, strip_total_ref, taps_ref, shifts, s)
 
 
 def own_rows_kernel(
@@ -192,15 +235,56 @@
         pieces = [wide_ref[pl.ds(GROUP * group + part, planes, stride=ambit), :] for part in range(GROUP)]
         place = planes * (plan.tap_groups - 1 - group)
         taps_ref[place : place + planes, :] = jnp.concatenate(pieces, axis=1).astype(jnp.bfloat16)
-    main_rows = {row - lead for s in plan.own_main for row in plan.main[s]}
-    strip_rows = {row - lead for s in plan.own_strip for row in plan.strip[s]}
-    lay_shifts(window_ref[...], ambit, main_ref, strip_ref, main_rows, strip_rows)
+    shifts = Shifts(window_ref[...], ambit, lead, main_ref, strip_ref)
     main_total_ref[...] = jnp.zeros_like(main_total_ref)
     strip_total_ref[...] = jnp.zeros_like(strip_total_ref)
-    for s in plan.own_main:
-        add_main(main_total_ref, taps_ref, main_ref, s, lead, plan.groups, plan.tap_groups, ambit)
-    for s in plan.own_strip:
-        add_strip(strip_total_ref, taps_ref, strip_ref, s, lead, plan.groups, plan.tap_groups, ambit)
+    plan.add("own", main_total_ref, strip_total_ref, taps_ref, shifts)
+
+
+def weighted_rows(weight, total_ref, group):
+    planes = weight.shape[0]
+    field = total_ref[planes * group : planes * (group + 1), :]
+    return jnp.sum(weight * (field * field), axis=0, keepdims=True)
+
+
+def write_main_rows(image_ref, weight, total_ref, groups):
+    for group in groups:
+        summed = weighted_rows(weight, total_ref, group)
+        for part in range(GROUP):
+            row = GROUP * group + part
+            image_ref[row : row + 1, :LANES] = summed[:, LANES * part : LANES * (part + 1)]
+
+
+def add_side(plan, below, main_total_ref, strip_total_ref, taps_ref, shifts, first_row):
+    @pl.when(below)
+    def _():
+        plan.add("lower", main_total_ref, strip_total_ref, taps_ref, shifts.view(first_row["lower"]))
+
+    @pl.when(jnp.logical_not(below))
+    def _():
+        plan.add("upper", main_total_ref, strip_total_ref, taps_ref, shifts.view(first_row["upper"]))
+
+
+def pair_rows_kernel(
+    plan,
+    own_ref,
+    pair_ref,
+    taps_ref,
+    main_in_ref,
+    strip_in_ref,
+    main_total_ref,
+    strip_total_ref,
+    main_ref,
+    strip_ref,
+):
+    even = lax.axis_index("tile") % 2 == 0
+    main_total_ref[...] = main_in_ref[...]
+    strip_total_ref[...] = strip_in_ref[...]
+    own, pair = own_ref[...], pair_ref[...]
+    window = jnp.concatenate([jnp.where(even, own, pair), jnp.where(even, pair, own)], axis=0)
+    shifts = Shifts(window, plan.ambit, 0, main_ref, strip_ref)
+    first_row = {"upper": RIM, "lower": plan.lead}
+    add_side(plan, even, main_total_ref, strip_total_ref, taps_ref, shifts, first_row)
 
 
 def resist_kernel(
@@ -208,13 +292,13 @@
     kern_count,
     tile_count,
     own_ref,
+    other_ref,
     pair_ref,
-    other_ref,
     received_ref,
     quencher_ref,
     taps_ref,
-    own_main_ref,
-    own_strip_ref,
+    main_in_ref,
+    strip_in_ref,
     weight_ref,
     intensity_ref,
     acid_ref,
@@ -228,8 +312,8 @@
     kern, tile = lax.axis_index("kern"), lax.axis_index("tile")
     rows, ambit = plan.rows, plan.ambit
     planes = taps_ref.shape[0] // plan.tap_groups
-    main_total_ref[...] = own_main_ref[...]
-    strip_total_ref[...] = own_strip_ref[...]
+    main_total_ref[...] = main_in_ref[...]
+    strip_total_ref[...] = strip_in_ref[...]
 
     def far_rows(step):
         place = jnp.clip(tile + step, 0, tile_count - 1)
@@ -246,27 +330,17 @@
     pair, other = pair_ref[...], other_ref[...]
     above, below = jnp.where(even, other, pair), jnp.where(even, pair, other)
     window = jnp.concatenate([far_rows(-2), above, own_ref[...], below, far_rows(2)], axis=0)
-    main_rows = {row for s in plan.far_main for row in plan.main[s]}
-    strip_rows = {row for s in plan.far_strip for row in plan.strip[s]}
-    lay_shifts(window, ambit, main_ref, strip_ref, main_rows, strip_rows)
-    for s in plan.far_main:
-        add_main(main_total_ref, taps_ref, main_ref, s, 0, plan.groups, plan.tap_groups, ambit)
-    for s in plan.far_strip:
-        add_strip(strip_total_ref, taps_ref, strip_ref, s, 0, plan.groups, plan.tap_groups, ambit)
+    shifts = Shifts(window, ambit, 0, main_ref, strip_ref)
+    first_row = {"upper": 0, "lower": 0}
+    add_side(plan, jnp.logical_not(even), main_total_ref, strip_total_ref, taps_ref, shifts, first_row)
+    shifts = shifts.view(0)
+    plan.add("top", main_total_ref, strip_total_ref, taps_ref, shifts)
+    plan.add("bottom", main_total_ref, strip_total_ref, taps_ref, shifts)
 
     weight = weight_ref[:, :1]
-
-    def weighted(total_ref, group):
-        field = total_ref[planes * group : planes * (group + 1), :]
-        return jnp.sum(weight * (field * field), axis=0, keepdims=True)
-
-    for group in range(plan.groups):
-        summed = weighted(main_total_ref, group)
-        for part in range(GROUP):
-            row = GROUP * group + part
-            image_ref[row : row + 1, :LANES] = summed[:, LANES * part : LANES * (part + 1)]
+    write_main_rows(image_ref, weight, main_total_ref, range(plan.groups))
     for group in range(plan.strip_groups):
-        summed = weighted(strip_total_ref, group)
+        summed = weighted_rows(weight, strip_total_ref, group)
         for part in range(16):
             row = 16 * group + part
             half = summed[:, LANES * (part // 8) : LANES * (part // 8 + 1)]
@@ -368,21 +442,29 @@
         compiler_params=limit,
         name="own_rows",
     )(kernels, socs_weights, mask)
+    totals = pl.pallas_call(
+        functools.partial(pair_rows_kernel, plan),
+        out_shape=(main_total, strip_total),
+        in_specs=[vmem] * 5,
+        out_specs=(vmem,) * 2,
+        scratch_shapes=[pltpu.VMEM((2 * rows * ambit, LANES), jnp.bfloat16)] * 2,
+        compiler_params=limit,
+        name="pair_rows",
+    )(own_mask, pair, taps, own_main, own_strip)
     block = jax.ShapeDtypeStruct((rows, LANES), jnp.float32)
     return pl.pallas_call(
         functools.partial(resist_kernel, plan, kern_count, tile_count),
         out_shape=(block, block, block),
         in_specs=[vmem] * 9,
-        scratch_shapes=[
-            pltpu.VMEM((plan.span * ambit, LANES), jnp.bfloat16),
-            pltpu.VMEM((plan.span * ambit, LANES), jnp.bfloat16),
+        scratch_shapes=[pltpu.VMEM((plan.span * ambit, LANES), jnp.bfloat16)] * 2
+        + [
             pltpu.VMEM(main_total.shape, jnp.float32),
             pltpu.VMEM(strip_total.shape, jnp.float32),
             pltpu.VMEM((plan.height, 2 * LANES), jnp.float32),
         ],
         compiler_params=limit,
         name="image_and_resist",
-    )(own_mask, pair, other, received, quencher, taps, own_main, own_strip, weight)
+    )(own_mask, other, pair, received, quencher, taps, *totals, weight)
 
 
 def solution(mesh):

time: 22.5 us -> 21.7 us (0.964)
  the two profiles are of different devices: /device:TPU:0 before, /device:TPU:4 now
where the time goes in v3:
time: 21.7 us; the launch traced here: 21.5 us
  starting transfers between devices  11 us (51%)
  Pallas kernels  9.7 us (45%)
  between operations  0.75 us (3%)
    all_to_all x1, starting transfers between devices, on_device(): lax.all_to_all(send.reshape(kern_count * tile_count, RIM, LANES), ('kern'...  6.1 us
    ppermute x2, starting transfers between devices, swapped(): lax.ppermute(value, axis, pairs + [(high, low) for low, high in pairs])  4.89 us
    pallas_call x1, Pallas kernels, on_device(): pl.pallas_call(functools.partial(resist_kernel, plan, kern_count, tile_co...  3.85 us
    pallas_call x1, Pallas kernels, on_device(): pl.pallas_call(functools.partial(own_rows_kernel, plan, kern_count), out_...  2.37 us
    pallas_call x1, Pallas kernels, on_device(): pl.pallas_call(functools.partial(prepare_kernel, kern_count, tile_count,...  1.82 us
    pallas_call x1, Pallas kernels, on_device(): pl.pallas_call(functools.partial(pair_rows_kernel, plan), out_shape=(main...  1.66 us
  transfers between devices with their start and end apart: 3, of which 0 were waited for; matrix products, arithmetic and copies ran while one was open for 0% of the time, Pallas kernels for 19%

profile of v3, /device:TPU:4, one launch (start us, length us, event | category | flops | bytes accessed | tf_op | source)
XLA Modules:
  0.0 21.5 jit_solution(17787393068621688606)
XLA Ops:
  0.6 0.0 copy-start.1
  0.6 0.0 copy-start.3
  0.7 0.0 copy-start
  0.7 1.8 %prepare.1 = (f32[4,8,8,128]{3,2,1,0:T(8,128)}, f32[32,256]{1,0:T(8,128)}) custom-call(s32[32,512]{1,0:T(8,128)} %mask_ref.3, f32[32,128]{1,0:T(8,128)} %quencher_ref.3), custom_call_target="tpu_custom_call" | custom-call | flops 1000000000 | bytes 10000000 | tf_op jit(solution)/shard_map/prepare/pallas_call | solution.py:409
  2.5 6.1 %all-to-all-start = ((f32[32,8,128]{2,1,0:T(8,128)}), f32[32,8,128]{2,1,0:T(8,128)S(1)}, u32[]{:S(2)}, u32[]{:S(2)}) async-start(f32[32,8,128]{2,1,0:T(8,128)} %bitcast.3), calls=%async_computation | async-start | bytes 262144 | tf_op jit(solution)/shard_map/all_to_all | solution.py:418
  8.6 0.0 copy-start.2
  8.6 0.3 %collective-permute-start.1 = (f32[32,256]{1,0:T(8,128)}, f32[32,256]{1,0:T(8,128)S(1)}, u32[]{:S(2)}, u32[]{:S(2)}) collective-permute-start(f32[32,256]{1,0:T(8,128)} %get-tuple-element.13), channel_id=1, source_target_pairs={{0,1},{2,3},{4,5},{6,7},{1,0},{3,2},{5,4},{7,6},{8,9},{10,11},{12,... | collective-permute-start | bytes 98312 | tf_op jit(solution)/shard_map/ppermute | solution.py:80
  8.9 4.6 %collective-permute-start = (f32[32,256]{1,0:T(8,128)}, f32[32,256]{1,0:T(8,128)S(1)}, u32[]{:S(2)}, u32[]{:S(2)}) collective-permute-start(f32[32,256]{1,0:T(8,128)} %get-tuple-element.13), channel_id=1, source_target_pairs={{1,2},{3,4},{5,6},{2,1},{4,3},{6,5},{9,10},{11,12},{13,14},{10,9},... | collective-permute-start | bytes 98312 | tf_op jit(solution)/shard_map/ppermute | solution.py:80
  13.5 0.0 copy-done.1
  13.5 0.0 copy-done.3
  13.5 0.0 copy-done
  13.5 2.4 %own_rows.1 = (bf16[768,256]{1,0:T(8,128)(2,1)S(1)}, f32[576,512]{1,0:T(8,128)S(1)}, f32[144,256]{1,0:T(8,128)S(1)}, f32[32,256]{1,0:T(8,128)S(1)}, f32[48,128]{1,0:T(8,128)S(1)}) custom-call(bf16[24,2,64,64]{3,2,1,0:T(8,128)(2,1)S(1)} %copy-done, f32[24]{0:T(128)S(1)} %copy-done.3, s32[32,512]{1,0:T(8,128)S(1)} %copy-done.1), custom_call_target="tpu_custom_call" | custom-call | tf_op jit(solution)/shard_map/own_rows/pallas_call | solution.py:426
  15.9 0.0 collective-permute-done.1.pair_ref
  15.9 1.7 %pair_rows.1 = (f32[576,512]{1,0:T(8,128)S(1)}, f32[144,256]{1,0:T(8,128)S(1)}) custom-call(f32[32,256]{1,0:T(8,128)S(1)} %get-tuple-element.12.own_ref, f32[32,256]{1,0:T(8,128)S(1)} %collective-permute-done.1.pair_ref, bf16[768,256]{1,0:T(8,128)(2,1)S(1)} %get-tuple-element.15.taps_ref, f32[576,512]{1,0:T(8,128)S(1)} %get-tuple-element.16.main_in_ref, ...), custom_call_target="tpu_custom_call" | custom-call | tf_op jit(solution)/shard_map/pair_rows/pallas_call | solution.py:445
  17.6 0.0 collective-permute-done.other_ref
  17.6 0.0 all-to-all-done
  17.6 0.0 copy-done.2
  17.6 3.9 %image_and_resist.1 = (f32[32,128]{1,0:T(8,128)}, f32[32,128]{1,0:T(8,128)}, f32[32,128]{1,0:T(8,128)}) custom-call(f32[32,256]{1,0:T(8,128)S(1)} %get-tuple-element.12.own_ref, f32[32,256]{1,0:T(8,128)S(1)} %collective-permute-done.other_ref, f32[32,256]{1,0:T(8,128)S(1)} %collective-permute-done.1.pair_ref, f32[4,8,8,128]{3,2,1,0:T(8,128)S(1)} %bitcast.2, ...), custom_call_target="tpu_custom_call" | custom-call | tf_op jit(solution)/shard_map/image_and_resist/pallas_call | solution.py:455
Async XLA Ops:
  0.6 12.9 %copy-start.1 = (s32[32,512]{1,0:T(8,128)S(1)}, s32[32,512]{1,0:T(8,128)}, u32[]{:S(2)}) copy-start(s32[32,512]{1,0:T(8,128)} %mask_ref.3) | copy-start | bytes 196612
  0.6 12.9 %copy-start.3 = (f32[24]{0:T(128)S(1)}, f32[24]{0:T(128)}, u32[]{:S(2)}) copy-start(f32[24]{0:T(128)} %weights_ref.1) | copy-start | bytes 292
  0.7 12.9 %copy-start = (bf16[24,2,64,64]{3,2,1,0:T(8,128)(2,1)S(1)}, bf16[24,2,64,64]{3,2,1,0:T(8,128)(2,1)}, u32[]{:S(2)}) copy-start(bf16[24,2,64,64]{3,2,1,0:T(8,128)(2,1)} %kernels_ref.1) | copy-start | bytes 1179652
  2.5 15.1 %all-to-all-start = ((f32[32,8,128]{2,1,0:T(8,128)}), f32[32,8,128]{2,1,0:T(8,128)S(1)}, u32[]{:S(2)}, u32[]{:S(2)}) async-start(f32[32,8,128]{2,1,0:T(8,128)} %bitcast.3), calls=%async_computation | async-start | bytes 262144 | tf_op jit(solution)/shard_map/all_to_all | solution.py:418
  8.6 9.0 %copy-start.2 = (f32[32,128]{1,0:T(8,128)S(1)}, f32[32,128]{1,0:T(8,128)}, u32[]{:S(2)}) copy-start(f32[32,128]{1,0:T(8,128)} %quencher_ref.3) | copy-start | bytes 49156
  8.6 7.3 %collective-permute-start.1 = (f32[32,256]{1,0:T(8,128)}, f32[32,256]{1,0:T(8,128)S(1)}, u32[]{:S(2)}, u32[]{:S(2)}) collective-permute-start(f32[32,256]{1,0:T(8,128)} %get-tuple-element.13), channel_id=1, source_target_pairs={{0,1},{2,3},{4,5},{6,7},{1,0},{3,2},{5,4},{7,6},{8,9},{10,11},{12,... | collective-permute-start | bytes 98312 | tf_op jit(solution)/shard_map/ppermute | solution.py:80
  8.9 8.7 %collective-permute-start = (f32[32,256]{1,0:T(8,128)}, f32[32,256]{1,0:T(8,128)S(1)}, u32[]{:S(2)}, u32[]{:S(2)}) collective-permute-start(f32[32,256]{1,0:T(8,128)} %get-tuple-element.13), channel_id=1, source_target_pairs={{1,2},{3,4},{5,6},{2,1},{4,3},{6,5},{9,10},{11,12},{13,14},{10,9},... | collective-permute-start | bytes 98312 | tf_op jit(solution)/shard_map/ppermute | solution.py:80

commit v4 on v3

--- a/solution.py
+++ b/solution.py
@@ -93,10 +93,11 @@
 class Shifts:
     def __init__(self, window, ambit, first_row, main_ref, strip_ref):
         words = mask_words(window)
-        slanted = jnp.concatenate([jnp.broadcast_to(word, (8, 2 * LANES)) for word in words], axis=0)
-        sublane = lax.broadcasted_iota(jnp.int32, slanted.shape, 0)
-        for bit in (1, 2, 4):
-            slanted = jnp.where((sublane & bit) != 0, lane_roll_left(slanted, bit), slanted)
+        slanted = [
+            pltpu.roll(jnp.broadcast_to(word, (8, 2 * LANES)), 2 * LANES - 7, 1, stride=1, stride_axis=0)
+            for word in words
+        ]
+        slanted = jnp.concatenate(slanted, axis=0)
         low, high = slanted[:, :LANES], slanted[:, LANES:]
         lane = lax.broadcasted_iota(jnp.int32, low.shape, 1)
         mains, strips = [], []
@@ -133,9 +134,43 @@
                 self.refs[kind][at : at + 16, :] = plane
 
 
-def add_main(plan, total_ref, taps_ref, shifts, s):
+class Total:
+    def __init__(self, ref, source, planes):
+        self.ref, self.source, self.planes = ref, source, planes
+        self.waiting = {
+            (group, half)
+            for group in range(ref.shape[0] // planes)
+            for half in range(ref.shape[1] // (2 * LANES))
+        }
+
+    def add(self, first, last, half, value):
+        lanes = slice(2 * LANES * half, 2 * LANES * (half + 1))
+        group = first
+        while group <= last:
+            fresh, end = (group, half) in self.waiting, group
+            while end <= last and ((end, half) in self.waiting) == fresh:
+                self.waiting.discard((end, half))
+                end += 1
+            place = (slice(self.planes * group, self.planes * end), lanes)
+            piece = value[self.planes * (group - first) : self.planes * (end - first)]
+            if not fresh:
+                piece = self.ref[place] + piece
+            elif self.source is not None:
+                piece = self.source[place] + piece
+            self.ref[place] = piece
+            group = end
+
+    def finish(self):
+        for group, half in sorted(self.waiting):
+            lanes = slice(2 * LANES * half, 2 * LANES * (half + 1))
+            place = (slice(self.planes * group, self.planes * (group + 1)), lanes)
+            self.ref[place] = jnp.zeros_like(self.ref[place]) if self.source is None else self.source[place]
+        self.waiting = set()
+
+
+def add_main(plan, total, taps_ref, shifts, s):
     groups, tap_groups, ambit = plan.groups, plan.tap_groups, plan.ambit
-    planes = taps_ref.shape[0] // tap_groups
+    planes = total.planes
     shifts.lay("main", plan.main[s])
     main_ref = shifts.refs["main"]
     first, last = max(0, s - tap_groups + 1), min(groups - 1, s)
@@ -144,13 +179,12 @@
     for half in range(2):
         at = ambit * (GROUP * s + 2 * half - shifts.first_row)
         moved = jnp.concatenate([main_ref[at : at + depth], main_ref[at + ambit : at + ambit + depth]], axis=1)
-        place = (slice(planes * first, planes * (last + 1)), slice(2 * LANES * half, 2 * LANES * (half + 1)))
-        total_ref[place] += jnp.dot(taps, moved, preferred_element_type=jnp.float32)
-
-
-def add_strip(plan, total_ref, taps_ref, shifts, s):
+        total.add(first, last, half, jnp.dot(taps, moved, preferred_element_type=jnp.float32))
+
+
+def add_strip(plan, total, taps_ref, shifts, s):
     groups, tap_groups, ambit = plan.groups, plan.tap_groups, plan.ambit
-    planes = taps_ref.shape[0] // tap_groups
+    planes = total.planes
     shifts.lay("strip", plan.strip[s])
     strip_ref = shifts.refs["strip"]
     members = [g for g in range(groups // GROUP) if 0 <= s - GROUP * g < tap_groups]
@@ -161,9 +195,7 @@
     moved = jnp.concatenate(
         [strip_ref[at : at + depth], strip_ref[at + 8 * ambit : at + 8 * ambit + depth]], axis=1
     )
-    total_ref[planes * members[0] : planes * (members[-1] + 1), :] += jnp.dot(
-        taps, moved, preferred_element_type=jnp.float32
-    )
+    total.add(members[0], members[-1], 0, jnp.dot(taps, moved, preferred_element_type=jnp.float32))
 
 
 class Plan:
@@ -198,29 +230,29 @@
                 self.parts[name][kind] = chosen
         assert taken == {"main": set(main), "strip": set(strip)}
 
-    def add(self, name, main_total_ref, strip_total_ref, taps_ref, shifts):
+    def add(self, name, totals, taps_ref, shifts):
         for s in self.parts[name]["main"]:
-            add_main(self, main_total_ref, taps_ref, shifts, s)
+            add_main(self, totals[0], taps_ref, shifts, s)
         for s in self.parts[name]["strip"]:
-            add_strip(self, strip_total_ref, taps_ref, shifts, s)
-
-
-def own_rows_kernel(
+            add_strip(self, totals[1], taps_ref, shifts, s)
+
+
+def near_rows_kernel(
     plan,
     kern_count,
     kernels_ref,
     weights_ref,
     mask_ref,
+    pair_ref,
     taps_ref,
     main_total_ref,
     strip_total_ref,
-    window_ref,
     weight_ref,
-    wide_ref,
+    own_ref,
     main_ref,
     strip_ref,
 ):
-    ambit, lead = plan.ambit, plan.lead
+    ambit = plan.ambit
     planes = kernels_ref.shape[0] * kernels_ref.shape[1]
     wanted = (weight_ref.shape[0], weights_ref.shape[0])
     plane = lax.broadcasted_iota(jnp.int32, wanted, 0)
@@ -228,17 +260,24 @@
     spread = jnp.broadcast_to(weights_ref[...].reshape(1, wanted[1]), wanted)
     column = jnp.sum(jnp.where(plane // 2 == member, spread, 0.0), axis=1, keepdims=True)
     weight_ref[...] = jnp.broadcast_to(column, weight_ref.shape)
-    kern = lax.axis_index("kern")
-    window_ref[...] = own_window(mask_ref, kern, kern_count, lead)
-    wide_ref[...] = kernels_ref[...].reshape(planes * ambit, ambit).astype(jnp.float32)
+    depth = GROUP * ambit
+    tap = lax.broadcasted_iota(jnp.int32, (depth, depth), 0)
+    lane = lax.broadcasted_iota(jnp.int32, (depth, depth), 1)
+    turned = jnp.where(tap == (lane ^ 7), 1.0, 0.0).astype(jnp.bfloat16)
+    by_row = jnp.transpose(kernels_ref[...].reshape(planes, ambit, ambit), (1, 0, 2))
     for group in range(plan.tap_groups):
-        pieces = [wide_ref[pl.ds(GROUP * group + part, planes, stride=ambit), :] for part in range(GROUP)]
+        pieces = [by_row[GROUP * group + part] for part in range(GROUP)]
         place = planes * (plan.tap_groups - 1 - group)
-        taps_ref[place : place + planes, :] = jnp.concatenate(pieces, axis=1).astype(jnp.bfloat16)
-    shifts = Shifts(window_ref[...], ambit, lead, main_ref, strip_ref)
-    main_total_ref[...] = jnp.zeros_like(main_total_ref)
-    strip_total_ref[...] = jnp.zeros_like(strip_total_ref)
-    plan.add("own", main_total_ref, strip_total_ref, taps_ref, shifts)
+        taps = jnp.concatenate(pieces, axis=1)
+        taps = jnp.dot(taps, turned, preferred_element_type=jnp.float32)
+        taps_ref[place : place + planes, :] = taps.astype(jnp.bfloat16)
+    even = lax.axis_index("tile") % 2 == 0
+    own, pair = own_window(mask_ref, lax.axis_index("kern"), kern_count, plan.lead), pair_ref[...]
+    own_ref[...] = own
+    window = jnp.concatenate([jnp.where(even, own, pair), jnp.where(even, pair, own)], axis=0)
+    shifts = Shifts(window, ambit, 0, main_ref, strip_ref)
+    first_row = {"upper": RIM, "lower": plan.lead}
+    add_side(plan, even, (main_total_ref, strip_total_ref), (None, None), taps_ref, shifts, first_row, before=("own",))
 
 
 def weighted_rows(weight, total_ref, group):
@@ -255,36 +294,21 @@
             image_ref[row : row + 1, :LANES] = summed[:, LANES * part : LANES * (part + 1)]
 
 
-def add_side(plan, below, main_total_ref, strip_total_ref, taps_ref, shifts, first_row):
-    @pl.when(below)
-    def _():
-        plan.add("lower", main_total_ref, strip_total_ref, taps_ref, shifts.view(first_row["lower"]))
-
-    @pl.when(jnp.logical_not(below))
-    def _():
-        plan.add("upper", main_total_ref, strip_total_ref, taps_ref, shifts.view(first_row["upper"]))
-
-
-def pair_rows_kernel(
-    plan,
-    own_ref,
-    pair_ref,
-    taps_ref,
-    main_in_ref,
-    strip_in_ref,
-    main_total_ref,
-    strip_total_ref,
-    main_ref,
-    strip_ref,
-):
-    even = lax.axis_index("tile") % 2 == 0
-    main_total_ref[...] = main_in_ref[...]
-    strip_total_ref[...] = strip_in_ref[...]
-    own, pair = own_ref[...], pair_ref[...]
-    window = jnp.concatenate([jnp.where(even, own, pair), jnp.where(even, pair, own)], axis=0)
-    shifts = Shifts(window, plan.ambit, 0, main_ref, strip_ref)
-    first_row = {"upper": RIM, "lower": plan.lead}
-    add_side(plan, even, main_total_ref, strip_total_ref, taps_ref, shifts, first_row)
+def add_side(plan, below, refs, sources, taps_ref, shifts, first_row, before=(), after=(), then=None):
+    planes = taps_ref.shape[0] // plan.tap_groups
+
+    def add(name):
+        totals = [Total(ref, source, planes) for ref, source in zip(refs, sources)]
+        view = shifts.view(first_row[name])
+        for part in (*before, name, *after):
+            plan.add(part, totals, taps_ref, view)
+        for total in totals:
+            total.finish()
+        if then is not None:
+            then()
+
+    pl.when(below)(lambda: add("lower"))
+    pl.when(jnp.logical_not(below))(lambda: add("upper"))
 
 
 def resist_kernel(
@@ -308,12 +332,12 @@
     main_total_ref,
     strip_total_ref,
     image_ref,
+    result_ref,
+    result_sem,
 ):
     kern, tile = lax.axis_index("kern"), lax.axis_index("tile")
     rows, ambit = plan.rows, plan.ambit
     planes = taps_ref.shape[0] // plan.tap_groups
-    main_total_ref[...] = main_in_ref[...]
-    strip_total_ref[...] = strip_in_ref[...]
 
     def far_rows(step):
         place = jnp.clip(tile + step, 0, tile_count - 1)
@@ -332,19 +356,22 @@
     window = jnp.concatenate([far_rows(-2), above, own_ref[...], below, far_rows(2)], axis=0)
     shifts = Shifts(window, ambit, 0, main_ref, strip_ref)
     first_row = {"upper": 0, "lower": 0}
-    add_side(plan, jnp.logical_not(even), main_total_ref, strip_total_ref, taps_ref, shifts, first_row)
-    shifts = shifts.view(0)
-    plan.add("top", main_total_ref, strip_total_ref, taps_ref, shifts)
-    plan.add("bottom", main_total_ref, strip_total_ref, taps_ref, shifts)
-
+    refs, sources = (main_total_ref, strip_total_ref), (main_in_ref, strip_in_ref)
     weight = weight_ref[:, :1]
-    write_main_rows(image_ref, weight, main_total_ref, range(plan.groups))
-    for group in range(plan.strip_groups):
-        summed = weighted_rows(weight, strip_total_ref, group)
-        for part in range(16):
-            row = 16 * group + part
-            half = summed[:, LANES * (part // 8) : LANES * (part // 8 + 1)]
-            image_ref[row : row + 1, LANES:] = lane_roll_left(half, 16 * (part % 8))
+
+    def write_image():
+        write_main_rows(image_ref, weight, main_total_ref, range(plan.groups))
+        for group in range(plan.strip_groups):
+            summed = weighted_rows(weight, strip_total_ref, group)
+            for part in range(16):
+                row = 16 * group + part
+                half = summed[:, LANES * (part // 8) : LANES * (part // 8 + 1)]
+                image_ref[row : row + 1, LANES:] = lane_roll_left(half, 16 * (part % 8))
+
+    below_is_new = jnp.logical_not(even)
+    add_side(
+        plan, below_is_new, refs, sources, taps_ref, shifts, first_row, after=("top", "bottom"), then=write_image
+    )
 
     image = image_ref[...]
     row_id = lax.broadcasted_iota(jnp.int32, image.shape, 0)
@@ -387,14 +414,24 @@
             - 4.0 * value
         )
 
+    sent = []
+
+    def send_out(place, value, ref):
+        result_ref[place] = lane_roll_left(value, RIM)[RIM : RIM + rows, :LANES]
+        sent.append(pltpu.make_async_copy(result_ref.at[place], ref, result_sem.at[place]))
+        sent[-1].start()
+
+    send_out(0, image, intensity_ref)
     for _ in range(STEPS):
         quenched = QUENCH_RATE * acid * base
         acid, base = (
             jnp.where(valid, acid + DIFFUSE_ACID * spread(acid) - quenched, 0.0),
             jnp.where(valid, base + DIFFUSE_BASE * spread(base) - quenched, 0.0),
         )
-    for ref, value in ((intensity_ref, image), (acid_ref, acid), (base_ref, base)):
-        ref[...] = lane_roll_left(value, RIM)[RIM : RIM + rows, :LANES]
+    send_out(1, acid, acid_ref)
+    send_out(2, base, base_ref)
+    for copy_out in sent:
+        copy_out.wait()
 
 
 def on_device(mask, kernels, socs_weights, quencher):
@@ -423,48 +460,38 @@
 
     main_total = jax.ShapeDtypeStruct((plan.groups * planes, 4 * LANES), jnp.float32)
     strip_total = jax.ShapeDtypeStruct((plan.strip_groups * planes, 2 * LANES), jnp.float32)
-    taps, own_main, own_strip, own_mask, weight = pl.pallas_call(
-        functools.partial(own_rows_kernel, plan, kern_count),
+    taps, *totals, weight, own = pl.pallas_call(
+        functools.partial(near_rows_kernel, plan, kern_count),
         out_shape=(
             jax.ShapeDtypeStruct((plan.tap_groups * planes, GROUP * ambit), jnp.bfloat16),
             main_total,
             strip_total,
+            jax.ShapeDtypeStruct((planes, LANES), jnp.float32),
             jax.ShapeDtypeStruct(window.shape, jnp.float32),
-            jax.ShapeDtypeStruct((planes, LANES), jnp.float32),
         ),
-        in_specs=[vmem] * 3,
+        in_specs=[vmem] * 4,
         out_specs=(vmem,) * 5,
-        scratch_shapes=[
-            pltpu.VMEM((planes * ambit, ambit), jnp.float32),
-            pltpu.VMEM((rows * ambit, LANES), jnp.bfloat16),
-            pltpu.VMEM((rows * ambit, LANES), jnp.bfloat16),
-        ],
-        compiler_params=limit,
-        name="own_rows",
-    )(kernels, socs_weights, mask)
-    totals = pl.pallas_call(
-        functools.partial(pair_rows_kernel, plan),
-        out_shape=(main_total, strip_total),
-        in_specs=[vmem] * 5,
-        out_specs=(vmem,) * 2,
         scratch_shapes=[pltpu.VMEM((2 * rows * ambit, LANES), jnp.bfloat16)] * 2,
         compiler_params=limit,
-        name="pair_rows",
-    )(own_mask, pair, taps, own_main, own_strip)
+        name="near_rows",
+    )(kernels, socs_weights, mask, pair)
     block = jax.ShapeDtypeStruct((rows, LANES), jnp.float32)
     return pl.pallas_call(
         functools.partial(resist_kernel, plan, kern_count, tile_count),
         out_shape=(block, block, block),
         in_specs=[vmem] * 9,
+        out_specs=(pl.BlockSpec(memory_space=pl.ANY),) * 3,
         scratch_shapes=[pltpu.VMEM((plan.span * ambit, LANES), jnp.bfloat16)] * 2
         + [
             pltpu.VMEM(main_total.shape, jnp.float32),
             pltpu.VMEM(strip_total.shape, jnp.float32),
             pltpu.VMEM((plan.height, 2 * LANES), jnp.float32),
+            pltpu.VMEM((3, rows, LANES), jnp.float32),
+            pltpu.SemaphoreType.DMA((3,)),
         ],
         compiler_params=limit,
         name="image_and_resist",
-    )(own_mask, other, pair, received, quencher, taps, *totals, weight)
+    )(own, other, pair, received, quencher, taps, *totals, weight)
 
 
 def solution(mesh):

time: 21.7 us -> 21.3 us (0.982)
  the two profiles are of different devices: /device:TPU:4 before, /device:TPU:0 now
where the time goes in v4:
time: 21.3 us; the launch traced here: 21.1 us
  starting transfers between devices  9.78 us (46%)
  Pallas kernels  8.43 us (40%)
  waiting for transfers between devices  2.16 us (10%)
  between operations  0.7 us (3%)
    all_to_all x1, starting transfers between devices, on_device(): lax.all_to_all(send.reshape(kern_count * tile_count, RIM, LANES), ('kern'...  7.3 us
    pallas_call x1, Pallas kernels, on_device(): pl.pallas_call(functools.partial(resist_kernel, plan, kern_count, tile_co...  3.54 us
    pallas_call x1, Pallas kernels, on_device(): pl.pallas_call(functools.partial(near_rows_kernel, plan, kern_count), out...  3.06 us
    ppermute x2, starting transfers between devices, swapped(): lax.ppermute(value, axis, pairs + [(high, low) for low, high in pairs])  2.48 us
    pallas_call x1, Pallas kernels, on_device(): pl.pallas_call(functools.partial(prepare_kernel, kern_count, tile_count,...  1.82 us
    ppermute x2, waiting for transfers between devices, swapped(): lax.ppermute(value, axis, pairs + [(high, low) for low, high in pairs])  1.8 us
  transfers between devices with their start and end apart: 3, of which 2 were waited for; matrix products, arithmetic and copies ran while one was open for 0% of the time, Pallas kernels for 15%

profile of v4, /device:TPU:0, one launch (start us, length us, event | category | flops | bytes accessed | tf_op | source)
XLA Modules:
  0.0 21.1 jit_solution(3506293713292424346)
XLA Ops:
  0.6 0.0 copy-start.2
  0.6 0.0 copy-start.1
  0.7 0.0 copy-start.3
  0.7 0.0 copy-start
  0.7 1.8 %prepare.1 = (f32[4,8,8,128]{3,2,1,0:T(8,128)}, f32[32,256]{1,0:T(8,128)}) custom-call(s32[32,512]{1,0:T(8,128)} %mask_ref.3, f32[32,128]{1,0:T(8,128)} %quencher_ref.3), custom_call_target="tpu_custom_call" | custom-call | flops 1000000000 | bytes 10000000 | tf_op jit(solution)/shard_map/prepare/pallas_call | solution.py:446
  2.5 7.3 %all-to-all-start = ((f32[32,8,128]{2,1,0:T(8,128)}), f32[32,8,128]{2,1,0:T(8,128)S(1)}, u32[]{:S(2)}, u32[]{:S(2)}) async-start(f32[32,8,128]{2,1,0:T(8,128)} %bitcast.3), calls=%async_computation | async-start | bytes 262144 | tf_op jit(solution)/shard_map/all_to_all | solution.py:455
  9.8 1.8 %collective-permute-start = (f32[32,256]{1,0:T(8,128)}, f32[32,256]{1,0:T(8,128)S(1)}, u32[]{:S(2)}, u32[]{:S(2)}) collective-permute-start(f32[32,256]{1,0:T(8,128)} %get-tuple-element.10), channel_id=1, source_target_pairs={{0,1},{2,3},{4,5},{6,7},{1,0},{3,2},{5,4},{7,6},{8,9},{10,11},{12,... | collective-permute-start | bytes 98312 | tf_op jit(solution)/shard_map/ppermute | solution.py:80
  11.6 0.7 %collective-permute-start.1 = (f32[32,256]{1,0:T(8,128)}, f32[32,256]{1,0:T(8,128)S(1)}, u32[]{:S(2)}, u32[]{:S(2)}) collective-permute-start(f32[32,256]{1,0:T(8,128)} %get-tuple-element.10), channel_id=1, source_target_pairs={{1,2},{3,4},{5,6},{2,1},{4,3},{6,5},{9,10},{11,12},{13,14},{10,9},... | collective-permute-start | bytes 98312 | tf_op jit(solution)/shard_map/ppermute | solution.py:80
  12.3 1.8 %collective-permute-done.pair_ref = f32[32,256]{1,0:T(8,128)S(1)} collective-permute-done((f32[32,256]{1,0:T(8,128)}, f32[32,256]{1,0:T(8,128)S(1)}, u32[]{:S(2)}, u32[]{:S(2)}) %collective-permute-start) | collective-permute-done | bytes 32800 | tf_op jit(solution)/shard_map/ppermute | solution.py:80
  14.1 0.0 copy-done.1
  14.1 0.0 copy-done.3
  14.1 0.0 copy-done
  14.1 3.1 %near_rows.1 = (bf16[768,256]{1,0:T(8,128)(2,1)S(1)}, f32[576,512]{1,0:T(8,128)S(1)}, f32[144,256]{1,0:T(8,128)S(1)}, f32[48,128]{1,0:T(8,128)S(1)}, f32[32,256]{1,0:T(8,128)S(1)}) custom-call(bf16[24,2,64,64]{3,2,1,0:T(8,128)(2,1)S(1)} %copy-done, f32[24]{0:T(128)S(1)} %copy-done.3, s32[32,512]{1,0:T(8,128)S(1)} %copy-done.1, ...), custom_call_target="tpu_custom_call" | custom-call | tf_op jit(solution)/shard_map/near_rows/pallas_call | solution.py:463
  17.2 0.0 collective-permute-done.1.other_ref
  17.2 0.4 %all-to-all-done = f32[32,8,128]{2,1,0:T(8,128)S(1)} async-done(((f32[32,8,128]{2,1,0:T(8,128)}), f32[32,8,128]{2,1,0:T(8,128)S(1)}, u32[]{:S(2)}, u32[]{:S(2)}) %all-to-all-start) | async-done | bytes 131104 | tf_op jit(solution)/shard_map/all_to_all | solution.py:455
  17.5 0.0 copy-done.2
  17.5 3.5 %image_and_resist.1 = (f32[32,128]{1,0:T(8,128)}, f32[32,128]{1,0:T(8,128)}, f32[32,128]{1,0:T(8,128)}) custom-call(f32[32,256]{1,0:T(8,128)S(1)} %get-tuple-element.11.own_ref, f32[32,256]{1,0:T(8,128)S(1)} %collective-permute-done.1.other_ref, f32[32,256]{1,0:T(8,128)S(1)} %collective-permute-done.pair_ref, f32[4,8,8,128]{3,2,1,0:T(8,128)S(1)} %bitcast.2, ...), custom_call_target="tpu_custom_call" | custom-call | tf_op jit(solution)/shard_map/image_and_resist/pallas_call | solution.py:479
Async XLA Ops:
  0.6 16.9 %copy-start.2 = (f32[32,128]{1,0:T(8,128)S(1)}, f32[32,128]{1,0:T(8,128)}, u32[]{:S(2)}) copy-start(f32[32,128]{1,0:T(8,128)} %quencher_ref.3) | copy-start | bytes 49156
  0.6 13.4 %copy-start.1 = (s32[32,512]{1,0:T(8,128)S(1)}, s32[32,512]{1,0:T(8,128)}, u32[]{:S(2)}) copy-start(s32[32,512]{1,0:T(8,128)} %mask_ref.3) | copy-start | bytes 196612
  0.7 13.4 %copy-start.3 = (f32[24]{0:T(128)S(1)}, f32[24]{0:T(128)}, u32[]{:S(2)}) copy-start(f32[24]{0:T(128)} %weights_ref.1) | copy-start | bytes 292
  0.7 13.4 %copy-start = (bf16[24,2,64,64]{3,2,1,0:T(8,128)(2,1)S(1)}, bf16[24,2,64,64]{3,2,1,0:T(8,128)(2,1)}, u32[]{:S(2)}) copy-start(bf16[24,2,64,64]{3,2,1,0:T(8,128)(2,1)} %kernels_ref.1) | copy-start | bytes 1179652
  2.5 15.0 %all-to-all-start = ((f32[32,8,128]{2,1,0:T(8,128)}), f32[32,8,128]{2,1,0:T(8,128)S(1)}, u32[]{:S(2)}, u32[]{:S(2)}) async-start(f32[32,8,128]{2,1,0:T(8,128)} %bitcast.3), calls=%async_computation | async-start | bytes 262144 | tf_op jit(solution)/shard_map/all_to_all | solution.py:455
  9.8 4.3 %collective-permute-start = (f32[32,256]{1,0:T(8,128)}, f32[32,256]{1,0:T(8,128)S(1)}, u32[]{:S(2)}, u32[]{:S(2)}) collective-permute-start(f32[32,256]{1,0:T(8,128)} %get-tuple-element.10), channel_id=1, source_target_pairs={{0,1},{2,3},{4,5},{6,7},{1,0},{3,2},{5,4},{7,6},{8,9},{10,11},{12,... | collective-permute-start | bytes 98312 | tf_op jit(solution)/shard_map/ppermute | solution.py:80
  11.6 5.5 %collective-permute-start.1 = (f32[32,256]{1,0:T(8,128)}, f32[32,256]{1,0:T(8,128)S(1)}, u32[]{:S(2)}, u32[]{:S(2)}) collective-permute-start(f32[32,256]{1,0:T(8,128)} %get-tuple-element.10), channel_id=1, source_target_pairs={{1,2},{3,4},{5,6},{2,1},{4,3},{6,5},{9,10},{11,12},{13,14},{10,9},... | collective-permute-start | bytes 98312 | tf_op jit(solution)/shard_map/ppermute | solution.py:80

commit v5 on v4

--- a/solution.py
+++ b/solution.py
@@ -41,42 +41,36 @@
     return lane_roll_left(blocks, LANES - lead)[:, : 2 * LANES]
 
 
-def prepare_kernel(kern_count, tile_count, lead, mask_ref, quencher_ref, send_ref, window_ref):
-    kern, tile = lax.axis_index("kern"), lax.axis_index("tile")
+def turn_kernel(turned_ref):
+    row = lax.broadcasted_iota(jnp.int32, turned_ref.shape, 0)
+    lane = lax.broadcasted_iota(jnp.int32, turned_ref.shape, 1)
+    turned_ref[...] = jnp.where(row == (lane ^ 7), 1.0, 0.0).astype(jnp.bfloat16)
+
+
+def rim_kernel(
+    kern_count, lead, _, mask_ref, quencher_ref, beside_ref, across_ref, wide_ref, for_pair_ref, for_other_ref
+):
     rows = mask_ref.shape[0]
-    window_ref[...] = own_window(mask_ref, kern, kern_count, lead)
-    send_ref[...] = jnp.zeros_like(send_ref)
-    own = pl.ds(pl.multiple_of(kern * LANES, LANES), LANES)
-    for step, value in (
-        (1, quencher_ref[rows - RIM :, :]),
-        (-1, quencher_ref[:RIM, :]),
-        (2, mask_ref[rows - RIM :, own].astype(jnp.float32)),
-        (-2, mask_ref[:RIM, own].astype(jnp.float32)),
-    ):
-        target = tile + step
-
-        @pl.when(jnp.logical_and(target >= 0, target < tile_count))
-        def _(target=target, value=value):
-            for column in range(kern_count):
-                send_ref[column, target] = value
-
-    lane = lax.broadcasted_iota(jnp.int32, (RIM, LANES), 1)
-    for step, first in ((-1, 0), (1, LANES - RIM)):
-        edge = jnp.zeros((RIM, LANES), jnp.float32)
-        for part in range(rows // RIM):
-            moved = lane_roll_left(quencher_ref[RIM * part : RIM * part + RIM, :], first - RIM * part)
-            here = jnp.logical_and(lane >= RIM * part, lane < RIM * part + RIM)
-            edge = jnp.where(here, moved, edge)
-        target = kern + step
-
-        @pl.when(jnp.logical_and(target >= 0, target < kern_count))
-        def _(target=target, edge=edge):
-            send_ref[target, tile] = edge
-
-
-def swapped(value, axis, first):
+    kern = lax.axis_index("kern")
+    odd = kern % 2 == 1
+    window = own_window(mask_ref, kern, kern_count, lead)
+    beside, across = beside_ref[...], across_ref[...]
+    before, after = jnp.where(odd, beside, across), jnp.where(odd, across, beside)
+    wide = jnp.concatenate([before, quencher_ref[...], after], axis=1)
+    wide = lane_roll_left(wide, LANES - RIM)[:, : 2 * LANES]
+    wide_ref[...] = wide
+    first, last = wide[:RIM], wide[rows - RIM :]
+    even = lax.axis_index("tile") % 2 == 0
+    for ref, rim in ((for_pair_ref, jnp.where(even, last, first)), (for_other_ref, jnp.where(even, first, last))):
+        ref[:rows, :] = window
+        ref[rows:, :] = rim
+
+
+def swapped(value, axis, first, step=1):
     count = lax.axis_size(axis)
-    pairs = [(low, low + 1) for low in range(first, count - 1, 2)]
+    pairs = [
+        (low, low + step) for low in range(count - step) if low // step >= first and (low // step - first) % 2 == 0
+    ]
     return lax.ppermute(value, axis, pairs + [(high, low) for low, high in pairs])
 
 
@@ -239,16 +233,15 @@
 
 def near_rows_kernel(
     plan,
-    kern_count,
     kernels_ref,
     weights_ref,
-    mask_ref,
+    turned_ref,
+    own_ref,
     pair_ref,
     taps_ref,
     main_total_ref,
     strip_total_ref,
     weight_ref,
-    own_ref,
     main_ref,
     strip_ref,
 ):
@@ -260,10 +253,7 @@
     spread = jnp.broadcast_to(weights_ref[...].reshape(1, wanted[1]), wanted)
     column = jnp.sum(jnp.where(plane // 2 == member, spread, 0.0), axis=1, keepdims=True)
     weight_ref[...] = jnp.broadcast_to(column, weight_ref.shape)
-    depth = GROUP * ambit
-    tap = lax.broadcasted_iota(jnp.int32, (depth, depth), 0)
-    lane = lax.broadcasted_iota(jnp.int32, (depth, depth), 1)
-    turned = jnp.where(tap == (lane ^ 7), 1.0, 0.0).astype(jnp.bfloat16)
+    turned = turned_ref[...]
     by_row = jnp.transpose(kernels_ref[...].reshape(planes, ambit, ambit), (1, 0, 2))
     for group in range(plan.tap_groups):
         pieces = [by_row[GROUP * group + part] for part in range(GROUP)]
@@ -272,8 +262,7 @@
         taps = jnp.dot(taps, turned, preferred_element_type=jnp.float32)
         taps_ref[place : place + planes, :] = taps.astype(jnp.bfloat16)
     even = lax.axis_index("tile") % 2 == 0
-    own, pair = own_window(mask_ref, lax.axis_index("kern"), kern_count, plan.lead), pair_ref[...]
-    own_ref[...] = own
+    own, pair = own_ref[: plan.rows], pair_ref[: plan.rows]
     window = jnp.concatenate([jnp.where(even, own, pair), jnp.where(even, pair, own)], axis=0)
     shifts = Shifts(window, ambit, 0, main_ref, strip_ref)
     first_row = {"upper": RIM, "lower": plan.lead}
@@ -318,8 +307,9 @@
     own_ref,
     other_ref,
     pair_ref,
-    received_ref,
-    quencher_ref,
+    far_pair_ref,
+    far_other_ref,
+    wide_ref,
     taps_ref,
     main_in_ref,
     strip_in_ref,
@@ -339,21 +329,19 @@
     rows, ambit = plan.rows, plan.ambit
     planes = taps_ref.shape[0] // plan.tap_groups
 
-    def far_rows(step):
-        place = jnp.clip(tile + step, 0, tile_count - 1)
-        inside_tile = jnp.logical_and(tile + step >= 0, tile + step < tile_count)
-        blocks = []
-        for side in (-1, 0, 1):
-            column = jnp.clip(kern + side, 0, kern_count - 1)
-            inside = jnp.logical_and(kern + side >= 0, kern + side < kern_count)
-            block = received_ref[column, place]
-            blocks.append(jnp.where(jnp.logical_and(inside, inside_tile), block, 0.0))
-        return lane_roll_left(jnp.concatenate(blocks, axis=1), LANES - plan.lead)[:, : 2 * LANES]
+    def far_rows(above_tile):
+        place = slice(rows - RIM, rows) if above_tile else slice(RIM)
+        blocks = [three_blocks(ref, place, kern, kern_count) for ref in (far_pair_ref, far_other_ref)]
+        with_pair = ((tile // 2) % 2 == 1) == above_tile
+        chosen = jnp.where(with_pair, blocks[0], blocks[1])
+        return lane_roll_left(chosen, LANES - plan.lead)[:, : 2 * LANES]
 
     even = tile % 2 == 0
     pair, other = pair_ref[...], other_ref[...]
     above, below = jnp.where(even, other, pair), jnp.where(even, pair, other)
-    window = jnp.concatenate([far_rows(-2), above, own_ref[...], below, far_rows(2)], axis=0)
+    window = jnp.concatenate(
+        [far_rows(True), above[:rows], own_ref[:rows], below[:rows], far_rows(False)], axis=0
+    )
     shifts = Shifts(window, ambit, 0, main_ref, strip_ref)
     first_row = {"upper": 0, "lower": 0}
     refs, sources = (main_total_ref, strip_total_ref), (main_in_ref, strip_in_ref)
@@ -381,27 +369,7 @@
     valid = (at_row >= 0) & (at_row < tile_count * rows) & (at_column >= 0) & (at_column < kern_count * LANES)
     valid = valid & (lane_id < LANES + 2 * RIM)
 
-    def rim_rows(step):
-        place = jnp.clip(tile + step, 0, tile_count - 1)
-        return jnp.concatenate(
-            [received_ref[jnp.clip(kern + side, 0, kern_count - 1), place] for side in (-1, 0, 1)], axis=1
-        )
-
-    before = received_ref[jnp.clip(kern - 1, 0, kern_count - 1), tile]
-    after = received_ref[jnp.clip(kern + 1, 0, kern_count - 1), tile]
-    middle = [
-        jnp.concatenate(
-            [
-                lane_roll_left(before, RIM * part + RIM),
-                quencher_ref[RIM * part : RIM * part + RIM, :],
-                lane_roll_left(after, RIM * part),
-            ],
-            axis=1,
-        )
-        for part in range(rows // RIM)
-    ]
-    base = jnp.concatenate([rim_rows(-1)] + middle + [rim_rows(1)], axis=0)
-    base = lane_roll_left(base, LANES - RIM)[:, : 2 * LANES]
+    base = jnp.concatenate([above[rows:], wide_ref[...], below[rows:]], axis=0)
     base = jnp.where(valid, base, 0.0)
     acid = jnp.where(valid, 1.0 - jnp.exp(-EXPOSURE * image), 0.0)
 
@@ -443,43 +411,53 @@
     vmem = pl.BlockSpec(memory_space=pltpu.VMEM)
     limit = pltpu.CompilerParams(vmem_limit_bytes=24 * 1024 * 1024)
 
-    send, window = pl.pallas_call(
-        functools.partial(prepare_kernel, kern_count, tile_count, plan.lead),
-        out_shape=(
-            jax.ShapeDtypeStruct((kern_count, tile_count, RIM, LANES), jnp.float32),
-            jax.ShapeDtypeStruct((rows, 2 * LANES), jnp.float32),
-        ),
+    assert kern_count <= 4
+    turned = pl.pallas_call(
+        turn_kernel,
+        out_shape=jax.ShapeDtypeStruct((GROUP * ambit, GROUP * ambit), jnp.bfloat16),
+        out_specs=vmem,
+        compiler_params=limit,
         cost_estimate=pl.CostEstimate(flops=10**9, bytes_accessed=10**7, transcendentals=0),
-        name="prepare",
-    )(mask, quencher)
-    received = lax.all_to_all(
-        send.reshape(kern_count * tile_count, RIM, LANES), ("kern", "tile"), 0, 0, tiled=True
-    ).reshape(send.shape)
-    pair = swapped(window, "tile", 0)
-    other = swapped(window, "tile", 1)
+        name="turned",
+    )()
+    across = swapped(quencher, "kern", 0, 2)
+    far_pair = swapped(mask, "tile", 0, 2)
+    beside = swapped(quencher, "kern", 0)
+    across = swapped(across, "kern", 0)
+    far_other = swapped(mask, "tile", 1, 2)
+    sent = jax.ShapeDtypeStruct((rows + RIM, 2 * LANES), jnp.float32)
+    wide, for_pair, for_other = pl.pallas_call(
+        functools.partial(rim_kernel, kern_count, plan.lead),
+        out_shape=(jax.ShapeDtypeStruct((rows, 2 * LANES), jnp.float32), sent, sent),
+        in_specs=[vmem] * 5,
+        out_specs=(vmem,) * 3,
+        compiler_params=limit,
+        name="rims",
+    )(turned, mask, quencher, beside, across)
+    pair = swapped(for_pair, "tile", 0)
+    other = swapped(for_other, "tile", 1)
 
     main_total = jax.ShapeDtypeStruct((plan.groups * planes, 4 * LANES), jnp.float32)
     strip_total = jax.ShapeDtypeStruct((plan.strip_groups * planes, 2 * LANES), jnp.float32)
-    taps, *totals, weight, own = pl.pallas_call(
-        functools.partial(near_rows_kernel, plan, kern_count),
+    taps, *totals, weight = pl.pallas_call(
+        functools.partial(near_rows_kernel, plan),
         out_shape=(
             jax.ShapeDtypeStruct((plan.tap_groups * planes, GROUP * ambit), jnp.bfloat16),
             main_total,
             strip_total,
             jax.ShapeDtypeStruct((planes, LANES), jnp.float32),
-            jax.ShapeDtypeStruct(window.shape, jnp.float32),
         ),
-        in_specs=[vmem] * 4,
-        out_specs=(vmem,) * 5,
+        in_specs=[vmem] * 5,
+        out_specs=(vmem,) * 4,
         scratch_shapes=[pltpu.VMEM((2 * rows * ambit, LANES), jnp.bfloat16)] * 2,
         compiler_params=limit,
         name="near_rows",
-    )(kernels, socs_weights, mask, pair)
+    )(kernels, socs_weights, turned, for_pair, pair)
     block = jax.ShapeDtypeStruct((rows, LANES), jnp.float32)
     return pl.pallas_call(
         functools.partial(resist_kernel, plan, kern_count, tile_count),
         out_shape=(block, block, block),
-        in_specs=[vmem] * 9,
+        in_specs=[vmem] * 10,
         out_specs=(pl.BlockSpec(memory_space=pl.ANY),) * 3,
         scratch_shapes=[pltpu.VMEM((plan.span * ambit, LANES), jnp.bfloat16)] * 2
         + [
@@ -491,7 +469,7 @@
         ],
         compiler_params=limit,
         name="image_and_resist",
-    )(own, other, pair, received, quencher, taps, *totals, weight)
+    )(for_pair, other, pair, far_pair, far_other, wide, taps, *totals, weight)
 
 
 def solution(mesh):

time: 21.3 us -> 20.7 us (0.972)
  the two profiles are of different devices: /device:TPU:0 before, /device:TPU:8 now
where the time goes in v5:
time: 20.7 us; the launch traced here: 20.6 us
  starting transfers between devices  10.2 us (49%)
  Pallas kernels  6.76 us (33%)
  waiting for transfers between devices  2.88 us (14%)
  between operations  0.74 us (4%)
    ppermute x7, starting transfers between devices, swapped(): lax.ppermute(value, axis, pairs + [(high, low) for low, high in pairs])  10.2 us
    pallas_call x1, Pallas kernels, on_device(): pl.pallas_call(functools.partial(resist_kernel, plan, kern_count, tile_co...  3.55 us
    pallas_call x1, Pallas kernels, on_device(): pl.pallas_call(functools.partial(near_rows_kernel, plan), out_shape=(jax....  3.09 us
    ppermute x7, waiting for transfers between devices, swapped(): lax.ppermute(value, axis, pairs + [(high, low) for low, high in pairs])  2.88 us
  transfers between devices with their start and end apart: 7, of which 3 were waited for; matrix products, arithmetic and copies ran while one was open for 0% of the time, Pallas kernels for 16%

profile of v5, /device:TPU:8, one launch (start us, length us, event | category | flops | bytes accessed | tf_op | source)
XLA Modules:
  0.0 20.6 jit_solution(2081087678406072376)
XLA Ops:
  0.6 0.0 copy-start.2
  0.6 0.0 copy-start.1
  0.7 0.0 copy-start
  0.7 0.0 copy-start.3
  0.7 1.6 %collective-permute-start.1 = (f32[32,128]{1,0:T(8,128)}, f32[32,128]{1,0:T(8,128)S(1)}, u32[]{:S(2)}, u32[]{:S(2)}) collective-permute-start(f32[32,128]{1,0:T(8,128)} %quencher_ref.1), channel_id=1, source_target_pairs={{0,16},{8,24},{16,0},{24,8},{1,17},{9,25},{17,1},{25,9},{2,18},{10... | collective-permute-start | bytes 49160 | tf_op jit(solution)/shard_map/ppermute | solution.py:74
  2.2 0.0 collective-permute-start
  2.2 0.4 %collective-permute-start.5 = (s32[32,512]{1,0:T(8,128)}, s32[32,512]{1,0:T(8,128)S(1)}, u32[]{:S(2)}, u32[]{:S(2)}) collective-permute-start(s32[32,512]{1,0:T(8,128)} %mask_ref.1), channel_id=1, source_target_pairs={{0,2},{1,3},{4,6},{5,7},{2,0},{3,1},{6,4},{7,5},{8,10},{9,11},{12,... | collective-permute-start | bytes 196616 | tf_op jit(solution)/shard_map/ppermute | solution.py:74
  2.7 4.6 %collective-permute-start.6 = (s32[32,512]{1,0:T(8,128)}, s32[32,512]{1,0:T(8,128)S(1)}, u32[]{:S(2)}, u32[]{:S(2)}) collective-permute-start(s32[32,512]{1,0:T(8,128)} %mask_ref.1), channel_id=1, source_target_pairs={{2,4},{3,5},{4,2},{5,3},{10,12},{11,13},{12,10},{13,11},{18,20},{1... | collective-permute-start | bytes 196616 | tf_op jit(solution)/shard_map/ppermute | solution.py:74
  7.3 0.0 collective-permute-done.1
  7.3 0.1 collective-permute-start.2
  7.4 0.0 collective-permute-done.beside_ref
  7.4 1.1 %collective-permute-done.2.across_ref = f32[32,128]{1,0:T(8,128)S(1)} collective-permute-done((f32[32,128]{1,0:T(8,128)S(1)}, f32[32,128]{1,0:T(8,128)S(1)}, u32[]{:S(2)}, u32[]{:S(2)}) %collective-permute-start.2) | collective-permute-done | bytes 16416 | tf_op jit(solution)/shard_map/ppermute | solution.py:74
  8.5 0.0 copy-done.2
  8.6 0.0 copy-done.1
  8.6 0.1 rims.1
  8.7 1.6 %collective-permute-start.4 = (f32[40,256]{1,0:T(8,128)S(1)}, f32[40,256]{1,0:T(8,128)S(1)}, u32[]{:S(2)}, u32[]{:S(2)}) collective-permute-start(f32[40,256]{1,0:T(8,128)S(1)} %get-tuple-element.10.own_ref), channel_id=1, source_target_pairs={{0,1},{2,3},{4,5},{6,7},{1,0},{3,2},{5,4},{7,6},{8,9},{10,11},{12,... | collective-permute-start | bytes 122888 | tf_op jit(solution)/shard_map/ppermute | solution.py:74
  10.2 1.9 %collective-permute-start.3 = (f32[40,256]{1,0:T(8,128)S(1)}, f32[40,256]{1,0:T(8,128)S(1)}, u32[]{:S(2)}, u32[]{:S(2)}) collective-permute-start(f32[40,256]{1,0:T(8,128)S(1)} %get-tuple-element.11), channel_id=1, source_target_pairs={{1,2},{3,4},{5,6},{2,1},{4,3},{6,5},{9,10},{11,12},{13,14},{10,9},... | collective-permute-start | bytes 122888 | tf_op jit(solution)/shard_map/ppermute | solution.py:74
  12.2 0.6 %collective-permute-done.4.pair_ref = f32[40,256]{1,0:T(8,128)S(1)} collective-permute-done((f32[40,256]{1,0:T(8,128)S(1)}, f32[40,256]{1,0:T(8,128)S(1)}, u32[]{:S(2)}, u32[]{:S(2)}) %collective-permute-start.4) | collective-permute-done | bytes 40992 | tf_op jit(solution)/shard_map/ppermute | solution.py:74
  12.7 0.0 copy-done
  12.7 0.0 copy-done.3
  12.7 3.1 %near_rows.1 = (bf16[768,256]{1,0:T(8,128)(2,1)S(1)}, f32[576,512]{1,0:T(8,128)S(1)}, f32[144,256]{1,0:T(8,128)S(1)}, f32[48,128]{1,0:T(8,128)S(1)}) custom-call(bf16[24,2,64,64]{3,2,1,0:T(8,128)(2,1)S(1)} %copy-done, f32[24]{0:T(128)S(1)} %copy-done.3, bf16[256,256]{1,0:T(8,128)(2,1)S(1)} %turned.1._.turned_ref, f32[40,256]{1,0:T(8,128)S(1)} %get-tuple-element.10.own_ref, ...), custom_call_target="tpu_custom_call" | custom-call | tf_op jit(solution)/shard_map/near_rows/pallas_call | solution.py:442
  15.8 0.0 collective-permute-done.5.far_pair_ref
  15.8 0.0 collective-permute-done.6.far_other_ref
  15.9 1.2 %collective-permute-done.3.other_ref = f32[40,256]{1,0:T(8,128)S(1)} collective-permute-done((f32[40,256]{1,0:T(8,128)S(1)}, f32[40,256]{1,0:T(8,128)S(1)}, u32[]{:S(2)}, u32[]{:S(2)}) %collective-permute-start.3) | collective-permute-done | bytes 40992 | tf_op jit(solution)/shard_map/ppermute | solution.py:74
  17.0 3.5 %image_and_resist.1 = (f32[32,128]{1,0:T(8,128)}, f32[32,128]{1,0:T(8,128)}, f32[32,128]{1,0:T(8,128)}) custom-call(f32[40,256]{1,0:T(8,128)S(1)} %get-tuple-element.10.own_ref, f32[40,256]{1,0:T(8,128)S(1)} %collective-permute-done.3.other_ref, f32[40,256]{1,0:T(8,128)S(1)} %collective-permute-done.4.pair_ref, ...), custom_call_target="tpu_custom_call" | custom-call | tf_op jit(solution)/shard_map/image_and_resist/pallas_call | solution.py:457
  (1 shorter events, 0.0 us)
Async XLA Ops:
  0.6 7.9 %copy-start.2 = (f32[32,128]{1,0:T(8,128)S(1)}, f32[32,128]{1,0:T(8,128)}, u32[]{:S(2)}) copy-start(f32[32,128]{1,0:T(8,128)} %quencher_ref.1) | copy-start | bytes 49156
  0.6 7.9 %copy-start.1 = (s32[32,512]{1,0:T(8,128)S(1)}, s32[32,512]{1,0:T(8,128)}, u32[]{:S(2)}) copy-start(s32[32,512]{1,0:T(8,128)} %mask_ref.1) | copy-start | bytes 196612
  0.7 12.1 %copy-start = (bf16[24,2,64,64]{3,2,1,0:T(8,128)(2,1)S(1)}, bf16[24,2,64,64]{3,2,1,0:T(8,128)(2,1)}, u32[]{:S(2)}) copy-start(bf16[24,2,64,64]{3,2,1,0:T(8,128)(2,1)} %kernels_ref.1) | copy-start | bytes 1179652
  0.7 12.1 %copy-start.3 = (f32[24]{0:T(128)S(1)}, f32[24]{0:T(128)}, u32[]{:S(2)}) copy-start(f32[24]{0:T(128)} %weights_ref.1) | copy-start | bytes 292
  0.7 6.6 %collective-permute-start.1 = (f32[32,128]{1,0:T(8,128)}, f32[32,128]{1,0:T(8,128)S(1)}, u32[]{:S(2)}, u32[]{:S(2)}) collective-permute-start(f32[32,128]{1,0:T(8,128)} %quencher_ref.1), channel_id=1, source_target_pairs={{0,16},{8,24},{16,0},{24,8},{1,17},{9,25},{17,1},{25,9},{2,18},{10... | collective-permute-start | bytes 49160 | tf_op jit(solution)/shard_map/ppermute | solution.py:74
  2.2 5.2 %collective-permute-start = (f32[32,128]{1,0:T(8,128)}, f32[32,128]{1,0:T(8,128)S(1)}, u32[]{:S(2)}, u32[]{:S(2)}) collective-permute-start(f32[32,128]{1,0:T(8,128)} %quencher_ref.1), channel_id=1, source_target_pairs={{0,8},{16,24},{8,0},{24,16},{1,9},{17,25},{9,1},{25,17},{2,10},{18... | collective-permute-start | bytes 49160 | tf_op jit(solution)/shard_map/ppermute | solution.py:74
  2.2 13.6 %collective-permute-start.5 = (s32[32,512]{1,0:T(8,128)}, s32[32,512]{1,0:T(8,128)S(1)}, u32[]{:S(2)}, u32[]{:S(2)}) collective-permute-start(s32[32,512]{1,0:T(8,128)} %mask_ref.1), channel_id=1, source_target_pairs={{0,2},{1,3},{4,6},{5,7},{2,0},{3,1},{6,4},{7,5},{8,10},{9,11},{12,... | collective-permute-start | bytes 196616 | tf_op jit(solution)/shard_map/ppermute | solution.py:74
  2.7 13.2 %collective-permute-start.6 = (s32[32,512]{1,0:T(8,128)}, s32[32,512]{1,0:T(8,128)S(1)}, u32[]{:S(2)}, u32[]{:S(2)}) collective-permute-start(s32[32,512]{1,0:T(8,128)} %mask_ref.1), channel_id=1, source_target_pairs={{2,4},{3,5},{4,2},{5,3},{10,12},{11,13},{12,10},{13,11},{18,20},{1... | collective-permute-start | bytes 196616 | tf_op jit(solution)/shard_map/ppermute | solution.py:74
  7.3 1.2 %collective-permute-start.2 = (f32[32,128]{1,0:T(8,128)S(1)}, f32[32,128]{1,0:T(8,128)S(1)}, u32[]{:S(2)}, u32[]{:S(2)}) collective-permute-start(f32[32,128]{1,0:T(8,128)S(1)} %collective-permute-done.1), channel_id=1, source_target_pairs={{0,8},{16,24},{8,0},{24,16},{1,9},{17,25},{9,1},{25,17},{2,10},{18... | collective-permute-start | bytes 49160 | tf_op jit(solution)/shard_map/ppermute | solution.py:74
  8.7 4.1 %collective-permute-start.4 = (f32[40,256]{1,0:T(8,128)S(1)}, f32[40,256]{1,0:T(8,128)S(1)}, u32[]{:S(2)}, u32[]{:S(2)}) collective-permute-start(f32[40,256]{1,0:T(8,128)S(1)} %get-tuple-element.10.own_ref), channel_id=1, source_target_pairs={{0,1},{2,3},{4,5},{6,7},{1,0},{3,2},{5,4},{7,6},{8,9},{10,11},{12,... | collective-permute-start | bytes 122888 | tf_op jit(solution)/shard_map/ppermute | solution.py:74
  10.2 6.8 %collective-permute-start.3 = (f32[40,256]{1,0:T(8,128)S(1)}, f32[40,256]{1,0:T(8,128)S(1)}, u32[]{:S(2)}, u32[]{:S(2)}) collective-permute-start(f32[40,256]{1,0:T(8,128)S(1)} %get-tuple-element.11), channel_id=1, source_target_pairs={{1,2},{3,4},{5,6},{2,1},{4,3},{6,5},{9,10},{11,12},{13,14},{10,9},... | collective-permute-start | bytes 122888 | tf_op jit(solution)/shard_map/ppermute | solution.py:74

commit v6 on v5

--- a/solution.py
+++ b/solution.py
@@ -48,12 +48,13 @@
 
 
 def rim_kernel(
-    kern_count, lead, _, mask_ref, quencher_ref, beside_ref, across_ref, wide_ref, for_pair_ref, for_other_ref
+    kern_count, lead, _, mask_ref, quencher_ref, beside_ref, across_ref, window_ref, wide_ref, for_pair_ref, for_other_ref
 ):
     rows = mask_ref.shape[0]
     kern = lax.axis_index("kern")
     odd = kern % 2 == 1
     window = own_window(mask_ref, kern, kern_count, lead)
+    window_ref[...] = window
     beside, across = beside_ref[...], across_ref[...]
     before, after = jnp.where(odd, beside, across), jnp.where(odd, across, beside)
     wide = jnp.concatenate([before, quencher_ref[...], after], axis=1)
@@ -231,13 +232,12 @@
             add_strip(self, totals[1], taps_ref, shifts, s)
 
 
-def near_rows_kernel(
+def own_rows_kernel(
     plan,
     kernels_ref,
     weights_ref,
     turned_ref,
-    own_ref,
-    pair_ref,
+    window_ref,
     taps_ref,
     main_total_ref,
     strip_total_ref,
@@ -261,12 +261,11 @@
         taps = jnp.concatenate(pieces, axis=1)
         taps = jnp.dot(taps, turned, preferred_element_type=jnp.float32)
         taps_ref[place : place + planes, :] = taps.astype(jnp.bfloat16)
-    even = lax.axis_index("tile") % 2 == 0
-    own, pair = own_ref[: plan.rows], pair_ref[: plan.rows]
-    window = jnp.concatenate([jnp.where(even, own, pair), jnp.where(even, pair, own)], axis=0)
-    shifts = Shifts(window, ambit, 0, main_ref, strip_ref)
-    first_row = {"upper": RIM, "lower": plan.lead}
-    add_side(plan, even, (main_total_ref, strip_total_ref), (None, None), taps_ref, shifts, first_row, before=("own",))
+    shifts = Shifts(window_ref[...], ambit, plan.lead, main_ref, strip_ref)
+    totals = Total(main_total_ref, None, planes), Total(strip_total_ref, None, planes)
+    plan.add("own", totals, taps_ref, shifts)
+    for total in totals:
+        total.finish()
 
 
 def weighted_rows(weight, total_ref, group):
@@ -283,13 +282,13 @@
             image_ref[row : row + 1, :LANES] = summed[:, LANES * part : LANES * (part + 1)]
 
 
-def add_side(plan, below, refs, sources, taps_ref, shifts, first_row, before=(), after=(), then=None):
+def add_side(plan, below, refs, sources, taps_ref, shifts, first_row, after=(), then=None):
     planes = taps_ref.shape[0] // plan.tap_groups
 
     def add(name):
         totals = [Total(ref, source, planes) for ref, source in zip(refs, sources)]
         view = shifts.view(first_row[name])
-        for part in (*before, name, *after):
+        for part in (name, *after):
             plan.add(part, totals, taps_ref, view)
         for total in totals:
             total.finish()
@@ -298,6 +297,26 @@
 
     pl.when(below)(lambda: add("lower"))
     pl.when(jnp.logical_not(below))(lambda: add("upper"))
+
+
+def pair_rows_kernel(
+    plan,
+    own_ref,
+    pair_ref,
+    taps_ref,
+    main_in_ref,
+    strip_in_ref,
+    main_total_ref,
+    strip_total_ref,
+    main_ref,
+    strip_ref,
+):
+    even = lax.axis_index("tile") % 2 == 0
+    own, pair = own_ref[...], pair_ref[: plan.rows]
+    window = jnp.concatenate([jnp.where(even, own, pair), jnp.where(even, pair, own)], axis=0)
+    shifts = Shifts(window, plan.ambit, 0, main_ref, strip_ref)
+    refs, sources = (main_total_ref, strip_total_ref), (main_in_ref, strip_in_ref)
+    add_side(plan, even, refs, sources, taps_ref, shifts, {"upper": RIM, "lower": plan.lead})
 
 
 def resist_kernel(
@@ -307,8 +326,8 @@
     own_ref,
     other_ref,
     pair_ref,
+    far_other_ref,
     far_pair_ref,
-    far_other_ref,
     wide_ref,
     taps_ref,
     main_in_ref,
@@ -340,7 +359,7 @@
     pair, other = pair_ref[...], other_ref[...]
     above, below = jnp.where(even, other, pair), jnp.where(even, pair, other)
     window = jnp.concatenate(
-        [far_rows(True), above[:rows], own_ref[:rows], below[:rows], far_rows(False)], axis=0
+        [far_rows(True), above[:rows], own_ref[...], below[:rows], far_rows(False)], axis=0
     )
     shifts = Shifts(window, ambit, 0, main_ref, strip_ref)
     first_row = {"upper": 0, "lower": 0}
@@ -423,36 +442,45 @@
     across = swapped(quencher, "kern", 0, 2)
     far_pair = swapped(mask, "tile", 0, 2)
     beside = swapped(quencher, "kern", 0)
+    far_other = swapped(mask, "tile", 1, 2)
+    main_total = jax.ShapeDtypeStruct((plan.groups * planes, 4 * LANES), jnp.float32)
+    strip_total = jax.ShapeDtypeStruct((plan.strip_groups * planes, 2 * LANES), jnp.float32)
+    wide_rows = jax.ShapeDtypeStruct((rows, 2 * LANES), jnp.float32)
+    sent = jax.ShapeDtypeStruct((rows + RIM, 2 * LANES), jnp.float32)
     across = swapped(across, "kern", 0)
-    far_other = swapped(mask, "tile", 1, 2)
-    sent = jax.ShapeDtypeStruct((rows + RIM, 2 * LANES), jnp.float32)
-    wide, for_pair, for_other = pl.pallas_call(
+    window, wide, for_pair, for_other = pl.pallas_call(
         functools.partial(rim_kernel, kern_count, plan.lead),
-        out_shape=(jax.ShapeDtypeStruct((rows, 2 * LANES), jnp.float32), sent, sent),
+        out_shape=(wide_rows, wide_rows, sent, sent),
         in_specs=[vmem] * 5,
-        out_specs=(vmem,) * 3,
+        out_specs=(vmem,) * 4,
         compiler_params=limit,
         name="rims",
     )(turned, mask, quencher, beside, across)
     pair = swapped(for_pair, "tile", 0)
     other = swapped(for_other, "tile", 1)
-
-    main_total = jax.ShapeDtypeStruct((plan.groups * planes, 4 * LANES), jnp.float32)
-    strip_total = jax.ShapeDtypeStruct((plan.strip_groups * planes, 2 * LANES), jnp.float32)
     taps, *totals, weight = pl.pallas_call(
-        functools.partial(near_rows_kernel, plan),
+        functools.partial(own_rows_kernel, plan),
         out_shape=(
             jax.ShapeDtypeStruct((plan.tap_groups * planes, GROUP * ambit), jnp.bfloat16),
             main_total,
             strip_total,
             jax.ShapeDtypeStruct((planes, LANES), jnp.float32),
         ),
+        in_specs=[vmem] * 4,
+        out_specs=(vmem,) * 4,
+        scratch_shapes=[pltpu.VMEM((rows * ambit, LANES), jnp.bfloat16)] * 2,
+        compiler_params=limit,
+        name="own_rows",
+    )(kernels, socs_weights, turned, window)
+    totals = pl.pallas_call(
+        functools.partial(pair_rows_kernel, plan),
+        out_shape=(main_total, strip_total),
         in_specs=[vmem] * 5,
-        out_specs=(vmem,) * 4,
+        out_specs=(vmem,) * 2,
         scratch_shapes=[pltpu.VMEM((2 * rows * ambit, LANES), jnp.bfloat16)] * 2,
         compiler_params=limit,
-        name="near_rows",
-    )(kernels, socs_weights, turned, for_pair, pair)
+        name="pair_rows",
+    )(window, pair, taps, *totals)
     block = jax.ShapeDtypeStruct((rows, LANES), jnp.float32)
     return pl.pallas_call(
         functools.partial(resist_kernel, plan, kern_count, tile_count),
@@ -469,7 +497,7 @@
         ],
         compiler_params=limit,
         name="image_and_resist",
-    )(for_pair, other, pair, far_pair, far_other, wide, taps, *totals, weight)
+    )(window, other, pair, far_other, far_pair, wide, taps, *totals, weight)
 
 
 def solution(mesh):

time: 20.7 us -> 19.7 us (0.952)
  the two profiles are of different devices: /device:TPU:8 before, /device:TPU:4 now
where the time goes in v6:
time: 19.7 us; the launch traced here: 19.5 us
  starting transfers between devices  10.2 us (52%)
  Pallas kernels  6.94 us (35%)
  waiting for transfers between devices  1.6 us (8%)
  between operations  0.75 us (4%)
    ppermute x7, starting transfers between devices, swapped(): lax.ppermute(value, axis, pairs + [(high, low) for low, high in pairs])  10.2 us
    pallas_call x1, Pallas kernels, on_device(): pl.pallas_call(functools.partial(resist_kernel, plan, kern_count, tile_co...  3.48 us
    pallas_call x1, Pallas kernels, on_device(): pl.pallas_call(functools.partial(own_rows_kernel, plan), out_shape=(jax.S...  1.85 us
    ppermute x7, waiting for transfers between devices, swapped(): lax.ppermute(value, axis, pairs + [(high, low) for low, high in pairs])  1.6 us
    pallas_call x1, Pallas kernels, on_device(): pl.pallas_call(functools.partial(pair_rows_kernel, plan), out_shape=(main...  1.48 us
  transfers between devices with their start and end apart: 7, of which 2 were waited for; matrix products, arithmetic and copies ran while one was open for 0% of the time, Pallas kernels for 18%

profile of v6, /device:TPU:4, one launch (start us, length us, event | category | flops | bytes accessed | tf_op | source)
XLA Modules:
  0.0 19.5 jit_solution(7427827077757550145)
XLA Ops:
  0.6 0.0 copy-start.2
  0.6 0.0 copy-start.1
  0.7 0.0 copy-start
  0.7 0.0 copy-start.3
  0.7 1.6 %collective-permute-start.1 = (f32[32,128]{1,0:T(8,128)}, f32[32,128]{1,0:T(8,128)S(1)}, u32[]{:S(2)}, u32[]{:S(2)}) collective-permute-start(f32[32,128]{1,0:T(8,128)} %quencher_ref.1), channel_id=1, source_target_pairs={{0,16},{8,24},{16,0},{24,8},{1,17},{9,25},{17,1},{25,9},{2,18},{10... | collective-permute-start | bytes 49160 | tf_op jit(solution)/shard_map/ppermute | solution.py:75
  2.2 0.0 collective-permute-start
  2.2 0.7 %collective-permute-start.5 = (s32[32,512]{1,0:T(8,128)}, s32[32,512]{1,0:T(8,128)S(1)}, u32[]{:S(2)}, u32[]{:S(2)}) collective-permute-start(s32[32,512]{1,0:T(8,128)} %mask_ref.1), channel_id=1, source_target_pairs={{2,4},{3,5},{4,2},{5,3},{10,12},{11,13},{12,10},{13,11},{18,20},{1... | collective-permute-start | bytes 196616 | tf_op jit(solution)/shard_map/ppermute | solution.py:75
  2.9 4.5 %collective-permute-start.6 = (s32[32,512]{1,0:T(8,128)}, s32[32,512]{1,0:T(8,128)S(1)}, u32[]{:S(2)}, u32[]{:S(2)}) collective-permute-start(s32[32,512]{1,0:T(8,128)} %mask_ref.1), channel_id=1, source_target_pairs={{0,2},{1,3},{4,6},{5,7},{2,0},{3,1},{6,4},{7,5},{8,10},{9,11},{12,... | collective-permute-start | bytes 196616 | tf_op jit(solution)/shard_map/ppermute | solution.py:75
  7.4 0.0 collective-permute-done.1
  7.4 0.0 collective-permute-start.2
  7.4 0.0 collective-permute-done.beside_ref
  7.4 1.1 %collective-permute-done.2.across_ref = f32[32,128]{1,0:T(8,128)S(1)} collective-permute-done((f32[32,128]{1,0:T(8,128)S(1)}, f32[32,128]{1,0:T(8,128)S(1)}, u32[]{:S(2)}, u32[]{:S(2)}) %collective-permute-start.2) | collective-permute-done | bytes 16416 | tf_op jit(solution)/shard_map/ppermute | solution.py:75
  8.5 0.0 copy-done.2
  8.5 0.0 copy-done.1
  8.5 0.1 rims.1
  8.7 0.6 %collective-permute-start.4 = (f32[40,256]{1,0:T(8,128)S(1)}, f32[40,256]{1,0:T(8,128)S(1)}, u32[]{:S(2)}, u32[]{:S(2)}) collective-permute-start(f32[40,256]{1,0:T(8,128)S(1)} %get-tuple-element.15), channel_id=1, source_target_pairs={{0,1},{2,3},{4,5},{6,7},{1,0},{3,2},{5,4},{7,6},{8,9},{10,11},{12,... | collective-permute-start | bytes 122888 | tf_op jit(solution)/shard_map/ppermute | solution.py:75
  9.2 2.9 %collective-permute-start.3 = (f32[40,256]{1,0:T(8,128)S(1)}, f32[40,256]{1,0:T(8,128)S(1)}, u32[]{:S(2)}, u32[]{:S(2)}) collective-permute-start(f32[40,256]{1,0:T(8,128)S(1)} %get-tuple-element.14), channel_id=1, source_target_pairs={{1,2},{3,4},{5,6},{2,1},{4,3},{6,5},{9,10},{11,12},{13,14},{10,9},... | collective-permute-start | bytes 122888 | tf_op jit(solution)/shard_map/ppermute | solution.py:75
  12.2 0.0 copy-done
  12.2 0.0 copy-done.3
  12.2 1.9 %own_rows.1 = (bf16[768,256]{1,0:T(8,128)(2,1)S(1)}, f32[576,512]{1,0:T(8,128)S(1)}, f32[144,256]{1,0:T(8,128)S(1)}, f32[48,128]{1,0:T(8,128)S(1)}) custom-call(bf16[24,2,64,64]{3,2,1,0:T(8,128)(2,1)S(1)} %copy-done, f32[24]{0:T(128)S(1)} %copy-done.3, bf16[256,256]{1,0:T(8,128)(2,1)S(1)} %turned.1._.turned_ref, ...), custom_call_target="tpu_custom_call" | custom-call | tf_op jit(solution)/shard_map/own_rows/pallas_call | solution.py:461
  14.1 0.0 collective-permute-done.4.pair_ref
  14.1 1.5 %pair_rows.1 = (f32[576,512]{1,0:T(8,128)S(1)}, f32[144,256]{1,0:T(8,128)S(1)}) custom-call(f32[32,256]{1,0:T(8,128)S(1)} %get-tuple-element.13.window_ref.own_ref, f32[40,256]{1,0:T(8,128)S(1)} %collective-permute-done.4.pair_ref, bf16[768,256]{1,0:T(8,128)(2,1)S(1)} %get-tuple-element.17.taps_ref, f32[576,512]{1,0:T(8,128)S(1)} %get-tuple-element.18.main_in_ref, ...), custom_call_target="tpu_custom_call" | custom-call | tf_op jit(solution)/shard_map/pair_rows/pallas_call | solution.py:475
  15.5 0.0 collective-permute-done.5.far_other_ref
  15.6 0.0 collective-permute-done.6.far_pair_ref
  15.6 0.4 %collective-permute-done.3.other_ref = f32[40,256]{1,0:T(8,128)S(1)} collective-permute-done((f32[40,256]{1,0:T(8,128)S(1)}, f32[40,256]{1,0:T(8,128)S(1)}, u32[]{:S(2)}, u32[]{:S(2)}) %collective-permute-start.3) | collective-permute-done | bytes 40992 | tf_op jit(solution)/shard_map/ppermute | solution.py:75
  16.0 3.5 %image_and_resist.1 = (f32[32,128]{1,0:T(8,128)}, f32[32,128]{1,0:T(8,128)}, f32[32,128]{1,0:T(8,128)}) custom-call(f32[32,256]{1,0:T(8,128)S(1)} %get-tuple-element.13.window_ref.own_ref, f32[40,256]{1,0:T(8,128)S(1)} %collective-permute-done.3.other_ref, f32[40,256]{1,0:T(8,128)S(1)} %collective-permute-done.4.pair_ref, ...), custom_call_target="tpu_custom_call" | custom-call | tf_op jit(solution)/shard_map/image_and_resist/pallas_call | solution.py:485
  (1 shorter events, 0.0 us)
Async XLA Ops:
  0.6 7.9 %copy-start.2 = (f32[32,128]{1,0:T(8,128)S(1)}, f32[32,128]{1,0:T(8,128)}, u32[]{:S(2)}) copy-start(f32[32,128]{1,0:T(8,128)} %quencher_ref.1) | copy-start | bytes 49156
  0.6 7.9 %copy-start.1 = (s32[32,512]{1,0:T(8,128)S(1)}, s32[32,512]{1,0:T(8,128)}, u32[]{:S(2)}) copy-start(s32[32,512]{1,0:T(8,128)} %mask_ref.1) | copy-start | bytes 196612
  0.7 11.5 %copy-start = (bf16[24,2,64,64]{3,2,1,0:T(8,128)(2,1)S(1)}, bf16[24,2,64,64]{3,2,1,0:T(8,128)(2,1)}, u32[]{:S(2)}) copy-start(bf16[24,2,64,64]{3,2,1,0:T(8,128)(2,1)} %kernels_ref.1) | copy-start | bytes 1179652
  0.7 11.5 %copy-start.3 = (f32[24]{0:T(128)S(1)}, f32[24]{0:T(128)}, u32[]{:S(2)}) copy-start(f32[24]{0:T(128)} %weights_ref.1) | copy-start | bytes 292
  0.7 6.7 %collective-permute-start.1 = (f32[32,128]{1,0:T(8,128)}, f32[32,128]{1,0:T(8,128)S(1)}, u32[]{:S(2)}, u32[]{:S(2)}) collective-permute-start(f32[32,128]{1,0:T(8,128)} %quencher_ref.1), channel_id=1, source_target_pairs={{0,16},{8,24},{16,0},{24,8},{1,17},{9,25},{17,1},{25,9},{2,18},{10... | collective-permute-start | bytes 49160 | tf_op jit(solution)/shard_map/ppermute | solution.py:75
  2.2 5.2 %collective-permute-start = (f32[32,128]{1,0:T(8,128)}, f32[32,128]{1,0:T(8,128)S(1)}, u32[]{:S(2)}, u32[]{:S(2)}) collective-permute-start(f32[32,128]{1,0:T(8,128)} %quencher_ref.1), channel_id=1, source_target_pairs={{0,8},{16,24},{8,0},{24,16},{1,9},{17,25},{9,1},{25,17},{2,10},{18... | collective-permute-start | bytes 49160 | tf_op jit(solution)/shard_map/ppermute | solution.py:75
  2.2 13.3 %collective-permute-start.5 = (s32[32,512]{1,0:T(8,128)}, s32[32,512]{1,0:T(8,128)S(1)}, u32[]{:S(2)}, u32[]{:S(2)}) collective-permute-start(s32[32,512]{1,0:T(8,128)} %mask_ref.1), channel_id=1, source_target_pairs={{2,4},{3,5},{4,2},{5,3},{10,12},{11,13},{12,10},{13,11},{18,20},{1... | collective-permute-start | bytes 196616 | tf_op jit(solution)/shard_map/ppermute | solution.py:75
  2.9 12.7 %collective-permute-start.6 = (s32[32,512]{1,0:T(8,128)}, s32[32,512]{1,0:T(8,128)S(1)}, u32[]{:S(2)}, u32[]{:S(2)}) collective-permute-start(s32[32,512]{1,0:T(8,128)} %mask_ref.1), channel_id=1, source_target_pairs={{0,2},{1,3},{4,6},{5,7},{2,0},{3,1},{6,4},{7,5},{8,10},{9,11},{12,... | collective-permute-start | bytes 196616 | tf_op jit(solution)/shard_map/ppermute | solution.py:75
  7.4 1.2 %collective-permute-start.2 = (f32[32,128]{1,0:T(8,128)S(1)}, f32[32,128]{1,0:T(8,128)S(1)}, u32[]{:S(2)}, u32[]{:S(2)}) collective-permute-start(f32[32,128]{1,0:T(8,128)S(1)} %collective-permute-done.1), channel_id=1, source_target_pairs={{0,8},{16,24},{8,0},{24,16},{1,9},{17,25},{9,1},{25,17},{2,10},{18... | collective-permute-start | bytes 49160 | tf_op jit(solution)/shard_map/ppermute | solution.py:75
  8.7 5.4 %collective-permute-start.4 = (f32[40,256]{1,0:T(8,128)S(1)}, f32[40,256]{1,0:T(8,128)S(1)}, u32[]{:S(2)}, u32[]{:S(2)}) collective-permute-start(f32[40,256]{1,0:T(8,128)S(1)} %get-tuple-element.15), channel_id=1, source_target_pairs={{0,1},{2,3},{4,5},{6,7},{1,0},{3,2},{5,4},{7,6},{8,9},{10,11},{12,... | collective-permute-start | bytes 122888 | tf_op jit(solution)/shard_map/ppermute | solution.py:75
  9.2 6.8 %collective-permute-start.3 = (f32[40,256]{1,0:T(8,128)S(1)}, f32[40,256]{1,0:T(8,128)S(1)}, u32[]{:S(2)}, u32[]{:S(2)}) collective-permute-start(f32[40,256]{1,0:T(8,128)S(1)} %get-tuple-element.14), channel_id=1, source_target_pairs={{1,2},{3,4},{5,6},{2,1},{4,3},{6,5},{9,10},{11,12},{13,14},{10,9},... | collective-permute-start | bytes 122888 | tf_op jit(solution)/shard_map/ppermute | solution.py:75

commit v7 on v6

--- a/solution.py
+++ b/solution.py
@@ -1,4 +1,3 @@
-import copy
 import functools
 
 import jax
@@ -99,18 +98,14 @@
         for offset in range(0, ambit, 8):
             mains.append(lane_roll_left(jnp.where(lane < offset, high, low), offset))
             strip = lane_roll_left(high, offset)
-            for width in (16, 32, 64):
-                strip = jnp.where(lane < width, strip, pltpu.roll(strip, width, 1))
+            for block in (1, 2, 3):
+                strip = jnp.where(lane < 16 * block, strip, lane_roll_left(high, offset - 16 * block))
+            strip = jnp.where(lane < 64, strip, pltpu.roll(strip, 64, 1))
             strips.append(strip >> (lane // 16))
         self.ambit, self.first_row = ambit, first_row
         self.sources = {"main": mains, "strip": strips}
         self.refs = {"main": main_ref, "strip": strip_ref}
         self.laid = {"main": set(), "strip": set()}
-
-    def view(self, first_row):
-        view = copy.copy(self)
-        view.first_row, view.laid = first_row, {"main": set(), "strip": set()}
-        return view
 
     def lay(self, kind, rows):
         for row in rows:
@@ -232,19 +227,7 @@
             add_strip(self, totals[1], taps_ref, shifts, s)
 
 
-def own_rows_kernel(
-    plan,
-    kernels_ref,
-    weights_ref,
-    turned_ref,
-    window_ref,
-    taps_ref,
-    main_total_ref,
-    strip_total_ref,
-    weight_ref,
-    main_ref,
-    strip_ref,
-):
+def taps_kernel(plan, kernels_ref, weights_ref, turned_ref, taps_ref, weight_ref):
     ambit = plan.ambit
     planes = kernels_ref.shape[0] * kernels_ref.shape[1]
     wanted = (weight_ref.shape[0], weights_ref.shape[0])
@@ -261,7 +244,11 @@
         taps = jnp.concatenate(pieces, axis=1)
         taps = jnp.dot(taps, turned, preferred_element_type=jnp.float32)
         taps_ref[place : place + planes, :] = taps.astype(jnp.bfloat16)
-    shifts = Shifts(window_ref[...], ambit, plan.lead, main_ref, strip_ref)
+
+
+def own_rows_kernel(plan, window_ref, taps_ref, main_total_ref, strip_total_ref, main_ref, strip_ref):
+    planes = taps_ref.shape[0] // plan.tap_groups
+    shifts = Shifts(window_ref[...], plan.ambit, plan.lead, main_ref, strip_ref)
     totals = Total(main_total_ref, None, planes), Total(strip_total_ref, None, planes)
     plan.add("own", totals, taps_ref, shifts)
     for total in totals:
@@ -282,14 +269,14 @@
             image_ref[row : row + 1, :LANES] = summed[:, LANES * part : LANES * (part + 1)]
 
 
-def add_side(plan, below, refs, sources, taps_ref, shifts, first_row, after=(), then=None):
+def add_side(plan, below, refs, sources, taps_ref, laid, windows, first_row, after=(), then=None):
     planes = taps_ref.shape[0] // plan.tap_groups
 
     def add(name):
         totals = [Total(ref, source, planes) for ref, source in zip(refs, sources)]
-        view = shifts.view(first_row[name])
+        shifts = Shifts(jnp.concatenate(windows[name], axis=0), plan.ambit, first_row[name], *laid)
         for part in (name, *after):
-            plan.add(part, totals, taps_ref, view)
+            plan.add(part, totals, taps_ref, shifts)
         for total in totals:
             total.finish()
         if then is not None:
@@ -313,10 +300,10 @@
 ):
     even = lax.axis_index("tile") % 2 == 0
     own, pair = own_ref[...], pair_ref[: plan.rows]
-    window = jnp.concatenate([jnp.where(even, own, pair), jnp.where(even, pair, own)], axis=0)
-    shifts = Shifts(window, plan.ambit, 0, main_ref, strip_ref)
+    windows = {"upper": [pair, own], "lower": [own, pair]}
     refs, sources = (main_total_ref, strip_total_ref), (main_in_ref, strip_in_ref)
-    add_side(plan, even, refs, sources, taps_ref, shifts, {"upper": RIM, "lower": plan.lead})
+    first_row = {"upper": RIM, "lower": plan.lead}
+    add_side(plan, even, refs, sources, taps_ref, (main_ref, strip_ref), windows, first_row)
 
 
 def resist_kernel(
@@ -358,10 +345,11 @@
     even = tile % 2 == 0
     pair, other = pair_ref[...], other_ref[...]
     above, below = jnp.where(even, other, pair), jnp.where(even, pair, other)
-    window = jnp.concatenate(
-        [far_rows(True), above[:rows], own_ref[...], below[:rows], far_rows(False)], axis=0
-    )
-    shifts = Shifts(window, ambit, 0, main_ref, strip_ref)
+    far_above, far_below, own = far_rows(True), far_rows(False), own_ref[...]
+    windows = {
+        "upper": [far_above, other[:rows], own, pair[:rows], far_below],
+        "lower": [far_above, pair[:rows], own, other[:rows], far_below],
+    }
     first_row = {"upper": 0, "lower": 0}
     refs, sources = (main_total_ref, strip_total_ref), (main_in_ref, strip_in_ref)
     weight = weight_ref[:, :1]
@@ -376,9 +364,9 @@
                 image_ref[row : row + 1, LANES:] = lane_roll_left(half, 16 * (part % 8))
 
     below_is_new = jnp.logical_not(even)
-    add_side(
-        plan, below_is_new, refs, sources, taps_ref, shifts, first_row, after=("top", "bottom"), then=write_image
-    )
+    laid = main_ref, strip_ref
+    after = "top", "bottom"
+    add_side(plan, below_is_new, refs, sources, taps_ref, laid, windows, first_row, after, write_image)
 
     image = image_ref[...]
     row_id = lax.broadcasted_iota(jnp.int32, image.shape, 0)
@@ -448,6 +436,17 @@
     wide_rows = jax.ShapeDtypeStruct((rows, 2 * LANES), jnp.float32)
     sent = jax.ShapeDtypeStruct((rows + RIM, 2 * LANES), jnp.float32)
     across = swapped(across, "kern", 0)
+    taps, weight = pl.pallas_call(
+        functools.partial(taps_kernel, plan),
+        out_shape=(
+            jax.ShapeDtypeStruct((plan.tap_groups * planes, GROUP * ambit), jnp.bfloat16),
+            jax.ShapeDtypeStruct((planes, LANES), jnp.float32),
+        ),
+        in_specs=[vmem] * 3,
+        out_specs=(vmem,) * 2,
+        compiler_params=limit,
+        name="taps",
+    )(kernels, socs_weights, turned)
     window, wide, for_pair, for_other = pl.pallas_call(
         functools.partial(rim_kernel, kern_count, plan.lead),
         out_shape=(wide_rows, wide_rows, sent, sent),
@@ -455,23 +454,18 @@
         out_specs=(vmem,) * 4,
         compiler_params=limit,
         name="rims",
-    )(turned, mask, quencher, beside, across)
+    )(taps, mask, quencher, beside, across)
     pair = swapped(for_pair, "tile", 0)
     other = swapped(for_other, "tile", 1)
-    taps, *totals, weight = pl.pallas_call(
+    totals = pl.pallas_call(
         functools.partial(own_rows_kernel, plan),
-        out_shape=(
-            jax.ShapeDtypeStruct((plan.tap_groups * planes, GROUP * ambit), jnp.bfloat16),
-            main_total,
-            strip_total,
-            jax.ShapeDtypeStruct((planes, LANES), jnp.float32),
-        ),
-        in_specs=[vmem] * 4,
-        out_specs=(vmem,) * 4,
+        out_shape=(main_total, strip_total),
+        in_specs=[vmem] * 2,
+        out_specs=(vmem,) * 2,
         scratch_shapes=[pltpu.VMEM((rows * ambit, LANES), jnp.bfloat16)] * 2,
         compiler_params=limit,
         name="own_rows",
-    )(kernels, socs_weights, turned, window)
+    )(window, taps)
     totals = pl.pallas_call(
         functools.partial(pair_rows_kernel, plan),
         out_shape=(main_total, strip_total),

time: 19.7 us -> 19.4 us (0.985)
  Pallas kernels: 6.94 us -> 6.58 us
    pallas_call x1, Pallas kernels: 1.48 us -> 1.21 us  [on_device(): pl.pallas_call(functools.partial(pair_rows_kernel, plan), out_shape=(main...]
    pallas_call x1, Pallas kernels: 3.48 us -> 3.25 us  [on_device(): pl.pallas_call(functools.partial(resist_kernel, plan, kern_count, tile_co...]
    pallas_call x1 -> x2, Pallas kernels: 1.85 us -> 1.99 us  [the longest x1 1.48 us: on_device(): pl.pallas_call(functools.partial(own_rows_kernel, plan), out_shape=(main_...]
  transfers between devices with their start and end apart: 7 -> 7, of which waited for: 2 -> 2; matrix products, arithmetic and copies ran while one was open for 0% -> 0% of each run, Pallas kernels for 18% -> 17%
where the time goes in v7:
time: 19.4 us; the launch traced here: 19.3 us
  starting transfers between devices  10.2 us (53%)
  Pallas kernels  6.58 us (34%)
  waiting for transfers between devices  1.72 us (9%)
  between operations  0.76 us (4%)
    ppermute x7, starting transfers between devices, swapped(): lax.ppermute(value, axis, pairs + [(high, low) for low, high in pairs])  10.2 us
    pallas_call x1, Pallas kernels, on_device(): pl.pallas_call(functools.partial(resist_kernel, plan, kern_count, tile_co...  3.25 us
    ppermute x7, waiting for transfers between devices, swapped(): lax.ppermute(value, axis, pairs + [(high, low) for low, high in pairs])  1.72 us
    pallas_call x1, Pallas kernels, on_device(): pl.pallas_call(functools.partial(own_rows_kernel, plan), out_shape=(main_...  1.48 us
    pallas_call x1, Pallas kernels, on_device(): pl.pallas_call(functools.partial(pair_rows_kernel, plan), out_shape=(main...  1.21 us
    pallas_call x1, Pallas kernels, on_device(): pl.pallas_call(functools.partial(taps_kernel, plan), out_shape=(jax.Shape...  0.52 us
  transfers between devices with their start and end apart: 7, of which 2 were waited for; matrix products, arithmetic and copies ran while one was open for 0% of the time, Pallas kernels for 17%

profile of v7, /device:TPU:4, one launch (start us, length us, event | category | flops | bytes accessed | tf_op | source)
XLA Modules:
  0.0 19.3 jit_solution(8278803543643868802)
XLA Ops:
  0.6 0.0 copy-start.2
  0.6 0.0 copy-start.1
  0.7 0.0 copy-start
  0.7 0.0 copy-start.3
  0.7 1.6 %collective-permute-start.1 = (f32[32,128]{1,0:T(8,128)}, f32[32,128]{1,0:T(8,128)S(1)}, u32[]{:S(2)}, u32[]{:S(2)}) collective-permute-start(f32[32,128]{1,0:T(8,128)} %quencher_ref.1), channel_id=1, source_target_pairs={{0,16},{8,24},{16,0},{24,8},{1,17},{9,25},{17,1},{25,9},{2,18},{10... | collective-permute-start | bytes 49160 | tf_op jit(solution)/shard_map/ppermute | solution.py:74
  2.2 0.0 collective-permute-start
  2.2 0.7 %collective-permute-start.5 = (s32[32,512]{1,0:T(8,128)}, s32[32,512]{1,0:T(8,128)S(1)}, u32[]{:S(2)}, u32[]{:S(2)}) collective-permute-start(s32[32,512]{1,0:T(8,128)} %mask_ref.1), channel_id=1, source_target_pairs={{2,4},{3,5},{4,2},{5,3},{10,12},{11,13},{12,10},{13,11},{18,20},{1... | collective-permute-start | bytes 196616 | tf_op jit(solution)/shard_map/ppermute | solution.py:74
  2.9 4.5 %collective-permute-start.6 = (s32[32,512]{1,0:T(8,128)}, s32[32,512]{1,0:T(8,128)S(1)}, u32[]{:S(2)}, u32[]{:S(2)}) collective-permute-start(s32[32,512]{1,0:T(8,128)} %mask_ref.1), channel_id=1, source_target_pairs={{0,2},{1,3},{4,6},{5,7},{2,0},{3,1},{6,4},{7,5},{8,10},{9,11},{12,... | collective-permute-start | bytes 196616 | tf_op jit(solution)/shard_map/ppermute | solution.py:74
  7.4 0.0 collective-permute-done.1
  7.4 0.0 collective-permute-start.2
  7.4 0.0 copy-done
  7.4 0.0 copy-done.3
  7.4 0.5 %taps.1 = (bf16[768,256]{1,0:T(8,128)(2,1)S(1)}, f32[48,128]{1,0:T(8,128)S(1)}) custom-call(bf16[24,2,64,64]{3,2,1,0:T(8,128)(2,1)S(1)} %copy-done, f32[24]{0:T(128)S(1)} %copy-done.3, bf16[256,256]{1,0:T(8,128)(2,1)S(1)} %turned.1.turned_ref), custom_call_target="tpu_custom_call" | custom-call | tf_op jit(solution)/shard_map/taps/pallas_call | solution.py:439
  7.9 0.0 collective-permute-done.beside_ref
  7.9 0.6 %collective-permute-done.2.across_ref = f32[32,128]{1,0:T(8,128)S(1)} collective-permute-done((f32[32,128]{1,0:T(8,128)S(1)}, f32[32,128]{1,0:T(8,128)S(1)}, u32[]{:S(2)}, u32[]{:S(2)}) %collective-permute-start.2) | collective-permute-done | bytes 16416 | tf_op jit(solution)/shard_map/ppermute | solution.py:74
  8.5 0.0 copy-done.2
  8.5 0.0 copy-done.1
  8.5 0.1 rims.1
  8.7 0.6 %collective-permute-start.4 = (f32[40,256]{1,0:T(8,128)S(1)}, f32[40,256]{1,0:T(8,128)S(1)}, u32[]{:S(2)}, u32[]{:S(2)}) collective-permute-start(f32[40,256]{1,0:T(8,128)S(1)} %get-tuple-element.16), channel_id=1, source_target_pairs={{0,1},{2,3},{4,5},{6,7},{1,0},{3,2},{5,4},{7,6},{8,9},{10,11},{12,... | collective-permute-start | bytes 122888 | tf_op jit(solution)/shard_map/ppermute | solution.py:74
  9.2 2.9 %collective-permute-start.3 = (f32[40,256]{1,0:T(8,128)S(1)}, f32[40,256]{1,0:T(8,128)S(1)}, u32[]{:S(2)}, u32[]{:S(2)}) collective-permute-start(f32[40,256]{1,0:T(8,128)S(1)} %get-tuple-element.15), channel_id=1, source_target_pairs={{1,2},{3,4},{5,6},{2,1},{4,3},{6,5},{9,10},{11,12},{13,14},{10,9},... | collective-permute-start | bytes 122888 | tf_op jit(solution)/shard_map/ppermute | solution.py:74
  12.2 1.5 %own_rows.1 = (f32[576,512]{1,0:T(8,128)S(1)}, f32[144,256]{1,0:T(8,128)S(1)}) custom-call(f32[32,256]{1,0:T(8,128)S(1)} %get-tuple-element.14.window_ref.own_ref, bf16[768,256]{1,0:T(8,128)(2,1)S(1)} %get-tuple-element.13._.taps_ref), custom_call_target="tpu_custom_call" | custom-call | tf_op jit(solution)/shard_map/own_rows/pallas_call | solution.py:460
  13.7 0.0 collective-permute-done.4.pair_ref
  13.7 1.2 %pair_rows.1 = (f32[576,512]{1,0:T(8,128)S(1)}, f32[144,256]{1,0:T(8,128)S(1)}) custom-call(f32[32,256]{1,0:T(8,128)S(1)} %get-tuple-element.14.window_ref.own_ref, f32[40,256]{1,0:T(8,128)S(1)} %collective-permute-done.4.pair_ref, bf16[768,256]{1,0:T(8,128)(2,1)S(1)} %get-tuple-element.13._.taps_ref, f32[576,512]{1,0:T(8,128)S(1)} %get-tuple-element.18.main_in_ref, ...), custom_call_target="tpu_custom_call" | custom-call | tf_op jit(solution)/shard_map/pair_rows/pallas_call | solution.py:469
  14.9 0.0 collective-permute-done.5.far_other_ref
  14.9 0.0 collective-permute-done.6.far_pair_ref
  14.9 1.1 %collective-permute-done.3.other_ref = f32[40,256]{1,0:T(8,128)S(1)} collective-permute-done((f32[40,256]{1,0:T(8,128)S(1)}, f32[40,256]{1,0:T(8,128)S(1)}, u32[]{:S(2)}, u32[]{:S(2)}) %collective-permute-start.3) | collective-permute-done | bytes 40992 | tf_op jit(solution)/shard_map/ppermute | solution.py:74
  16.0 3.2 %image_and_resist.1 = (f32[32,128]{1,0:T(8,128)}, f32[32,128]{1,0:T(8,128)}, f32[32,128]{1,0:T(8,128)}) custom-call(f32[32,256]{1,0:T(8,128)S(1)} %get-tuple-element.14.window_ref.own_ref, f32[40,256]{1,0:T(8,128)S(1)} %collective-permute-done.3.other_ref, f32[40,256]{1,0:T(8,128)S(1)} %collective-permute-done.4.pair_ref, ...), custom_call_target="tpu_custom_call" | custom-call | tf_op jit(solution)/shard_map/image_and_resist/pallas_call | solution.py:479
  (1 shorter events, 0.0 us)
Async XLA Ops:
  0.6 7.9 %copy-start.2 = (f32[32,128]{1,0:T(8,128)S(1)}, f32[32,128]{1,0:T(8,128)}, u32[]{:S(2)}) copy-start(f32[32,128]{1,0:T(8,128)} %quencher_ref.1) | copy-start | bytes 49156
  0.6 7.9 %copy-start.1 = (s32[32,512]{1,0:T(8,128)S(1)}, s32[32,512]{1,0:T(8,128)}, u32[]{:S(2)}) copy-start(s32[32,512]{1,0:T(8,128)} %mask_ref.1) | copy-start | bytes 196612
  0.7 6.7 %copy-start = (bf16[24,2,64,64]{3,2,1,0:T(8,128)(2,1)S(1)}, bf16[24,2,64,64]{3,2,1,0:T(8,128)(2,1)}, u32[]{:S(2)}) copy-start(bf16[24,2,64,64]{3,2,1,0:T(8,128)(2,1)} %kernels_ref.1) | copy-start | bytes 1179652
  0.7 6.7 %copy-start.3 = (f32[24]{0:T(128)S(1)}, f32[24]{0:T(128)}, u32[]{:S(2)}) copy-start(f32[24]{0:T(128)} %weights_ref.1) | copy-start | bytes 292
  0.7 6.7 %collective-permute-start.1 = (f32[32,128]{1,0:T(8,128)}, f32[32,128]{1,0:T(8,128)S(1)}, u32[]{:S(2)}, u32[]{:S(2)}) collective-permute-start(f32[32,128]{1,0:T(8,128)} %quencher_ref.1), channel_id=1, source_target_pairs={{0,16},{8,24},{16,0},{24,8},{1,17},{9,25},{17,1},{25,9},{2,18},{10... | collective-permute-start | bytes 49160 | tf_op jit(solution)/shard_map/ppermute | solution.py:74
  2.2 5.7 %collective-permute-start = (f32[32,128]{1,0:T(8,128)}, f32[32,128]{1,0:T(8,128)S(1)}, u32[]{:S(2)}, u32[]{:S(2)}) collective-permute-start(f32[32,128]{1,0:T(8,128)} %quencher_ref.1), channel_id=1, source_target_pairs={{0,8},{16,24},{8,0},{24,16},{1,9},{17,25},{9,1},{25,17},{2,10},{18... | collective-permute-start | bytes 49160 | tf_op jit(solution)/shard_map/ppermute | solution.py:74
  2.2 12.7 %collective-permute-start.5 = (s32[32,512]{1,0:T(8,128)}, s32[32,512]{1,0:T(8,128)S(1)}, u32[]{:S(2)}, u32[]{:S(2)}) collective-permute-start(s32[32,512]{1,0:T(8,128)} %mask_ref.1), channel_id=1, source_target_pairs={{2,4},{3,5},{4,2},{5,3},{10,12},{11,13},{12,10},{13,11},{18,20},{1... | collective-permute-start | bytes 196616 | tf_op jit(solution)/shard_map/ppermute | solution.py:74
  2.9 12.0 %collective-permute-start.6 = (s32[32,512]{1,0:T(8,128)}, s32[32,512]{1,0:T(8,128)S(1)}, u32[]{:S(2)}, u32[]{:S(2)}) collective-permute-start(s32[32,512]{1,0:T(8,128)} %mask_ref.1), channel_id=1, source_target_pairs={{0,2},{1,3},{4,6},{5,7},{2,0},{3,1},{6,4},{7,5},{8,10},{9,11},{12,... | collective-permute-start | bytes 196616 | tf_op jit(solution)/shard_map/ppermute | solution.py:74
  7.4 1.2 %collective-permute-start.2 = (f32[32,128]{1,0:T(8,128)S(1)}, f32[32,128]{1,0:T(8,128)S(1)}, u32[]{:S(2)}, u32[]{:S(2)}) collective-permute-start(f32[32,128]{1,0:T(8,128)S(1)} %collective-permute-done.1), channel_id=1, source_target_pairs={{0,8},{16,24},{8,0},{24,16},{1,9},{17,25},{9,1},{25,17},{2,10},{18... | collective-permute-start | bytes 49160 | tf_op jit(solution)/shard_map/ppermute | solution.py:74
  8.7 5.0 %collective-permute-start.4 = (f32[40,256]{1,0:T(8,128)S(1)}, f32[40,256]{1,0:T(8,128)S(1)}, u32[]{:S(2)}, u32[]{:S(2)}) collective-permute-start(f32[40,256]{1,0:T(8,128)S(1)} %get-tuple-element.16), channel_id=1, source_target_pairs={{0,1},{2,3},{4,5},{6,7},{1,0},{3,2},{5,4},{7,6},{8,9},{10,11},{12,... | collective-permute-start | bytes 122888 | tf_op jit(solution)/shard_map/ppermute | solution.py:74
  9.2 6.8 %collective-permute-start.3 = (f32[40,256]{1,0:T(8,128)S(1)}, f32[40,256]{1,0:T(8,128)S(1)}, u32[]{:S(2)}, u32[]{:S(2)}) collective-permute-start(f32[40,256]{1,0:T(8,128)S(1)} %get-tuple-element.15), channel_id=1, source_target_pairs={{1,2},{3,4},{5,6},{2,1},{4,3},{6,5},{9,10},{11,12},{13,14},{10,9},... | collective-permute-start | bytes 122888 | tf_op jit(solution)/shard_map/ppermute | solution.py:74

commit v8 on v7

--- a/solution.py
+++ b/solution.py
@@ -269,13 +269,29 @@
             image_ref[row : row + 1, :LANES] = summed[:, LANES * part : LANES * (part + 1)]
 
 
-def add_side(plan, below, refs, sources, taps_ref, laid, windows, first_row, after=(), then=None):
+def far_rows(plan, far_pair_ref, far_other_ref, above_tile):
+    kern, tile = lax.axis_index("kern"), lax.axis_index("tile")
+    kern_count = far_pair_ref.shape[1] // LANES
+    place = slice(plan.rows - RIM, plan.rows) if above_tile else slice(RIM)
+    blocks = [three_blocks(ref, place, kern, kern_count) for ref in (far_pair_ref, far_other_ref)]
+    with_pair = ((tile // 2) % 2 == 1) == above_tile
+    chosen = jnp.where(with_pair, blocks[0], blocks[1])
+    return lane_roll_left(chosen, LANES - plan.lead)[:, : 2 * LANES]
+
+
+def add_side(plan, below, refs, sources, taps_ref, laid, own, rows, far_refs, then=None):
     planes = taps_ref.shape[0] // plan.tap_groups
+    rest = jnp.zeros((RIM, 2 * LANES), jnp.float32)
 
     def add(name):
         totals = [Total(ref, source, planes) for ref, source in zip(refs, sources)]
-        shifts = Shifts(jnp.concatenate(windows[name], axis=0), plan.ambit, first_row[name], *laid)
-        for part in (name, *after):
+        far = far_rows(plan, *far_refs, name == "upper")
+        if name == "upper":
+            window, first_row, parts = [far, rows, own, rest], 0, ("upper", "top")
+        else:
+            window, first_row, parts = [rest, own, rows, far], plan.lead - RIM, ("lower", "bottom")
+        shifts = Shifts(jnp.concatenate(window, axis=0), plan.ambit, first_row, *laid)
+        for part in parts:
             plan.add(part, totals, taps_ref, shifts)
         for total in totals:
             total.finish()
@@ -290,6 +306,8 @@
     plan,
     own_ref,
     pair_ref,
+    far_other_ref,
+    far_pair_ref,
     taps_ref,
     main_in_ref,
     strip_in_ref,
@@ -300,10 +318,9 @@
 ):
     even = lax.axis_index("tile") % 2 == 0
     own, pair = own_ref[...], pair_ref[: plan.rows]
-    windows = {"upper": [pair, own], "lower": [own, pair]}
     refs, sources = (main_total_ref, strip_total_ref), (main_in_ref, strip_in_ref)
-    first_row = {"upper": RIM, "lower": plan.lead}
-    add_side(plan, even, refs, sources, taps_ref, (main_ref, strip_ref), windows, first_row)
+    far_refs = far_pair_ref, far_other_ref
+    add_side(plan, even, refs, sources, taps_ref, (main_ref, strip_ref), own, pair, far_refs)
 
 
 def resist_kernel(
@@ -313,8 +330,8 @@
     own_ref,
     other_ref,
     pair_ref,
+    far_pair_ref,
     far_other_ref,
-    far_pair_ref,
     wide_ref,
     taps_ref,
     main_in_ref,
@@ -335,22 +352,9 @@
     rows, ambit = plan.rows, plan.ambit
     planes = taps_ref.shape[0] // plan.tap_groups
 
-    def far_rows(above_tile):
-        place = slice(rows - RIM, rows) if above_tile else slice(RIM)
-        blocks = [three_blocks(ref, place, kern, kern_count) for ref in (far_pair_ref, far_other_ref)]
-        with_pair = ((tile // 2) % 2 == 1) == above_tile
-        chosen = jnp.where(with_pair, blocks[0], blocks[1])
-        return lane_roll_left(chosen, LANES - plan.lead)[:, : 2 * LANES]
-
     even = tile % 2 == 0
     pair, other = pair_ref[...], other_ref[...]
     above, below = jnp.where(even, other, pair), jnp.where(even, pair, other)
-    far_above, far_below, own = far_rows(True), far_rows(False), own_ref[...]
-    windows = {
-        "upper": [far_above, other[:rows], own, pair[:rows], far_below],
-        "lower": [far_above, pair[:rows], own, other[:rows], far_below],
-    }
-    first_row = {"upper": 0, "lower": 0}
     refs, sources = (main_total_ref, strip_total_ref), (main_in_ref, strip_in_ref)
     weight = weight_ref[:, :1]
 
@@ -364,9 +368,10 @@
                 image_ref[row : row + 1, LANES:] = lane_roll_left(half, 16 * (part % 8))
 
     below_is_new = jnp.logical_not(even)
-    laid = main_ref, strip_ref
-    after = "top", "bottom"
-    add_side(plan, below_is_new, refs, sources, taps_ref, laid, windows, first_row, after, write_image)
+    laid, far_refs = (main_ref, strip_ref), (far_pair_ref, far_other_ref)
+    add_side(
+        plan, below_is_new, refs, sources, taps_ref, laid, own_ref[...], other[:rows], far_refs, write_image
+    )
 
     image = image_ref[...]
     row_id = lax.broadcasted_iota(jnp.int32, image.shape, 0)
@@ -469,19 +474,19 @@
     totals = pl.pallas_call(
         functools.partial(pair_rows_kernel, plan),
         out_shape=(main_total, strip_total),
-        in_specs=[vmem] * 5,
+        in_specs=[vmem] * 7,
         out_specs=(vmem,) * 2,
-        scratch_shapes=[pltpu.VMEM((2 * rows * ambit, LANES), jnp.bfloat16)] * 2,
+        scratch_shapes=[pltpu.VMEM(((2 * rows + 2 * RIM) * ambit, LANES), jnp.bfloat16)] * 2,
         compiler_params=limit,
         name="pair_rows",
-    )(window, pair, taps, *totals)
+    )(window, pair, far_other, far_pair, taps, *totals)
     block = jax.ShapeDtypeStruct((rows, LANES), jnp.float32)
     return pl.pallas_call(
         functools.partial(resist_kernel, plan, kern_count, tile_count),
         out_shape=(block, block, block),
         in_specs=[vmem] * 10,
         out_specs=(pl.BlockSpec(memory_space=pl.ANY),) * 3,
-        scratch_shapes=[pltpu.VMEM((plan.span * ambit, LANES), jnp.bfloat16)] * 2
+        scratch_shapes=[pltpu.VMEM(((2 * rows + 2 * RIM) * ambit, LANES), jnp.bfloat16)] * 2
         + [
             pltpu.VMEM(main_total.shape, jnp.float32),
             pltpu.VMEM(strip_total.shape, jnp.float32),
@@ -491,7 +496,7 @@
         ],
         compiler_params=limit,
         name="image_and_resist",
-    )(window, other, pair, far_other, far_pair, wide, taps, *totals, weight)
+    )(window, other, pair, far_pair, far_other, wide, taps, *totals, weight)
 
 
 def solution(mesh):

time: 19.4 us -> 19.3 us (level)
  waiting for transfers between devices: 1.72 us -> 1.51 us
    ppermute x7, waiting for transfers between devices: 1.72 us -> 1.51 us  [swapped(): lax.ppermute(value, axis, pairs + [(high, low) for low, high in pairs])]
    pallas_call x1, Pallas kernels: 1.21 us -> 1.42 us  [on_device(): pl.pallas_call(functools.partial(pair_rows_kernel, plan), out_shape=(main...]
  transfers between devices with their start and end apart: 7 -> 7, of which waited for: 2 -> 2; matrix products, arithmetic and copies ran while one was open for 0% -> 0% of each run, Pallas kernels for 17% -> 19%
where the time goes in v8:
time: 19.3 us; the launch traced here: 19.1 us
  starting transfers between devices  10.2 us (53%)
  Pallas kernels  6.64 us (34%)
  waiting for transfers between devices  1.51 us (8%)
  between operations  0.76 us (4%)
    ppermute x7, starting transfers between devices, swapped(): lax.ppermute(value, axis, pairs + [(high, low) for low, high in pairs])  10.2 us
    pallas_call x1, Pallas kernels, on_device(): pl.pallas_call(functools.partial(resist_kernel, plan, kern_count, tile_co...  3.1 us
    ppermute x7, waiting for transfers between devices, swapped(): lax.ppermute(value, axis, pairs + [(high, low) for low, high in pairs])  1.51 us
    pallas_call x1, Pallas kernels, on_device(): pl.pallas_call(functools.partial(own_rows_kernel, plan), out_shape=(main_...  1.48 us
    pallas_call x1, Pallas kernels, on_device(): pl.pallas_call(functools.partial(pair_rows_kernel, plan), out_shape=(main...  1.42 us
    pallas_call x1, Pallas kernels, on_device(): pl.pallas_call(functools.partial(taps_kernel, plan), out_shape=(jax.Shape...  0.52 us
  transfers between devices with their start and end apart: 7, of which 2 were waited for; matrix products, arithmetic and copies ran while one was open for 0% of the time, Pallas kernels for 19%

profile of v8, /device:TPU:4, one launch (start us, length us, event | category | flops | bytes accessed | tf_op | source)
XLA Modules:
  0.0 19.1 jit_solution(9482775672363728736)
XLA Ops:
  0.6 0.0 copy-start.2
  0.6 0.0 copy-start.1
  0.7 0.0 copy-start.3
  0.7 0.0 copy-start
  0.7 1.6 %collective-permute-start.1 = (f32[32,128]{1,0:T(8,128)}, f32[32,128]{1,0:T(8,128)S(1)}, u32[]{:S(2)}, u32[]{:S(2)}) collective-permute-start(f32[32,128]{1,0:T(8,128)} %quencher_ref.1), channel_id=1, source_target_pairs={{0,16},{8,24},{16,0},{24,8},{1,17},{9,25},{17,1},{25,9},{2,18},{10... | collective-permute-start | bytes 49160 | tf_op jit(solution)/shard_map/ppermute | solution.py:74
  2.2 0.0 collective-permute-start
  2.2 0.7 %collective-permute-start.6 = (s32[32,512]{1,0:T(8,128)}, s32[32,512]{1,0:T(8,128)S(1)}, u32[]{:S(2)}, u32[]{:S(2)}) collective-permute-start(s32[32,512]{1,0:T(8,128)} %mask_ref.1), channel_id=1, source_target_pairs={{2,4},{3,5},{4,2},{5,3},{10,12},{11,13},{12,10},{13,11},{18,20},{1... | collective-permute-start | bytes 196616 | tf_op jit(solution)/shard_map/ppermute | solution.py:74
  2.9 4.5 %collective-permute-start.5 = (s32[32,512]{1,0:T(8,128)}, s32[32,512]{1,0:T(8,128)S(1)}, u32[]{:S(2)}, u32[]{:S(2)}) collective-permute-start(s32[32,512]{1,0:T(8,128)} %mask_ref.1), channel_id=1, source_target_pairs={{0,2},{1,3},{4,6},{5,7},{2,0},{3,1},{6,4},{7,5},{8,10},{9,11},{12,... | collective-permute-start | bytes 196616 | tf_op jit(solution)/shard_map/ppermute | solution.py:74
  7.4 0.0 collective-permute-done.1
  7.4 0.0 collective-permute-start.2
  7.4 0.0 copy-done.3
  7.4 0.0 copy-done
  7.4 0.5 %taps.1 = (bf16[768,256]{1,0:T(8,128)(2,1)S(1)}, f32[48,128]{1,0:T(8,128)S(1)}) custom-call(bf16[24,2,64,64]{3,2,1,0:T(8,128)(2,1)S(1)} %copy-done, f32[24]{0:T(128)S(1)} %copy-done.3, bf16[256,256]{1,0:T(8,128)(2,1)S(1)} %turned.1.turned_ref), custom_call_target="tpu_custom_call" | custom-call | tf_op jit(solution)/shard_map/taps/pallas_call | solution.py:444
  7.9 0.0 collective-permute-done.beside_ref
  7.9 0.6 %collective-permute-done.2.across_ref = f32[32,128]{1,0:T(8,128)S(1)} collective-permute-done((f32[32,128]{1,0:T(8,128)S(1)}, f32[32,128]{1,0:T(8,128)S(1)}, u32[]{:S(2)}, u32[]{:S(2)}) %collective-permute-start.2) | collective-permute-done | bytes 16416 | tf_op jit(solution)/shard_map/ppermute | solution.py:74
  8.5 0.0 copy-done.2
  8.5 0.0 copy-done.1
  8.5 0.1 rims.1
  8.7 0.6 %collective-permute-start.4 = (f32[40,256]{1,0:T(8,128)S(1)}, f32[40,256]{1,0:T(8,128)S(1)}, u32[]{:S(2)}, u32[]{:S(2)}) collective-permute-start(f32[40,256]{1,0:T(8,128)S(1)} %get-tuple-element.16), channel_id=1, source_target_pairs={{0,1},{2,3},{4,5},{6,7},{1,0},{3,2},{5,4},{7,6},{8,9},{10,11},{12,... | collective-permute-start | bytes 122888 | tf_op jit(solution)/shard_map/ppermute | solution.py:74
  9.2 2.9 %collective-permute-start.3 = (f32[40,256]{1,0:T(8,128)S(1)}, f32[40,256]{1,0:T(8,128)S(1)}, u32[]{:S(2)}, u32[]{:S(2)}) collective-permute-start(f32[40,256]{1,0:T(8,128)S(1)} %get-tuple-element.15), channel_id=1, source_target_pairs={{1,2},{3,4},{5,6},{2,1},{4,3},{6,5},{9,10},{11,12},{13,14},{10,9},... | collective-permute-start | bytes 122888 | tf_op jit(solution)/shard_map/ppermute | solution.py:74
  12.2 1.5 %own_rows.1 = (f32[576,512]{1,0:T(8,128)S(1)}, f32[144,256]{1,0:T(8,128)S(1)}) custom-call(f32[32,256]{1,0:T(8,128)S(1)} %get-tuple-element.14.window_ref.own_ref, bf16[768,256]{1,0:T(8,128)(2,1)S(1)} %get-tuple-element.13._.taps_ref), custom_call_target="tpu_custom_call" | custom-call | tf_op jit(solution)/shard_map/own_rows/pallas_call | solution.py:465
  13.7 0.0 collective-permute-done.6.far_other_ref
  13.7 0.0 collective-permute-done.5.far_pair_ref
  13.7 0.0 collective-permute-done.4.pair_ref
  13.7 1.4 %pair_rows.1 = (f32[576,512]{1,0:T(8,128)S(1)}, f32[144,256]{1,0:T(8,128)S(1)}) custom-call(f32[32,256]{1,0:T(8,128)S(1)} %get-tuple-element.14.window_ref.own_ref, f32[40,256]{1,0:T(8,128)S(1)} %collective-permute-done.4.pair_ref, s32[32,512]{1,0:T(8,128)S(1)} %collective-permute-done.6.far_other_ref, s32[32,512]{1,0:T(8,128)S(1)} %collective-permute-done.5.far_pair_ref, ...), custom_call_target="tpu_custom_call" | custom-call | tf_op jit(solution)/shard_map/pair_rows/pallas_call | solution.py:474
  15.1 0.9 %collective-permute-done.3.other_ref = f32[40,256]{1,0:T(8,128)S(1)} collective-permute-done((f32[40,256]{1,0:T(8,128)S(1)}, f32[40,256]{1,0:T(8,128)S(1)}, u32[]{:S(2)}, u32[]{:S(2)}) %collective-permute-start.3) | collective-permute-done | bytes 40992 | tf_op jit(solution)/shard_map/ppermute | solution.py:74
  16.0 3.1 %image_and_resist.1 = (f32[32,128]{1,0:T(8,128)}, f32[32,128]{1,0:T(8,128)}, f32[32,128]{1,0:T(8,128)}) custom-call(f32[32,256]{1,0:T(8,128)S(1)} %get-tuple-element.14.window_ref.own_ref, f32[40,256]{1,0:T(8,128)S(1)} %collective-permute-done.3.other_ref, f32[40,256]{1,0:T(8,128)S(1)} %collective-permute-done.4.pair_ref, ...), custom_call_target="tpu_custom_call" | custom-call | tf_op jit(solution)/shard_map/image_and_resist/pallas_call | solution.py:484
  (1 shorter events, 0.0 us)
Async XLA Ops:
  0.6 7.9 %copy-start.2 = (f32[32,128]{1,0:T(8,128)S(1)}, f32[32,128]{1,0:T(8,128)}, u32[]{:S(2)}) copy-start(f32[32,128]{1,0:T(8,128)} %quencher_ref.1) | copy-start | bytes 49156
  0.6 7.9 %copy-start.1 = (s32[32,512]{1,0:T(8,128)S(1)}, s32[32,512]{1,0:T(8,128)}, u32[]{:S(2)}) copy-start(s32[32,512]{1,0:T(8,128)} %mask_ref.1) | copy-start | bytes 196612
  0.7 6.7 %copy-start.3 = (f32[24]{0:T(128)S(1)}, f32[24]{0:T(128)}, u32[]{:S(2)}) copy-start(f32[24]{0:T(128)} %weights_ref.1) | copy-start | bytes 292
  0.7 6.7 %copy-start = (bf16[24,2,64,64]{3,2,1,0:T(8,128)(2,1)S(1)}, bf16[24,2,64,64]{3,2,1,0:T(8,128)(2,1)}, u32[]{:S(2)}) copy-start(bf16[24,2,64,64]{3,2,1,0:T(8,128)(2,1)} %kernels_ref.1) | copy-start | bytes 1179652
  0.7 6.7 %collective-permute-start.1 = (f32[32,128]{1,0:T(8,128)}, f32[32,128]{1,0:T(8,128)S(1)}, u32[]{:S(2)}, u32[]{:S(2)}) collective-permute-start(f32[32,128]{1,0:T(8,128)} %quencher_ref.1), channel_id=1, source_target_pairs={{0,16},{8,24},{16,0},{24,8},{1,17},{9,25},{17,1},{25,9},{2,18},{10... | collective-permute-start | bytes 49160 | tf_op jit(solution)/shard_map/ppermute | solution.py:74
  2.2 5.7 %collective-permute-start = (f32[32,128]{1,0:T(8,128)}, f32[32,128]{1,0:T(8,128)S(1)}, u32[]{:S(2)}, u32[]{:S(2)}) collective-permute-start(f32[32,128]{1,0:T(8,128)} %quencher_ref.1), channel_id=1, source_target_pairs={{0,8},{16,24},{8,0},{24,16},{1,9},{17,25},{9,1},{25,17},{2,10},{18... | collective-permute-start | bytes 49160 | tf_op jit(solution)/shard_map/ppermute | solution.py:74
  2.2 11.4 %collective-permute-start.6 = (s32[32,512]{1,0:T(8,128)}, s32[32,512]{1,0:T(8,128)S(1)}, u32[]{:S(2)}, u32[]{:S(2)}) collective-permute-start(s32[32,512]{1,0:T(8,128)} %mask_ref.1), channel_id=1, source_target_pairs={{2,4},{3,5},{4,2},{5,3},{10,12},{11,13},{12,10},{13,11},{18,20},{1... | collective-permute-start | bytes 196616 | tf_op jit(solution)/shard_map/ppermute | solution.py:74
  2.9 10.8 %collective-permute-start.5 = (s32[32,512]{1,0:T(8,128)}, s32[32,512]{1,0:T(8,128)S(1)}, u32[]{:S(2)}, u32[]{:S(2)}) collective-permute-start(s32[32,512]{1,0:T(8,128)} %mask_ref.1), channel_id=1, source_target_pairs={{0,2},{1,3},{4,6},{5,7},{2,0},{3,1},{6,4},{7,5},{8,10},{9,11},{12,... | collective-permute-start | bytes 196616 | tf_op jit(solution)/shard_map/ppermute | solution.py:74
  7.4 1.2 %collective-permute-start.2 = (f32[32,128]{1,0:T(8,128)S(1)}, f32[32,128]{1,0:T(8,128)S(1)}, u32[]{:S(2)}, u32[]{:S(2)}) collective-permute-start(f32[32,128]{1,0:T(8,128)S(1)} %collective-permute-done.1), channel_id=1, source_target_pairs={{0,8},{16,24},{8,0},{24,16},{1,9},{17,25},{9,1},{25,17},{2,10},{18... | collective-permute-start | bytes 49160 | tf_op jit(solution)/shard_map/ppermute | solution.py:74
  8.7 5.0 %collective-permute-start.4 = (f32[40,256]{1,0:T(8,128)S(1)}, f32[40,256]{1,0:T(8,128)S(1)}, u32[]{:S(2)}, u32[]{:S(2)}) collective-permute-start(f32[40,256]{1,0:T(8,128)S(1)} %get-tuple-element.16), channel_id=1, source_target_pairs={{0,1},{2,3},{4,5},{6,7},{1,0},{3,2},{5,4},{7,6},{8,9},{10,11},{12,... | collective-permute-start | bytes 122888 | tf_op jit(solution)/shard_map/ppermute | solution.py:74
  9.2 6.8 %collective-permute-start.3 = (f32[40,256]{1,0:T(8,128)S(1)}, f32[40,256]{1,0:T(8,128)S(1)}, u32[]{:S(2)}, u32[]{:S(2)}) collective-permute-start(f32[40,256]{1,0:T(8,128)S(1)} %get-tuple-element.15), channel_id=1, source_target_pairs={{1,2},{3,4},{5,6},{2,1},{4,3},{6,5},{9,10},{11,12},{13,14},{10,9},... | collective-permute-start | bytes 122888 | tf_op jit(solution)/shard_map/ppermute | solution.py:74

commit v9 on v8

--- a/solution.py
+++ b/solution.py
@@ -279,13 +279,13 @@
     return lane_roll_left(chosen, LANES - plan.lead)[:, : 2 * LANES]
 
 
-def add_side(plan, below, refs, sources, taps_ref, laid, own, rows, far_refs, then=None):
+def add_side(plan, below, refs, sources, taps_ref, laid, own, rows, far_of, then=None):
     planes = taps_ref.shape[0] // plan.tap_groups
     rest = jnp.zeros((RIM, 2 * LANES), jnp.float32)
 
     def add(name):
         totals = [Total(ref, source, planes) for ref, source in zip(refs, sources)]
-        far = far_rows(plan, *far_refs, name == "upper")
+        far = far_of(name)
         if name == "upper":
             window, first_row, parts = [far, rows, own, rest], 0, ("upper", "top")
         else:
@@ -306,21 +306,23 @@
     plan,
     own_ref,
     pair_ref,
+    far_pair_ref,
     far_other_ref,
-    far_pair_ref,
     taps_ref,
     main_in_ref,
     strip_in_ref,
     main_total_ref,
     strip_total_ref,
+    next_far_ref,
     main_ref,
     strip_ref,
 ):
     even = lax.axis_index("tile") % 2 == 0
     own, pair = own_ref[...], pair_ref[: plan.rows]
     refs, sources = (main_total_ref, strip_total_ref), (main_in_ref, strip_in_ref)
-    far_refs = far_pair_ref, far_other_ref
-    add_side(plan, even, refs, sources, taps_ref, (main_ref, strip_ref), own, pair, far_refs)
+    far = {name: far_rows(plan, far_pair_ref, far_other_ref, name == "upper") for name in ("upper", "lower")}
+    next_far_ref[...] = jnp.where(even, far["upper"], far["lower"])
+    add_side(plan, even, refs, sources, taps_ref, (main_ref, strip_ref), own, pair, far.get)
 
 
 def resist_kernel(
@@ -330,8 +332,7 @@
     own_ref,
     other_ref,
     pair_ref,
-    far_pair_ref,
-    far_other_ref,
+    next_far_ref,
     wide_ref,
     taps_ref,
     main_in_ref,
@@ -368,9 +369,9 @@
                 image_ref[row : row + 1, LANES:] = lane_roll_left(half, 16 * (part % 8))
 
     below_is_new = jnp.logical_not(even)
-    laid, far_refs = (main_ref, strip_ref), (far_pair_ref, far_other_ref)
+    laid, next_far = (main_ref, strip_ref), next_far_ref[...]
     add_side(
-        plan, below_is_new, refs, sources, taps_ref, laid, own_ref[...], other[:rows], far_refs, write_image
+        plan, below_is_new, refs, sources, taps_ref, laid, own_ref[...], other[:rows], lambda _: next_far, write_image
     )
 
     image = image_ref[...]
@@ -471,20 +472,20 @@
         compiler_params=limit,
         name="own_rows",
     )(window, taps)
-    totals = pl.pallas_call(
+    *totals, next_far = pl.pallas_call(
         functools.partial(pair_rows_kernel, plan),
-        out_shape=(main_total, strip_total),
+        out_shape=(main_total, strip_total, jax.ShapeDtypeStruct((RIM, 2 * LANES), jnp.float32)),
         in_specs=[vmem] * 7,
-        out_specs=(vmem,) * 2,
+        out_specs=(vmem,) * 3,
         scratch_shapes=[pltpu.VMEM(((2 * rows + 2 * RIM) * ambit, LANES), jnp.bfloat16)] * 2,
         compiler_params=limit,
         name="pair_rows",
-    )(window, pair, far_other, far_pair, taps, *totals)
+    )(window, pair, far_pair, far_other, taps, *totals)
     block = jax.ShapeDtypeStruct((rows, LANES), jnp.float32)
     return pl.pallas_call(
         functools.partial(resist_kernel, plan, kern_count, tile_count),
         out_shape=(block, block, block),
-        in_specs=[vmem] * 10,
+        in_specs=[vmem] * 9,
         out_specs=(pl.BlockSpec(memory_space=pl.ANY),) * 3,
         scratch_shapes=[pltpu.VMEM(((2 * rows + 2 * RIM) * ambit, LANES), jnp.bfloat16)] * 2
         + [
@@ -496,7 +497,7 @@
         ],
         compiler_params=limit,
         name="image_and_resist",
-    )(window, other, pair, far_pair, far_other, wide, taps, *totals, weight)
+    )(window, other, pair, next_far, wide, taps, *totals, weight)
 
 
 def solution(mesh):

time: 19.3 us -> 19.1 us (0.990)
  Pallas kernels: 6.64 us -> 6.43 us
  transfers between devices with their start and end apart: 7 -> 7, of which waited for: 2 -> 2; matrix products, arithmetic and copies ran while one was open for 0% -> 0% of each run, Pallas kernels for 19% -> 18%
where the time goes in v9:
time: 19.1 us; the launch traced here: 19 us
  starting transfers between devices  10.2 us (53%)
  Pallas kernels  6.43 us (34%)
  waiting for transfers between devices  1.59 us (8%)
  between operations  0.76 us (4%)
    ppermute x7, starting transfers between devices, swapped(): lax.ppermute(value, axis, pairs + [(high, low) for low, high in pairs])  10.2 us
    pallas_call x1, Pallas kernels, on_device(): pl.pallas_call(functools.partial(resist_kernel, plan, kern_count, tile_co...  2.97 us
    ppermute x7, waiting for transfers between devices, swapped(): lax.ppermute(value, axis, pairs + [(high, low) for low, high in pairs])  1.59 us
    pallas_call x1, Pallas kernels, on_device(): pl.pallas_call(functools.partial(own_rows_kernel, plan), out_shape=(main_...  1.45 us
    pallas_call x1, Pallas kernels, on_device(): pl.pallas_call(functools.partial(pair_rows_kernel, plan), out_shape=(main...  1.36 us
    pallas_call x1, Pallas kernels, on_device(): pl.pallas_call(functools.partial(taps_kernel, plan), out_shape=(jax.Shape...  0.52 us
  transfers between devices with their start and end apart: 7, of which 2 were waited for; matrix products, arithmetic and copies ran while one was open for 0% of the time, Pallas kernels for 18%

profile of v9, /device:TPU:4, one launch (start us, length us, event | category | flops | bytes accessed | tf_op | source)
XLA Modules:
  0.0 19.0 jit_solution(1259056217999632906)
XLA Ops:
  0.6 0.0 copy-start.2
  0.6 0.0 copy-start.1
  0.7 0.0 copy-start.3
  0.7 0.0 copy-start
  0.7 1.6 %collective-permute-start.1 = (f32[32,128]{1,0:T(8,128)}, f32[32,128]{1,0:T(8,128)S(1)}, u32[]{:S(2)}, u32[]{:S(2)}) collective-permute-start(f32[32,128]{1,0:T(8,128)} %quencher_ref.1), channel_id=1, source_target_pairs={{0,16},{8,24},{16,0},{24,8},{1,17},{9,25},{17,1},{25,9},{2,18},{10... | collective-permute-start | bytes 49160 | tf_op jit(solution)/shard_map/ppermute | solution.py:74
  2.2 0.0 collective-permute-start
  2.2 0.7 %collective-permute-start.6 = (s32[32,512]{1,0:T(8,128)}, s32[32,512]{1,0:T(8,128)S(1)}, u32[]{:S(2)}, u32[]{:S(2)}) collective-permute-start(s32[32,512]{1,0:T(8,128)} %mask_ref.1), channel_id=1, source_target_pairs={{2,4},{3,5},{4,2},{5,3},{10,12},{11,13},{12,10},{13,11},{18,20},{1... | collective-permute-start | bytes 196616 | tf_op jit(solution)/shard_map/ppermute | solution.py:74
  2.9 4.5 %collective-permute-start.5 = (s32[32,512]{1,0:T(8,128)}, s32[32,512]{1,0:T(8,128)S(1)}, u32[]{:S(2)}, u32[]{:S(2)}) collective-permute-start(s32[32,512]{1,0:T(8,128)} %mask_ref.1), channel_id=1, source_target_pairs={{0,2},{1,3},{4,6},{5,7},{2,0},{3,1},{6,4},{7,5},{8,10},{9,11},{12,... | collective-permute-start | bytes 196616 | tf_op jit(solution)/shard_map/ppermute | solution.py:74
  7.4 0.0 collective-permute-done.1
  7.4 0.0 collective-permute-start.2
  7.4 0.0 copy-done.3
  7.4 0.0 copy-done
  7.4 0.5 %taps.1 = (bf16[768,256]{1,0:T(8,128)(2,1)S(1)}, f32[48,128]{1,0:T(8,128)S(1)}) custom-call(bf16[24,2,64,64]{3,2,1,0:T(8,128)(2,1)S(1)} %copy-done, f32[24]{0:T(128)S(1)} %copy-done.3, bf16[256,256]{1,0:T(8,128)(2,1)S(1)} %turned.1.turned_ref), custom_call_target="tpu_custom_call" | custom-call | tf_op jit(solution)/shard_map/taps/pallas_call | solution.py:445
  7.9 0.0 collective-permute-done.beside_ref
  7.9 0.6 %collective-permute-done.2.across_ref = f32[32,128]{1,0:T(8,128)S(1)} collective-permute-done((f32[32,128]{1,0:T(8,128)S(1)}, f32[32,128]{1,0:T(8,128)S(1)}, u32[]{:S(2)}, u32[]{:S(2)}) %collective-permute-start.2) | collective-permute-done | bytes 16416 | tf_op jit(solution)/shard_map/ppermute | solution.py:74
  8.5 0.0 copy-done.2
  8.5 0.0 copy-done.1
  8.5 0.1 rims.1
  8.7 0.6 %collective-permute-start.4 = (f32[40,256]{1,0:T(8,128)S(1)}, f32[40,256]{1,0:T(8,128)S(1)}, u32[]{:S(2)}, u32[]{:S(2)}) collective-permute-start(f32[40,256]{1,0:T(8,128)S(1)} %get-tuple-element.17), channel_id=1, source_target_pairs={{0,1},{2,3},{4,5},{6,7},{1,0},{3,2},{5,4},{7,6},{8,9},{10,11},{12,... | collective-permute-start | bytes 122888 | tf_op jit(solution)/shard_map/ppermute | solution.py:74
  9.2 2.9 %collective-permute-start.3 = (f32[40,256]{1,0:T(8,128)S(1)}, f32[40,256]{1,0:T(8,128)S(1)}, u32[]{:S(2)}, u32[]{:S(2)}) collective-permute-start(f32[40,256]{1,0:T(8,128)S(1)} %get-tuple-element.16), channel_id=1, source_target_pairs={{1,2},{3,4},{5,6},{2,1},{4,3},{6,5},{9,10},{11,12},{13,14},{10,9},... | collective-permute-start | bytes 122888 | tf_op jit(solution)/shard_map/ppermute | solution.py:74
  12.2 1.5 %own_rows.1 = (f32[576,512]{1,0:T(8,128)S(1)}, f32[144,256]{1,0:T(8,128)S(1)}) custom-call(f32[32,256]{1,0:T(8,128)S(1)} %get-tuple-element.15.window_ref.own_ref, bf16[768,256]{1,0:T(8,128)(2,1)S(1)} %get-tuple-element.14._.taps_ref), custom_call_target="tpu_custom_call" | custom-call | tf_op jit(solution)/shard_map/own_rows/pallas_call | solution.py:466
  13.6 0.0 collective-permute-done.6.far_other_ref
  13.6 0.0 collective-permute-done.5.far_pair_ref
  13.6 0.0 collective-permute-done.4.pair_ref
  13.7 1.4 %pair_rows.1 = (f32[576,512]{1,0:T(8,128)S(1)}, f32[144,256]{1,0:T(8,128)S(1)}, f32[8,256]{1,0:T(8,128)S(1)}) custom-call(f32[32,256]{1,0:T(8,128)S(1)} %get-tuple-element.15.window_ref.own_ref, f32[40,256]{1,0:T(8,128)S(1)} %collective-permute-done.4.pair_ref, s32[32,512]{1,0:T(8,128)S(1)} %collective-permute-done.5.far_pair_ref, ...), custom_call_target="tpu_custom_call" | custom-call | tf_op jit(solution)/shard_map/pair_rows/pallas_call | solution.py:475
  15.0 1.0 %collective-permute-done.3.other_ref = f32[40,256]{1,0:T(8,128)S(1)} collective-permute-done((f32[40,256]{1,0:T(8,128)S(1)}, f32[40,256]{1,0:T(8,128)S(1)}, u32[]{:S(2)}, u32[]{:S(2)}) %collective-permute-start.3) | collective-permute-done | bytes 40992 | tf_op jit(solution)/shard_map/ppermute | solution.py:74
  16.0 3.0 %image_and_resist.1 = (f32[32,128]{1,0:T(8,128)}, f32[32,128]{1,0:T(8,128)}, f32[32,128]{1,0:T(8,128)}) custom-call(f32[32,256]{1,0:T(8,128)S(1)} %get-tuple-element.15.window_ref.own_ref, f32[40,256]{1,0:T(8,128)S(1)} %collective-permute-done.3.other_ref, f32[40,256]{1,0:T(8,128)S(1)} %collective-permute-done.4.pair_ref, ...), custom_call_target="tpu_custom_call" | custom-call | tf_op jit(solution)/shard_map/image_and_resist/pallas_call | solution.py:485
  (1 shorter events, 0.0 us)
Async XLA Ops:
  0.6 7.9 %copy-start.2 = (f32[32,128]{1,0:T(8,128)S(1)}, f32[32,128]{1,0:T(8,128)}, u32[]{:S(2)}) copy-start(f32[32,128]{1,0:T(8,128)} %quencher_ref.1) | copy-start | bytes 49156
  0.6 7.9 %copy-start.1 = (s32[32,512]{1,0:T(8,128)S(1)}, s32[32,512]{1,0:T(8,128)}, u32[]{:S(2)}) copy-start(s32[32,512]{1,0:T(8,128)} %mask_ref.1) | copy-start | bytes 196612
  0.7 6.7 %copy-start.3 = (f32[24]{0:T(128)S(1)}, f32[24]{0:T(128)}, u32[]{:S(2)}) copy-start(f32[24]{0:T(128)} %weights_ref.1) | copy-start | bytes 292
  0.7 6.7 %copy-start = (bf16[24,2,64,64]{3,2,1,0:T(8,128)(2,1)S(1)}, bf16[24,2,64,64]{3,2,1,0:T(8,128)(2,1)}, u32[]{:S(2)}) copy-start(bf16[24,2,64,64]{3,2,1,0:T(8,128)(2,1)} %kernels_ref.1) | copy-start | bytes 1179652
  0.7 6.7 %collective-permute-start.1 = (f32[32,128]{1,0:T(8,128)}, f32[32,128]{1,0:T(8,128)S(1)}, u32[]{:S(2)}, u32[]{:S(2)}) collective-permute-start(f32[32,128]{1,0:T(8,128)} %quencher_ref.1), channel_id=1, source_target_pairs={{0,16},{8,24},{16,0},{24,8},{1,17},{9,25},{17,1},{25,9},{2,18},{10... | collective-permute-start | bytes 49160 | tf_op jit(solution)/shard_map/ppermute | solution.py:74
  2.2 5.7 %collective-permute-start = (f32[32,128]{1,0:T(8,128)}, f32[32,128]{1,0:T(8,128)S(1)}, u32[]{:S(2)}, u32[]{:S(2)}) collective-permute-start(f32[32,128]{1,0:T(8,128)} %quencher_ref.1), channel_id=1, source_target_pairs={{0,8},{16,24},{8,0},{24,16},{1,9},{17,25},{9,1},{25,17},{2,10},{18... | collective-permute-start | bytes 49160 | tf_op jit(solution)/shard_map/ppermute | solution.py:74
  2.2 11.4 %collective-permute-start.6 = (s32[32,512]{1,0:T(8,128)}, s32[32,512]{1,0:T(8,128)S(1)}, u32[]{:S(2)}, u32[]{:S(2)}) collective-permute-start(s32[32,512]{1,0:T(8,128)} %mask_ref.1), channel_id=1, source_target_pairs={{2,4},{3,5},{4,2},{5,3},{10,12},{11,13},{12,10},{13,11},{18,20},{1... | collective-permute-start | bytes 196616 | tf_op jit(solution)/shard_map/ppermute | solution.py:74
  2.9 10.7 %collective-permute-start.5 = (s32[32,512]{1,0:T(8,128)}, s32[32,512]{1,0:T(8,128)S(1)}, u32[]{:S(2)}, u32[]{:S(2)}) collective-permute-start(s32[32,512]{1,0:T(8,128)} %mask_ref.1), channel_id=1, source_target_pairs={{0,2},{1,3},{4,6},{5,7},{2,0},{3,1},{6,4},{7,5},{8,10},{9,11},{12,... | collective-permute-start | bytes 196616 | tf_op jit(solution)/shard_map/ppermute | solution.py:74
  7.4 1.2 %collective-permute-start.2 = (f32[32,128]{1,0:T(8,128)S(1)}, f32[32,128]{1,0:T(8,128)S(1)}, u32[]{:S(2)}, u32[]{:S(2)}) collective-permute-start(f32[32,128]{1,0:T(8,128)S(1)} %collective-permute-done.1), channel_id=1, source_target_pairs={{0,8},{16,24},{8,0},{24,16},{1,9},{17,25},{9,1},{25,17},{2,10},{18... | collective-permute-start | bytes 49160 | tf_op jit(solution)/shard_map/ppermute | solution.py:74
  8.7 5.0 %collective-permute-start.4 = (f32[40,256]{1,0:T(8,128)S(1)}, f32[40,256]{1,0:T(8,128)S(1)}, u32[]{:S(2)}, u32[]{:S(2)}) collective-permute-start(f32[40,256]{1,0:T(8,128)S(1)} %get-tuple-element.17), channel_id=1, source_target_pairs={{0,1},{2,3},{4,5},{6,7},{1,0},{3,2},{5,4},{7,6},{8,9},{10,11},{12,... | collective-permute-start | bytes 122888 | tf_op jit(solution)/shard_map/ppermute | solution.py:74
  9.2 6.8 %collective-permute-start.3 = (f32[40,256]{1,0:T(8,128)S(1)}, f32[40,256]{1,0:T(8,128)S(1)}, u32[]{:S(2)}, u32[]{:S(2)}) collective-permute-start(f32[40,256]{1,0:T(8,128)S(1)} %get-tuple-element.16), channel_id=1, source_target_pairs={{1,2},{3,4},{5,6},{2,1},{4,3},{6,5},{9,10},{11,12},{13,14},{10,9},... | collective-permute-start | bytes 122888 | tf_op jit(solution)/shard_map/ppermute | solution.py:74

commit v10 on v9

--- a/solution.py
+++ b/solution.py
@@ -346,6 +346,7 @@
     main_total_ref,
     strip_total_ref,
     image_ref,
+    start_ref,
     result_ref,
     result_sem,
 ):
@@ -360,6 +361,7 @@
     weight = weight_ref[:, :1]
 
     def write_image():
+        start_ref[...] = jnp.concatenate([above[rows:], wide_ref[...], below[rows:]], axis=0)
         write_main_rows(image_ref, weight, main_total_ref, range(plan.groups))
         for group in range(plan.strip_groups):
             summed = weighted_rows(weight, strip_total_ref, group)
@@ -382,8 +384,7 @@
     valid = (at_row >= 0) & (at_row < tile_count * rows) & (at_column >= 0) & (at_column < kern_count * LANES)
     valid = valid & (lane_id < LANES + 2 * RIM)
 
-    base = jnp.concatenate([above[rows:], wide_ref[...], below[rows:]], axis=0)
-    base = jnp.where(valid, base, 0.0)
+    base = jnp.where(valid, start_ref[...], 0.0)
     acid = jnp.where(valid, 1.0 - jnp.exp(-EXPOSURE * image), 0.0)
 
     def spread(value):
@@ -492,6 +493,7 @@
             pltpu.VMEM(main_total.shape, jnp.float32),
             pltpu.VMEM(strip_total.shape, jnp.float32),
             pltpu.VMEM((plan.height, 2 * LANES), jnp.float32),
+            pltpu.VMEM((plan.height, 2 * LANES), jnp.float32),
             pltpu.VMEM((3, rows, LANES), jnp.float32),
             pltpu.SemaphoreType.DMA((3,)),
         ],

time: 19.1 us -> 19.1 us (level)
  no operation moved by 1% of the time
where the time goes in v10:
time: 19.1 us; the launch traced here: 19 us
  starting transfers between devices  10.2 us (53%)
  Pallas kernels  6.43 us (34%)
  waiting for transfers between devices  1.59 us (8%)
  between operations  0.76 us (4%)
    ppermute x7, starting transfers between devices, swapped(): lax.ppermute(value, axis, pairs + [(high, low) for low, high in pairs])  10.2 us
    pallas_call x1, Pallas kernels, on_device(): pl.pallas_call(functools.partial(resist_kernel, plan, kern_count, tile_co...  2.97 us
    ppermute x7, waiting for transfers between devices, swapped(): lax.ppermute(value, axis, pairs + [(high, low) for low, high in pairs])  1.59 us
    pallas_call x1, Pallas kernels, on_device(): pl.pallas_call(functools.partial(own_rows_kernel, plan), out_shape=(main_...  1.45 us
    pallas_call x1, Pallas kernels, on_device(): pl.pallas_call(functools.partial(pair_rows_kernel, plan), out_shape=(main...  1.36 us
    pallas_call x1, Pallas kernels, on_device(): pl.pallas_call(functools.partial(taps_kernel, plan), out_shape=(jax.Shape...  0.52 us
  transfers between devices with their start and end apart: 7, of which 2 were waited for; matrix products, arithmetic and copies ran while one was open for 0% of the time, Pallas kernels for 18%

profile of v10, /device:TPU:4, one launch (start us, length us, event | category | flops | bytes accessed | tf_op | source)
XLA Modules:
  0.0 19.0 jit_solution(62868428623758773)
XLA Ops:
  0.6 0.0 copy-start.2
  0.6 0.0 copy-start.1
  0.7 0.0 copy-start.3
  0.7 0.0 copy-start
  0.7 1.6 %collective-permute-start.1 = (f32[32,128]{1,0:T(8,128)}, f32[32,128]{1,0:T(8,128)S(1)}, u32[]{:S(2)}, u32[]{:S(2)}) collective-permute-start(f32[32,128]{1,0:T(8,128)} %quencher_ref.1), channel_id=1, source_target_pairs={{0,16},{8,24},{16,0},{24,8},{1,17},{9,25},{17,1},{25,9},{2,18},{10... | collective-permute-start | bytes 49160 | tf_op jit(solution)/shard_map/ppermute | solution.py:74
  2.2 0.0 collective-permute-start
  2.2 0.7 %collective-permute-start.6 = (s32[32,512]{1,0:T(8,128)}, s32[32,512]{1,0:T(8,128)S(1)}, u32[]{:S(2)}, u32[]{:S(2)}) collective-permute-start(s32[32,512]{1,0:T(8,128)} %mask_ref.1), channel_id=1, source_target_pairs={{2,4},{3,5},{4,2},{5,3},{10,12},{11,13},{12,10},{13,11},{18,20},{1... | collective-permute-start | bytes 196616 | tf_op jit(solution)/shard_map/ppermute | solution.py:74
  2.9 4.5 %collective-permute-start.5 = (s32[32,512]{1,0:T(8,128)}, s32[32,512]{1,0:T(8,128)S(1)}, u32[]{:S(2)}, u32[]{:S(2)}) collective-permute-start(s32[32,512]{1,0:T(8,128)} %mask_ref.1), channel_id=1, source_target_pairs={{0,2},{1,3},{4,6},{5,7},{2,0},{3,1},{6,4},{7,5},{8,10},{9,11},{12,... | collective-permute-start | bytes 196616 | tf_op jit(solution)/shard_map/ppermute | solution.py:74
  7.4 0.0 collective-permute-done.1
  7.4 0.0 collective-permute-start.2
  7.4 0.0 copy-done.3
  7.4 0.0 copy-done
  7.4 0.5 %taps.1 = (bf16[768,256]{1,0:T(8,128)(2,1)S(1)}, f32[48,128]{1,0:T(8,128)S(1)}) custom-call(bf16[24,2,64,64]{3,2,1,0:T(8,128)(2,1)S(1)} %copy-done, f32[24]{0:T(128)S(1)} %copy-done.3, bf16[256,256]{1,0:T(8,128)(2,1)S(1)} %turned.1.turned_ref), custom_call_target="tpu_custom_call" | custom-call | tf_op jit(solution)/shard_map/taps/pallas_call | solution.py:446
  7.9 0.0 collective-permute-done.beside_ref
  7.9 0.6 %collective-permute-done.2.across_ref = f32[32,128]{1,0:T(8,128)S(1)} collective-permute-done((f32[32,128]{1,0:T(8,128)S(1)}, f32[32,128]{1,0:T(8,128)S(1)}, u32[]{:S(2)}, u32[]{:S(2)}) %collective-permute-start.2) | collective-permute-done | bytes 16416 | tf_op jit(solution)/shard_map/ppermute | solution.py:74
  8.5 0.0 copy-done.2
  8.5 0.0 copy-done.1
  8.5 0.1 rims.1
  8.7 0.6 %collective-permute-start.4 = (f32[40,256]{1,0:T(8,128)S(1)}, f32[40,256]{1,0:T(8,128)S(1)}, u32[]{:S(2)}, u32[]{:S(2)}) collective-permute-start(f32[40,256]{1,0:T(8,128)S(1)} %get-tuple-element.17), channel_id=1, source_target_pairs={{0,1},{2,3},{4,5},{6,7},{1,0},{3,2},{5,4},{7,6},{8,9},{10,11},{12,... | collective-permute-start | bytes 122888 | tf_op jit(solution)/shard_map/ppermute | solution.py:74
  9.2 2.9 %collective-permute-start.3 = (f32[40,256]{1,0:T(8,128)S(1)}, f32[40,256]{1,0:T(8,128)S(1)}, u32[]{:S(2)}, u32[]{:S(2)}) collective-permute-start(f32[40,256]{1,0:T(8,128)S(1)} %get-tuple-element.16), channel_id=1, source_target_pairs={{1,2},{3,4},{5,6},{2,1},{4,3},{6,5},{9,10},{11,12},{13,14},{10,9},... | collective-permute-start | bytes 122888 | tf_op jit(solution)/shard_map/ppermute | solution.py:74
  12.2 1.5 %own_rows.1 = (f32[576,512]{1,0:T(8,128)S(1)}, f32[144,256]{1,0:T(8,128)S(1)}) custom-call(f32[32,256]{1,0:T(8,128)S(1)} %get-tuple-element.15.window_ref.own_ref, bf16[768,256]{1,0:T(8,128)(2,1)S(1)} %get-tuple-element.14._.taps_ref), custom_call_target="tpu_custom_call" | custom-call | tf_op jit(solution)/shard_map/own_rows/pallas_call | solution.py:467
  13.6 0.0 collective-permute-done.6.far_other_ref
  13.6 0.0 collective-permute-done.5.far_pair_ref
  13.6 0.0 collective-permute-done.4.pair_ref
  13.7 1.4 %pair_rows.1 = (f32[576,512]{1,0:T(8,128)S(1)}, f32[144,256]{1,0:T(8,128)S(1)}, f32[8,256]{1,0:T(8,128)S(1)}) custom-call(f32[32,256]{1,0:T(8,128)S(1)} %get-tuple-element.15.window_ref.own_ref, f32[40,256]{1,0:T(8,128)S(1)} %collective-permute-done.4.pair_ref, s32[32,512]{1,0:T(8,128)S(1)} %collective-permute-done.5.far_pair_ref, ...), custom_call_target="tpu_custom_call" | custom-call | tf_op jit(solution)/shard_map/pair_rows/pallas_call | solution.py:476
  15.0 1.0 %collective-permute-done.3.other_ref = f32[40,256]{1,0:T(8,128)S(1)} collective-permute-done((f32[40,256]{1,0:T(8,128)S(1)}, f32[40,256]{1,0:T(8,128)S(1)}, u32[]{:S(2)}, u32[]{:S(2)}) %collective-permute-start.3) | collective-permute-done | bytes 40992 | tf_op jit(solution)/shard_map/ppermute | solution.py:74
  16.0 3.0 %image_and_resist.1 = (f32[32,128]{1,0:T(8,128)}, f32[32,128]{1,0:T(8,128)}, f32[32,128]{1,0:T(8,128)}) custom-call(f32[32,256]{1,0:T(8,128)S(1)} %get-tuple-element.15.window_ref.own_ref, f32[40,256]{1,0:T(8,128)S(1)} %collective-permute-done.3.other_ref, f32[40,256]{1,0:T(8,128)S(1)} %collective-permute-done.4.pair_ref, ...), custom_call_target="tpu_custom_call" | custom-call | tf_op jit(solution)/shard_map/image_and_resist/pallas_call | solution.py:486
  (1 shorter events, 0.0 us)
Async XLA Ops:
  0.6 7.9 %copy-start.2 = (f32[32,128]{1,0:T(8,128)S(1)}, f32[32,128]{1,0:T(8,128)}, u32[]{:S(2)}) copy-start(f32[32,128]{1,0:T(8,128)} %quencher_ref.1) | copy-start | bytes 49156
  0.6 7.9 %copy-start.1 = (s32[32,512]{1,0:T(8,128)S(1)}, s32[32,512]{1,0:T(8,128)}, u32[]{:S(2)}) copy-start(s32[32,512]{1,0:T(8,128)} %mask_ref.1) | copy-start | bytes 196612
  0.7 6.7 %copy-start.3 = (f32[24]{0:T(128)S(1)}, f32[24]{0:T(128)}, u32[]{:S(2)}) copy-start(f32[24]{0:T(128)} %weights_ref.1) | copy-start | bytes 292
  0.7 6.7 %copy-start = (bf16[24,2,64,64]{3,2,1,0:T(8,128)(2,1)S(1)}, bf16[24,2,64,64]{3,2,1,0:T(8,128)(2,1)}, u32[]{:S(2)}) copy-start(bf16[24,2,64,64]{3,2,1,0:T(8,128)(2,1)} %kernels_ref.1) | copy-start | bytes 1179652
  0.7 6.7 %collective-permute-start.1 = (f32[32,128]{1,0:T(8,128)}, f32[32,128]{1,0:T(8,128)S(1)}, u32[]{:S(2)}, u32[]{:S(2)}) collective-permute-start(f32[32,128]{1,0:T(8,128)} %quencher_ref.1), channel_id=1, source_target_pairs={{0,16},{8,24},{16,0},{24,8},{1,17},{9,25},{17,1},{25,9},{2,18},{10... | collective-permute-start | bytes 49160 | tf_op jit(solution)/shard_map/ppermute | solution.py:74
  2.2 5.7 %collective-permute-start = (f32[32,128]{1,0:T(8,128)}, f32[32,128]{1,0:T(8,128)S(1)}, u32[]{:S(2)}, u32[]{:S(2)}) collective-permute-start(f32[32,128]{1,0:T(8,128)} %quencher_ref.1), channel_id=1, source_target_pairs={{0,8},{16,24},{8,0},{24,16},{1,9},{17,25},{9,1},{25,17},{2,10},{18... | collective-permute-start | bytes 49160 | tf_op jit(solution)/shard_map/ppermute | solution.py:74
  2.2 11.4 %collective-permute-start.6 = (s32[32,512]{1,0:T(8,128)}, s32[32,512]{1,0:T(8,128)S(1)}, u32[]{:S(2)}, u32[]{:S(2)}) collective-permute-start(s32[32,512]{1,0:T(8,128)} %mask_ref.1), channel_id=1, source_target_pairs={{2,4},{3,5},{4,2},{5,3},{10,12},{11,13},{12,10},{13,11},{18,20},{1... | collective-permute-start | bytes 196616 | tf_op jit(solution)/shard_map/ppermute | solution.py:74
  2.9 10.7 %collective-permute-start.5 = (s32[32,512]{1,0:T(8,128)}, s32[32,512]{1,0:T(8,128)S(1)}, u32[]{:S(2)}, u32[]{:S(2)}) collective-permute-start(s32[32,512]{1,0:T(8,128)} %mask_ref.1), channel_id=1, source_target_pairs={{0,2},{1,3},{4,6},{5,7},{2,0},{3,1},{6,4},{7,5},{8,10},{9,11},{12,... | collective-permute-start | bytes 196616 | tf_op jit(solution)/shard_map/ppermute | solution.py:74
  7.4 1.2 %collective-permute-start.2 = (f32[32,128]{1,0:T(8,128)S(1)}, f32[32,128]{1,0:T(8,128)S(1)}, u32[]{:S(2)}, u32[]{:S(2)}) collective-permute-start(f32[32,128]{1,0:T(8,128)S(1)} %collective-permute-done.1), channel_id=1, source_target_pairs={{0,8},{16,24},{8,0},{24,16},{1,9},{17,25},{9,1},{25,17},{2,10},{18... | collective-permute-start | bytes 49160 | tf_op jit(solution)/shard_map/ppermute | solution.py:74
  8.7 5.0 %collective-permute-start.4 = (f32[40,256]{1,0:T(8,128)S(1)}, f32[40,256]{1,0:T(8,128)S(1)}, u32[]{:S(2)}, u32[]{:S(2)}) collective-permute-start(f32[40,256]{1,0:T(8,128)S(1)} %get-tuple-element.17), channel_id=1, source_target_pairs={{0,1},{2,3},{4,5},{6,7},{1,0},{3,2},{5,4},{7,6},{8,9},{10,11},{12,... | collective-permute-start | bytes 122888 | tf_op jit(solution)/shard_map/ppermute | solution.py:74
  9.2 6.8 %collective-permute-start.3 = (f32[40,256]{1,0:T(8,128)S(1)}, f32[40,256]{1,0:T(8,128)S(1)}, u32[]{:S(2)}, u32[]{:S(2)}) collective-permute-start(f32[40,256]{1,0:T(8,128)S(1)} %get-tuple-element.16), channel_id=1, source_target_pairs={{1,2},{3,4},{5,6},{2,1},{4,3},{6,5},{9,10},{11,12},{13,14},{10,9},... | collective-permute-start | bytes 122888 | tf_op jit(solution)/shard_map/ppermute | solution.py:74
